TPU v7x, 32 devices: a whole 2x2x4 slice. The times are simulated.
32 devices in a mesh: dp: 8 (over z, y), strip: 4 (over x, core).
Axes of the slice: x: 2, y: 2, z: 4, core: 2. Of those that a mesh axis runs over, the one named last changes fastest.
Arguments:
- images: bfloat16 [48, 36, 36, 320], P('dp', 'strip'), may hold values from -6 to 6
- counts: int32 [8], replicated, may hold values from 1 to 6, as said below
- gain_one: bfloat16 [320], replicated, may hold values from 0.5 to 1.5
- shift_one: bfloat16 [320], replicated, may hold values from -3 to 3
- proj_in: bfloat16 [320, 320], replicated, may hold values from -0.3125 to 0.3125
- kernel_five: bfloat16 [25, 320], replicated, may hold values from -1.25 to 1.25
- kernel_seven: bfloat16 [49, 320], replicated, may hold values from -0.875 to 0.875
- lka_proj: bfloat16 [320, 320], replicated, may hold values from -0.3125 to 0.3125
- proj_out: bfloat16 [320, 320], replicated, may hold values from -0.3125 to 0.3125
- scale_one: bfloat16 [320], replicated, may hold values from 0.5 to 1.5
- gain_two: bfloat16 [320], replicated, may hold values from 0.5 to 1.5
- shift_two: bfloat16 [320], replicated, may hold values from -3 to 3
- fc_in: bfloat16 [320, 1280], replicated, may hold values from -0.3125 to 0.3125
- kernel_three: bfloat16 [9, 1280], replicated, may hold values from -2 to 2
- fc_out: bfloat16 [1280, 320], replicated, may hold values from -0.15625 to 0.15625
- scale_two: bfloat16 [320], replicated, may hold values from 0.5 to 1.5
- cotangent: bfloat16 [48, 36, 36, 320], P('dp', 'strip'), may hold values from -6 to 6
Outputs:
- out_image: bfloat16 [48, 36, 36, 320], P('dp', 'strip')
- grad_images: float32 [48, 36, 36, 320], P('dp', 'strip')
- gradient_first_gain: float32 [320], replicated
- gradient_first_shift: float32 [320], replicated
- grad_proj_in: float32 [320, 320], replicated
- grad_kernel_five: float32 [25, 320], replicated
- grad_kernel_seven: float32 [49, 320], replicated
- grad_lka_proj: float32 [320, 320], replicated
- grad_proj_out: float32 [320, 320], replicated
- grad_scale_one: float32 [320], replicated
- grad_gain_two: float32 [320], replicated
- grad_shift_two: float32 [320], replicated
- grad_fc_in: float32 [320, 1280], replicated
- grad_kernel_three: float32 [9, 1280], replicated
- grad_fc_out: float32 [1280, 320], replicated
- grad_scale_two: float32 [320], replicated
Inputs may be any that keep to these rules, and one draw needn't show every extreme that they name: `counts`: live images of each index of dp; some index has all 6 slots live.
All inputs are finite; a program needn't handle non-finite values.
Results may differ from a plain program's by a relative error of at most 0.012.
Values may be sent and summed in bfloat16 or wider, within the bound.
No kernel may reach another device: no remote copies, remote signals or barrier semaphores. Data moves between devices by JAX's collectives and lax.ppermute only.
A program may use at most 256 MiB of HBM per device.

v0:
```python
import jax
import jax.numpy as jnp
from jax import lax
from jax.sharding import PartitionSpec as P

epsilon = 1e-05


def extended(value, sides, width):
    for axis, dim in sides:
        devices, length = (lax.axis_size(axis), value.shape[dim])
        up = [(i, (i + 1) % devices) for i in range(devices - 1)]
        down = [(j, i) for i, j in up]
        last = lax.slice_in_dim(value, length - width, length, axis=dim)
        leading = lax.slice_in_dim(value, 0, width, axis=dim)
        before = lax.ppermute(last, axis, up)
        after = lax.ppermute(leading, axis, down)
        value = jnp.concatenate([before, value, after], axis=dim)
    return value


def depthwise(padded, kernel, across, spread):
    margin = across // 2 * spread
    height = padded.shape[1] - 2 * margin
    breadth = padded.shape[2]
    padded = jnp.pad(padded, ((0, 0), (0, 0), (margin, margin), (0, 0)))
    total = jnp.zeros((padded.shape[0], height, breadth, padded.shape[3]), jnp.float32)
    for row_tap in range(across):
        for col_tap in range(across):
            window = padded[
                :,
                row_tap * spread : row_tap * spread + height,
                col_tap * spread : col_tap * spread + breadth,
                :,
            ]
            total = total + window * kernel[row_tap * across + col_tap]
    return total


def kernel_grad(padded, grad_out, across, spread):
    margin = across // 2 * spread
    height = grad_out.shape[1]
    breadth = grad_out.shape[2]
    padded = jnp.pad(padded, ((0, 0), (0, 0), (margin, margin), (0, 0)))
    tap_sums = []
    for row_tap in range(across):
        for col_tap in range(across):
            window = padded[
                :,
                row_tap * spread : row_tap * spread + height,
                col_tap * spread : col_tap * spread + breadth,
                :,
            ]
            tap_sums.append(jnp.sum(window * grad_out, axis=(0, 1, 2)))
    return jnp.stack(tap_sums)


def project(values, matrix):
    return jnp.einsum("bhwc,cd->bhwd", values, matrix, preferred_element_type=jnp.float32)


def project_back(grads, matrix):
    return jnp.einsum("bhwd,cd->bhwc", grads, matrix, preferred_element_type=jnp.float32)


def outer_sum(values, grads):
    return jnp.einsum("bhwc,bhwd->cd", values, grads, preferred_element_type=jnp.float32)


def gelu_grad(before, grad):
    return jax.vjp(lambda value: jax.nn.gelu(value, approximate=False), before)[1](grad)[0]


def per_channel_sum(values):
    return jnp.sum(values, axis=(0, 1, 2))


def body(
    images,
    counts,
    gain_one,
    shift_one,
    proj_in,
    kernel_five,
    kernel_seven,
    lka_proj,
    proj_out,
    scale_one,
    gain_two,
    shift_two,
    fc_in,
    kernel_three,
    fc_out,
    scale_two,
    cotangent,
):
    slots_here = images.shape[0]
    alive = (jnp.arange(slots_here) < counts[lax.axis_index("dp")]).astype(jnp.float32)[
        :, None, None, None
    ]
    pixel_count = jnp.sum(counts).astype(jnp.float32) * (
        images.shape[1] * lax.axis_size("strip") * images.shape[2]
    )
    first_gain = gain_one.astype(jnp.float32)
    first_shift = shift_one.astype(jnp.float32)
    gain_b = gain_two.astype(jnp.float32)
    shift_b = shift_two.astype(jnp.float32)
    layer_one = scale_one.astype(jnp.float32)
    layer_two = scale_two.astype(jnp.float32)
    taps_five = kernel_five.astype(jnp.float32)
    taps_seven = kernel_seven.astype(jnp.float32)
    taps_three = kernel_three.astype(jnp.float32)
    input_images = images.astype(jnp.float32)
    first_sums = lax.psum(
        (
            per_channel_sum(input_images * alive),
            per_channel_sum(input_images * input_images * alive),
        ),
        ("dp", "strip"),
    )
    first_mean = first_sums[0] / pixel_count
    first_inverse_deviation = lax.rsqrt(
        first_sums[1] / pixel_count - first_mean * first_mean + epsilon
    )
    centered_scaled_input = (input_images - first_mean) * first_inverse_deviation
    normalized_input = centered_scaled_input * first_gain + first_shift
    normed_low = normalized_input.astype(jnp.bfloat16)
    pre_gelu = project(normed_low, proj_in)
    gelu_low = jax.nn.gelu(pre_gelu, approximate=False).astype(jnp.bfloat16)
    gelu_rim = extended(gelu_low, (("strip", 1),), 2)
    lka_mid = depthwise(gelu_rim.astype(jnp.float32), taps_five, 5, 1).astype(jnp.bfloat16)
    mid_rim = extended(lka_mid, (("strip", 1),), 9)
    lka_out = depthwise(mid_rim.astype(jnp.float32), taps_seven, 7, 3)
    lka_low = lka_out.astype(jnp.bfloat16)
    attend = project(lka_low, lka_proj)
    gelu_value = gelu_low.astype(jnp.float32)
    gated_low = (gelu_value * attend).astype(jnp.bfloat16)
    branch = project(gated_low, proj_out)
    attn = branch + normalized_input
    first_sum = input_images + layer_one * attn
    second_sums = lax.psum(
        (per_channel_sum(first_sum * alive), per_channel_sum(first_sum * first_sum * alive)),
        ("dp", "strip"),
    )
    mean_two = second_sums[0] / pixel_count
    rstd_two = lax.rsqrt(second_sums[1] / pixel_count - mean_two * mean_two + epsilon)
    yhat = (first_sum - mean_two) * rstd_two
    normed_two_low = (yhat * gain_b + shift_b).astype(jnp.bfloat16)
    hidden_low = project(normed_two_low, fc_in).astype(jnp.bfloat16)
    hidden_pad = extended(hidden_low, (("strip", 1),), 1).astype(jnp.float32)
    mixed = depthwise(hidden_pad, taps_three, 3, 1)
    active_low = jax.nn.gelu(mixed, approximate=False).astype(jnp.bfloat16)
    mlp_out = project(active_low, fc_out)
    out_image = (alive * (first_sum + layer_two * mlp_out)).astype(jnp.bfloat16)
    grad_out = cotangent.astype(jnp.float32) * alive
    grad_scale_two = per_channel_sum(grad_out * mlp_out)
    grad_mlp_low = (grad_out * layer_two).astype(jnp.bfloat16)
    grad_active = project_back(grad_mlp_low, fc_out)
    grad_fc_out = outer_sum(active_low, grad_mlp_low)
    grad_mixed = gelu_grad(mixed, grad_active)
    grad_mixed_pad = extended(grad_mixed.astype(jnp.bfloat16), (("strip", 1),), 1).astype(
        grad_mixed.dtype
    )
    grad_hidden = depthwise(grad_mixed_pad, taps_three[::-1], 3, 1).astype(jnp.bfloat16)
    grad_kernel_three = kernel_grad(hidden_pad, grad_mixed, 3, 1)
    grad_normed_two = project_back(grad_hidden, fc_in)
    grad_fc_in = outer_sum(normed_two_low, grad_hidden)
    grad_shift_two, grad_gain_two = lax.psum(
        (per_channel_sum(grad_normed_two), per_channel_sum(grad_normed_two * yhat)), ("dp", "strip")
    )
    grad_first = grad_out + alive * rstd_two * gain_b * (
        grad_normed_two - (grad_shift_two + yhat * grad_gain_two) / pixel_count
    )
    grad_scale_one = per_channel_sum(grad_first * attn)
    grad_attn = grad_first * layer_one
    grad_branch_low = grad_attn.astype(jnp.bfloat16)
    grad_gated = project_back(grad_branch_low, proj_out)
    grad_proj_out = outer_sum(gated_low, grad_branch_low)
    grad_attend_low = (grad_gated * gelu_value).astype(jnp.bfloat16)
    grad_lka_out = project_back(grad_attend_low, lka_proj)
    grad_lka_proj = outer_sum(lka_low, grad_attend_low)
    grad_out_rim = extended(grad_lka_out.astype(jnp.bfloat16), (("strip", 1),), 9).astype(
        grad_lka_out.dtype
    )
    grad_mid = depthwise(grad_out_rim, taps_seven[::-1], 7, 3)
    grad_kernel_seven = kernel_grad(mid_rim.astype(jnp.float32), grad_lka_out, 7, 3)
    grad_mid_rim = extended(grad_mid.astype(jnp.bfloat16), (("strip", 1),), 2).astype(
        grad_mid.dtype
    )
    grad_gelu = grad_gated * attend + depthwise(grad_mid_rim, taps_five[::-1], 5, 1)
    grad_kernel_five = kernel_grad(gelu_rim.astype(jnp.float32), grad_mid, 5, 1)
    grad_pre_low = gelu_grad(pre_gelu, grad_gelu).astype(jnp.bfloat16)
    normalized_gradient = grad_attn + project_back(grad_pre_low, proj_in)
    grad_proj_in = outer_sum(normed_low, grad_pre_low)
    totals = lax.psum(
        (
            per_channel_sum(normalized_gradient),
            per_channel_sum(normalized_gradient * centered_scaled_input),
            grad_proj_in,
            grad_kernel_five,
            grad_kernel_seven,
            grad_lka_proj,
            grad_proj_out,
            grad_scale_one,
            grad_fc_in,
            grad_kernel_three,
            grad_fc_out,
            grad_scale_two,
        ),
        ("dp", "strip"),
    )
    gradient_first_shift = totals[0]
    gradient_first_gain = totals[1]
    grad_images = grad_first + alive * first_inverse_deviation * first_gain * (
        normalized_gradient
        - (gradient_first_shift + centered_scaled_input * gradient_first_gain) / pixel_count
    )
    return (
        out_image,
        grad_images,
        gradient_first_gain,
        gradient_first_shift,
        totals[2],
        totals[3],
        totals[4],
        totals[5],
        totals[6],
        totals[7],
        grad_gain_two,
        grad_shift_two,
        totals[8],
        totals[9],
        totals[10],
        totals[11],
    )


def solution(mesh):
    return jax.shard_map(
        body,
        mesh=mesh,
        in_specs=(
            P("dp", "strip", None, None),
            P(),
            P(),
            P(),
            P(),
            P(),
            P(),
            P(),
            P(),
            P(),
            P(),
            P(),
            P(),
            P(),
            P(),
            P(),
            P("dp", "strip", None, None),
        ),
        out_specs=(
            P("dp", "strip", None, None),
            P("dp", "strip", None, None),
            P(),
            P(),
            P(),
            P(),
            P(),
            P(),
            P(),
            P(),
            P(),
            P(),
            P(),
            P(),
            P(),
            P(),
        ),
        check_vma=False,
    )
```

profile of v0, /device:TPU:0, one launch (start us, length us, event | category | flops | bytes accessed | tf_op | source)
XLA Modules:
  0.0 1018.6 jit_solution(5147239496691669218)
XLA Ops:
  16.7 42.0 %all-reduce.9 = (f32[320]{0:T(512)S(1)}, f32[320]{0:T(512)S(1)}) all-reduce(f32[320]{0:T(512)S(1)} %get-tuple-element.106, f32[320]{0:T(512)S(1)} %get-tuple-element.105), channel_id=1, replica_groups=mesh['dp'=8,'strip'=4] {'dp','strip'}, use_global_device_ids=true, to_apply=%region_4.0 | all-reduce | flops 640 | bytes 5120 | tf_op jit(solution)/shard_map/psum | solution.py:114
  59.3 10.5 %multiply_convert_fusion.3 = (bf16[6,9,36,320]{3,2,1,0:T(8,128)(2,1)S(1)}, f32[6,9,36,320]{3,2,1,0:T(8,128)}) fusion(bf16[320,320]{1,0:T(8,128)(2,1)} %param.21, bf16[6,9,36,320]{3,2,1,0:T(8,128)(2,1)} %param.17, f32[320]{0:T(512)} %convert_element_type.132, f32[320]{0:T(512)} %convert_element_type.131, f32[320]{0:T(512)S(1)} %get-tuple-element.233, ...), kind=kOutput, calls=%fused_computation.385 | convolution fusion | flops 442298880 | bytes 5186560 | tf_op jit(solution)/shard_map/bhwc,cd->bhwd/dot_general | solution.py:59
  76.4 11.9 %add_convert_fusion.3 = bf16[6,9,36,320]{3,2,1,0:T(8,128)(2,1)S(1)} fusion(f32[6,13,36,320]{3,2,1,0:T(8,128)S(1)} %maximum_convert_fusion.4, f32[320]{0:T(512)S(1)} %get-tuple-element.166, f32[320]{0:T(512)S(1)} %get-tuple-element.167, f32[320]{0:T(512)S(1)} %get-tuple-element.168, f32[320]{0:T(512)S(1)} %get-tuple-element.169, ...), kind=kLoop, calls=%fused_computation.384 | loop fusion | flops 31104000 | bytes 22676480 | tf_op jit(solution)/shard_map/convert_element_type | solution.py:131
  89.7 9.2 collective-permute-start.2
  103.5 29.9 %add_convert_fusion.2 = bf16[6,9,36,320]{3,2,1,0:T(8,128)(2,1)} fusion(f32[6,27,36,320]{3,2,1,0:T(8,128)S(1)} %maximum_convert_fusion.2, f32[320]{0:T(512)S(1)} %get-tuple-element.108, f32[320]{0:T(512)S(1)} %get-tuple-element.109, f32[320]{0:T(512)S(1)} %get-tuple-element.110, f32[320]{0:T(512)S(1)} %get-tuple-element.111, f32[320]{0:T(512)S(1)} %get-tuple-element.112, ...), kind=kLoop, calls=%fused_computation.383 | loop fusion | flops 60963840 | bytes 34511360 | tf_op jit(solution)/shard_map/convert_element_type | solution.py:134
  136.4 6.3 multiply_reduce_fusion.87
  142.8 57.5 %all-reduce.8 = (f32[320]{0:T(512)S(1)}, f32[320]{0:T(512)S(1)}) all-reduce(f32[320]{0:T(512)S(1)} %get-tuple-element.100, f32[320]{0:T(512)S(1)} %get-tuple-element.99), channel_id=1, replica_groups=mesh['dp'=8,'strip'=4] {'dp','strip'}, use_global_device_ids=true, to_apply=%region_8.9 | all-reduce | flops 640 | bytes 5120 | tf_op jit(solution)/shard_map/psum | solution.py:141
  200.3 5.2 convolution_convert_fusion
  211.9 5.3 maximum_convert_fusion
  217.2 50.1 %multiply_convert_fusion = (bf16[6,9,36,1280]{3,2,1,0:T(8,128)(2,1)}, f32[6,9,36,1280]{3,2,1,0:T(8,128)}, f32[6,9,36,1280]{3,2,1,0:T(8,128)}) fusion(f32[1280]{0:T(1024)S(1)} %get-tuple-element.157, f32[1280]{0:T(1024)S(1)} %get-tuple-element.158, f32[6,11,36,1280]{3,2,1,0:T(8,128)} %maximum_convert_fusion, f32[1280]{0:T(1024)S(1)} %get-tuple-element.159, ...), kind=kLoop, calls=%fused_computation.114 | loop fusion | flops 204042240 | bytes 71623680 | tf_op jit(solution)/shard_map/convert_element_type | solution.py:152
  267.3 53.8 %multiply_reduce_fusion = (f32[1280]{0:T(1024)}, f32[1280]{0:T(1024)}, f32[1280]{0:T(1024)}, f32[1280]{0:T(1024)}, f32[1280]{0:T(1024)}, /*index=5*/f32[1280]{0:...) fusion(f32[6,11,36,1280]{3,2,1,0:T(8,128)} %maximum_convert_fusion, ...), kind=kOutput, calls=%fused_computation.98 | convolution fusion | flops 1674627840 | bytes 75900672 | tf_op jit(solution)/shard_map/bhwd,cd->bhwc/dot_general | solution.py:63
  323.7 10.0 collective-permute-start.6
  348.2 6.6 convolution_bitcast_fusion
  354.8 5.3 maximum_convert_fusion.1
  360.2 35.5 %fusion.3 = bf16[6,9,36,1280]{3,2,1,0:T(8,128)(2,1)} fusion(f32[6,11,36,1280]{3,2,1,0:T(8,128)} %maximum_convert_fusion.1, f32[1280]{0:T(1024)S(1)} %get-tuple-element.157, f32[1280]{0:T(1024)S(1)} %get-tuple-element.158, f32[1280]{0:T(1024)S(1)} %get-tuple-element.159, f32[1280]{0:T(1024)S(1)} %copy-done.27, f32[1280]{0:T(1024)S(1)} %copy-done.29, ...), kind=kLoop, calls=%fused_computation.89 | loop fusion | flops 44789760 | bytes 51717120 | tf_op jit(solution)/shard_map/convert_element_type | solution.py:164
  395.7 9.0 fusion.185
  404.7 40.9 %all-reduce.7 = (f32[320]{0:T(512)S(1)}, f32[320]{0:T(512)S(1)}) all-reduce(f32[320]{0:T(512)S(1)} %get-tuple-element.104, f32[320]{0:T(512)S(1)} %get-tuple-element.103), channel_id=1, replica_groups=mesh['dp'=8,'strip'=4] {'dp','strip'}, use_global_device_ids=true, to_apply=%region_12.13 | all-reduce | flops 640 | bytes 5120 | tf_op jit(solution)/shard_map/psum | solution.py:168
  445.7 12.4 %multiply_reduce_fusion.9 = (f32[320]{0:T(512)}, bf16[6,9,36,320]{3,2,1,0:T(8,128)(2,1)}, f32[320]{0:T(512)}, f32[6,9,36,320]{3,2,1,0:T(8,128)S(1)}) fusion(bf16[6,9,36,320]{3,2,1,0:T(8,128)(2,1)S(1)} %copy-done.183, f32[6]{0:T(128)} %compare_convert_fusion, f32[6,9,36,320]{3,2,1,0:T(8,128)} %get-tuple-element.214, f32[320]{0:T(512)S(1)} %copy-done.175, ...), kind=kOutput, calls=%fused_computation.286 | convolution fusion | flops 1603721728 | bytes 18254108 | tf_op jit(solution)/shard_map/bhwc,cd->bhwd/dot_general | solution.py:59
  463.6 30.5 %multiply_reduce_fusion.11 = (f32[320]{0:T(512)S(1)}, f32[320]{0:T(512)S(1)}, f32[320]{0:T(512)S(1)}, f32[320]{0:T(512)S(1)}, f32[320]{0:T(512)S(1)}, /*index=5*...) fusion(f32[6,27,36,320]{3,2,1,0:T(8,128)} %copy-done.2, ...), kind=kOutput, calls=%fused_computation.288 | convolution fusion | flops 423008640 | bytes 28428800 | tf_op jit(solution)/shard_map/bhwd,cd->bhwc/dot_general | solution.py:63
  495.4 4.4 collective-permute-start.8
  499.7 21.9 %multiply_reduce_fusion.47 = (f32[320]{0:T(512)S(1)}, f32[320]{0:T(512)S(1)}, f32[320]{0:T(512)S(1)}, f32[320]{0:T(512)S(1)}, f32[320]{0:T(512)S(1)}, /*index=5*...) fusion(f32[6,9,36,320]{3,2,1,0:T(8,128)} %get-tuple-element.241, ...), kind=kLoop, calls=%fused_computation.324 | loop fusion | flops 16169920 | bytes 19923200 | tf_op jit(solution)/shard_map/reduce_sum | solution.py:54
  521.6 28.9 %multiply_reduce_fusion.29 = (f32[320]{0:T(512)S(1)}, f32[320]{0:T(512)S(1)}, f32[320]{0:T(512)S(1)}, f32[320]{0:T(512)S(1)}, f32[320]{0:T(512)S(1)}, /*index=5*...) fusion(f32[6,9,36,320]{3,2,1,0:T(8,128)} %get-tuple-element.241, ...), kind=kLoop, calls=%fused_computation.306 | loop fusion | flops 22389120 | bytes 19929600 | tf_op jit(solution)/shard_map/reduce_sum | solution.py:54
  558.3 4.4 stack.333
  562.6 7.0 convolution_bitcast_fusion.1
  570.0 6.9 maximum_convert_fusion.3
  577.2 78.5 %multiply_reduce_fusion.60 = (f32[320]{0:T(512)S(1)}, f32[320]{0:T(512)S(1)}, f32[320]{0:T(512)S(1)}, f32[320]{0:T(512)S(1)}, f32[320]{0:T(512)S(1)}, /*index=5*...) fusion(f32[6,13,36,320]{3,2,1,0:T(8,128)} %copy-done.1, ...), kind=kLoop, calls=%fused_computation.337 | loop fusion | flops 72780160 | bytes 47180032 | tf_op jit(solution)/shard_map/reduce_sum | solution.py:54
  655.7 18.2 %multiply_reduce_fusion.70 = (f32[320]{0:T(512)S(1)}, f32[320]{0:T(512)S(1)}, f32[320]{0:T(512)S(1)}, f32[320]{0:T(512)S(1)}, f32[320]{0:T(512)S(1)}, /*index=5*...) fusion(f32[6,9,36,320]{3,2,1,0:T(8,128)} %get-tuple-element.210, ...), kind=kLoop, calls=%fused_computation.347 | loop fusion | flops 13060480 | bytes 16002560 | tf_op jit(solution)/shard_map/reduce_sum | solution.py:54
  688.1 22.1 %add_convert_fusion = bf16[6,9,36,320]{3,2,1,0:T(8,128)(2,1)} fusion(f32[6,13,36,320]{3,2,1,0:T(8,128)S(1)} %maximum_convert_fusion.5, f32[6,9,36,320]{3,2,1,0:T(8,128)S(1)} %copy-done.5, f32[6,9,36,320]{3,2,1,0:T(8,128)S(1)} %copy-done.13, f32[6,9,36,320]{3,2,1,0:T(8,128)} %get-tuple-element.237, f32[320]{0:T(512)S(1)} %copy-done.54, ...), kind=kLoop, calls=%fused_computation.362 | loop fusion | flops 76515840 | bytes 31800320 | tf_op jit(solution)/shard_map/convert_element_type | solution.py:192
  710.3 5.6 fusion.184
  719.2 122.8 %all-reduce.14.cloned.1.call-done = (f32[320]{0:T(512)}, f32[320]{0:T(512)}, f32[25,320]{1,0:T(8,128)}, f32[49,320]{1,0:T(8,128)}, f32[320]{0:T(512)}, /*index=5*/f32[9,1280]{1,0:T(8,128)}, f32[320]{0:T(512)}) async-done(((f32[320]{0:T(512)}, f32[320]{0:T(512)}, f32[25,320]{1,0:T(8,128)}, f32[49,320]{1,0:T(8,128)}, f32[320]{0:T(512)}, /*index=5*/f32[9,1280]{1,0:T(8,128)}, f32[320]{0:T(512)}), ...) | async-done | bytes 145936 | tf_op jit(solution)/shard_map/psum | solution.py:195
  842.0 5.7 fusion.34
  847.7 151.4 %all-reduce.16.cloned.1.call-done = (f32[320,320]{1,0:T(8,128)}, f32[320,320]{1,0:T(8,128)}, f32[320,320]{1,0:T(8,128)}, f32[320,1280]{1,0:T(8,128)}, f32[1280,320]{0,1:T(8,128)}) async-done(((f32[320,320]{1,0:T(8,128)}, f32[320,320]{1,0:T(8,128)}, f32[320,320]{1,0:T(8,128)}, f32[320,1280]{1,0:T(8,128)}, f32[1280,320]{0,1:T(8,128)}), (f32[320,320]{1,0:T(8,128)}, f32[320,320]{1,0:T(8,128)}, ...) | async-done | bytes 4505616 | tf_op jit(solution)/shard_map/psum | solution.py:195
  (541 shorter events, 90.4 us)
Async XLA Ops:
  7.2 260.1 %copy-start = (bf16[1280,320]{0,1:T(8,128)(2,1)S(1)}, bf16[1280,320]{0,1:T(8,128)(2,1)}, u32[]{:S(2)}) copy-start(bf16[1280,320]{0,1:T(8,128)(2,1)} %param.31) | copy-start | bytes 2457604
  7.2 834.8 %all-reduce.14.cloned.1.call-start = ((), (), s32[]{:S(2)}) async-start(), calls=%async_computation | async-start | bytes 450560 | tf_op jit(solution)/shard_map/psum | solution.py:195
  59.3 151.1 %copy-start.48 = (f32[320]{0:T(512)}, f32[320]{0:T(512)S(1)}, u32[]{:S(2)}) copy-start(f32[320]{0:T(512)S(1)} %get-tuple-element.233) | copy-start | bytes 3844
  69.9 4.8 collective-permute-start.1
  71.2 4.3 collective-permute-start
  88.4 12.4 %collective-permute-start.3 = (bf16[6,9,36,320]{3,2,1,0:T(8,128)(2,1)S(1)}, bf16[6,9,36,320]{3,2,1,0:T(8,128)(2,1)S(1)}, u32[]{:S(2)}, u32[]{:S(2)}) collective-permute-start(bf16[6,9,36,320]{3,2,1,0:T(8,128)(2,1)S(1)} %add_convert_fusion.3), channel_id=1, source_target_pairs={{1,0},{2,1},{3,2},{5,4},{6,5},{7,6},{9,8},{10,9},{11,10},{13,12},{... | collective-permute-start | bytes 3732488 | tf_op jit(solution)/shard_map/ppermute | solution.py:17
  89.7 11.1 %collective-permute-start.2 = (bf16[6,9,36,320]{3,2,1,0:T(8,128)(2,1)S(1)}, bf16[6,9,36,320]{3,2,1,0:T(8,128)(2,1)}, u32[]{:S(2)}, u32[]{:S(2)}) collective-permute-start(bf16[6,9,36,320]{3,2,1,0:T(8,128)(2,1)S(1)} %add_convert_fusion.3), channel_id=1, source_target_pairs={{0,1},{1,2},{2,3},{4,5},{5,6},{6,7},{8,9},{9,10},{10,11},{12,13},{... | collective-permute-start | bytes 3732488 | tf_op jit(solution)/shard_map/ppermute | solution.py:16
  99.5 100.8 %copy-start.46 = (f32[320]{0:T(512)}, f32[320]{0:T(512)S(1)}, u32[]{:S(2)}) copy-start(f32[320]{0:T(512)S(1)} %convert_element_type.145) | copy-start | bytes 3844
  99.6 110.9 %copy-start.36 = (f32[320]{0:T(512)}, f32[320]{0:T(512)S(1)}, u32[]{:S(2)}) copy-start(f32[320]{0:T(512)S(1)} %convert_element_type.144) | copy-start | bytes 3844
  136.4 63.9 %copy-start.184 = (bf16[320,1280]{1,0:T(8,128)(2,1)S(1)}, bf16[320,1280]{1,0:T(8,128)(2,1)}, u32[]{:S(2)}) copy-start(bf16[320,1280]{1,0:T(8,128)(2,1)} %param.29) | copy-start | bytes 2457604
  205.7 6.2 collective-permute-start.5
  207.2 4.7 collective-permute-start.4
  210.3 57.0 %copy-start.174 = (f32[320]{0:T(512)}, f32[320]{0:T(512)S(1)}, u32[]{:S(2)}) copy-start(f32[320]{0:T(512)S(1)} %convert_element_type.143) | copy-start | bytes 3844
  217.2 50.1 %copy-start.182 = (bf16[6,9,36,320]{3,2,1,0:T(8,128)(2,1)S(1)}, bf16[6,9,36,320]{3,2,1,0:T(8,128)(2,1)}, u32[]{:S(2)}) copy-start(bf16[6,9,36,320]{3,2,1,0:T(8,128)(2,1)} %param.33) | copy-start | bytes 3732484
  322.4 32.4 %collective-permute-start.7 = (bf16[6,1,36,1280]{3,2,1,0:T(8,128)(2,1)S(1)}, bf16[6,1,36,1280]{3,2,1,0:T(8,128)(2,1)S(1)}, u32[]{:S(2)}, u32[]{:S(2)}) collective-permute-start(bf16[6,1,36,1280]{3,2,1,0:T(8,128)(2,1)S(1)} %get-tuple-element.217), channel_id=1, source_target_pairs={{1,0},{2,1},{3,2},{5,4},{6,5},{7,6},{9,8},{10,9},{11,10},{13,12},{... | collective-permute-start | bytes 1658888 | tf_op jit(solution)/shard_map/ppermute | solution.py:17
  323.7 31.1 %collective-permute-start.6 = (bf16[6,1,36,1280]{3,2,1,0:T(8,128)(2,1)S(1)}, bf16[6,1,36,1280]{3,2,1,0:T(8,128)(2,1)S(1)}, u32[]{:S(2)}, u32[]{:S(2)}) collective-permute-start(bf16[6,1,36,1280]{3,2,1,0:T(8,128)(2,1)S(1)} %get-tuple-element.216), channel_id=1, source_target_pairs={{0,1},{1,2},{2,3},{4,5},{5,6},{6,7},{8,9},{9,10},{10,11},{12,13},{... | collective-permute-start | bytes 1658888 | tf_op jit(solution)/shard_map/ppermute | solution.py:16
  360.1 35.6 %copy-start.39 = (f32[320]{0:T(512)S(1)}, f32[320]{0:T(512)}, u32[]{:S(2)}) copy-start(f32[320]{0:T(512)} %copy-done.38) | copy-start | bytes 3844
  395.7 49.9 %copy-start.171 = (f32[6,320]{1,0:T(8,128)S(1)}, f32[6,320]{1,0:T(8,128)}, u32[]{:S(2)}) copy-start(f32[6,320]{1,0:T(8,128)} %get-tuple-element.235) | copy-start | bytes 23044
  395.7 49.9 %copy-start.175 = (f32[320]{0:T(512)S(1)}, f32[320]{0:T(512)}, u32[]{:S(2)}) copy-start(f32[320]{0:T(512)} %copy-done.174) | copy-start | bytes 3844
  395.7 49.9 %copy-start.183 = (bf16[6,9,36,320]{3,2,1,0:T(8,128)(2,1)S(1)}, bf16[6,9,36,320]{3,2,1,0:T(8,128)(2,1)}, u32[]{:S(2)}) copy-start(bf16[6,9,36,320]{3,2,1,0:T(8,128)(2,1)} %param.33) | copy-start | bytes 3732484
  494.1 75.9 %collective-permute-start.9 = (bf16[6,9,36,320]{3,2,1,0:T(8,128)(2,1)}, bf16[6,9,36,320]{3,2,1,0:T(8,128)(2,1)}, u32[]{:S(2)}, u32[]{:S(2)}) collective-permute-start(bf16[6,9,36,320]{3,2,1,0:T(8,128)(2,1)} %get-tuple-element.224), channel_id=1, source_target_pairs={{1,0},{2,1},{3,2},{5,4},{6,5},{7,6},{9,8},{10,9},{11,10},{13,12},{... | collective-permute-start | bytes 3732488 | tf_op jit(solution)/shard_map/ppermute | solution.py:17
  495.4 74.6 %collective-permute-start.8 = (bf16[6,9,36,320]{3,2,1,0:T(8,128)(2,1)}, bf16[6,9,36,320]{3,2,1,0:T(8,128)(2,1)}, u32[]{:S(2)}, u32[]{:S(2)}) collective-permute-start(bf16[6,9,36,320]{3,2,1,0:T(8,128)(2,1)} %get-tuple-element.224), channel_id=1, source_target_pairs={{0,1},{1,2},{2,3},{4,5},{5,6},{6,7},{8,9},{9,10},{10,11},{12,13},{... | collective-permute-start | bytes 3732488 | tf_op jit(solution)/shard_map/ppermute | solution.py:16
  674.0 10.9 %collective-permute-start.11 = (bf16[6,2,36,320]{3,2,1,0:T(8,128)(2,1)S(1)}, bf16[6,2,36,320]{3,2,1,0:T(8,128)(2,1)}, u32[]{:S(2)}, u32[]{:S(2)}) collective-permute-start(bf16[6,2,36,320]{3,2,1,0:T(8,128)(2,1)S(1)} %get-tuple-element.227), channel_id=1, source_target_pairs={{1,0},{2,1},{3,2},{5,4},{6,5},{7,6},{9,8},{10,9},{11,10},{13,12},{... | collective-permute-start | bytes 829448 | tf_op jit(solution)/shard_map/ppermute | solution.py:17
  675.3 9.6 collective-permute-start.10
  715.9 283.2 %all-reduce.16.cloned.1.call-start = ((), (), s32[]{:S(2)}) async-start(), calls=%async_computation.1 | async-start | bytes 9502720 | tf_op jit(solution)/shard_map/psum | solution.py:195
  719.2 122.9 %copy-start.40 = (f32[6,320]{1,0:T(8,128)S(1)}, f32[6,320]{1,0:T(8,128)}, u32[]{:S(2)}) copy-start(f32[6,320]{1,0:T(8,128)} %get-tuple-element.234) | copy-start | bytes 23044
  842.0 157.1 %copy-start.173 = (f32[320]{0:T(512)S(1)}, f32[320]{0:T(512)}, u32[]{:S(2)}) copy-start(f32[320]{0:T(512)} %get-tuple-element.245) | copy-start | bytes 3844
  842.0 157.7 %copy-start.172 = (f32[320]{0:T(512)S(1)}, f32[320]{0:T(512)}, u32[]{:S(2)}) copy-start(f32[320]{0:T(512)} %get-tuple-element.246) | copy-start | bytes 3844
  842.0 160.2 %copy-start.41 = (f32[25,320]{1,0:T(8,128)S(1)}, f32[25,320]{1,0:T(8,128)}, u32[]{:S(2)}) copy-start(f32[25,320]{1,0:T(8,128)} %get-tuple-element.248) | copy-start | bytes 96004
  842.0 160.8 %copy-start.24 = (f32[49,320]{1,0:T(8,128)S(1)}, f32[49,320]{1,0:T(8,128)}, u32[]{:S(2)}) copy-start(f32[49,320]{1,0:T(8,128)} %get-tuple-element.249) | copy-start | bytes 188164
  842.0 165.1 %copy-start.177 = (f32[320]{0:T(512)S(1)}, f32[320]{0:T(512)}, u32[]{:S(2)}) copy-start(f32[320]{0:T(512)} %get-tuple-element.252) | copy-start | bytes 3844
  847.7 161.2 %copy-start.25 = (f32[9,1280]{1,0:T(8,128)S(1)}, f32[9,1280]{1,0:T(8,128)}, u32[]{:S(2)}) copy-start(f32[9,1280]{1,0:T(8,128)} %get-tuple-element.256) | copy-start | bytes 138244
  (173 other events, 1116.4 us)
Sparse Core Ops, SparseCore 0:
  716.0 125.9 all-reduce.13
  850.7 148.3 all-reduce.15
where the time goes:
time: 1030 us; the launch traced here: 1020 us
  other arithmetic  338 us (33%)
  waiting for transfers between devices  275 us (27%)
  matrix products  164 us (16%)
  blocking collectives  140 us (14%)
  starting transfers between devices  41.8 us (4%)
  local copies, waits for them, and re-layouts  41.3 us (4%)
  between operations  18.5 us (2%)
    psum x2, waiting for transfers between devices, body(): lax.psum((per_channel_sum(normalized_gradient), per_channel_sum(normalize...  274 us
    reduce_sum x5, other arithmetic, kernel_grad(): tap_sums.append(jnp.sum(window * grad_out, axis=(0, 1, 2)))  150 us
    dot_general x5, matrix products, project_back(): jnp.einsum('bhwd,cd->bhwc', grads, matrix, preferred_element_type=jnp.flo...  103 us
    psum x1, blocking collectives, body(): lax.psum((per_channel_sum(first_sum * alive), per_channel_sum(first_sum *...  57.5 us
    convert_element_type x1, other arithmetic, body(): active_low = jax.nn.gelu(mixed, approximate=False).astype(jnp.bfloat16)  50.1 us
    psum x1, blocking collectives, body(): lax.psum((per_channel_sum(input_images * alive), per_channel_sum(input_im...  42 us
    psum x1, blocking collectives, body(): lax.psum((per_channel_sum(grad_normed_two), per_channel_sum(grad_normed_t...  40.9 us
    dot_general x5, matrix products, project(): jnp.einsum('bhwc,cd->bhwd', values, matrix, preferred_element_type=jnp.fl...  37.4 us
  transfers between devices with their start and end apart: 14, of which 3 were waited for; matrix products, arithmetic and copies ran while one was open for 11% of the time, Pallas kernels for 0%

commit v1 on v0

--- a/solution.py
+++ b/solution.py
@@ -4,6 +4,42 @@
 from jax.sharding import PartitionSpec as P
 
 epsilon = 1e-05
+
+
+def exchange_steps():
+    return [
+        (axis, 1 << bit)
+        for axis in ("strip", "dp")
+        for bit in range(lax.axis_size(axis).bit_length() - 1)
+    ]
+
+
+def swapped(value, axis, bit):
+    return lax.ppermute(value, axis, [(i, i ^ bit) for i in range(lax.axis_size(axis))])
+
+
+def summed_everywhere(value):
+    for axis, bit in exchange_steps():
+        value = value + swapped(value, axis, bit)
+    return value
+
+
+def summed_by_halves(rows):
+    steps = exchange_steps()
+    part = rows.astype(jnp.bfloat16)
+    for axis, bit in steps:
+        upper = (lax.axis_index(axis) // bit) % 2
+        halves = part.reshape((2, part.shape[0] // 2) + part.shape[1:])
+        got = swapped(lax.dynamic_index_in_dim(halves, 1 - upper, 0, False), axis, bit)
+        kept = lax.dynamic_index_in_dim(halves, upper, 0, False)
+        part = (kept.astype(jnp.float32) + got.astype(jnp.float32)).astype(jnp.bfloat16)
+    for axis, bit in reversed(steps):
+        upper = (lax.axis_index(axis) // bit) % 2
+        got = swapped(part, axis, bit)
+        part = jnp.where(
+            upper == 0, jnp.concatenate([part, got]), jnp.concatenate([got, part])
+        )
+    return part.astype(jnp.float32)
 
 
 def extended(value, sides, width):
@@ -111,12 +147,13 @@
     taps_seven = kernel_seven.astype(jnp.float32)
     taps_three = kernel_three.astype(jnp.float32)
     input_images = images.astype(jnp.float32)
-    first_sums = lax.psum(
-        (
-            per_channel_sum(input_images * alive),
-            per_channel_sum(input_images * input_images * alive),
-        ),
-        ("dp", "strip"),
+    first_sums = summed_everywhere(
+        jnp.stack(
+            [
+                per_channel_sum(input_images * alive),
+                per_channel_sum(input_images * input_images * alive),
+            ]
+        )
     )
     first_mean = first_sums[0] / pixel_count
     first_inverse_deviation = lax.rsqrt(
@@ -138,9 +175,10 @@
     branch = project(gated_low, proj_out)
     attn = branch + normalized_input
     first_sum = input_images + layer_one * attn
-    second_sums = lax.psum(
-        (per_channel_sum(first_sum * alive), per_channel_sum(first_sum * first_sum * alive)),
-        ("dp", "strip"),
+    second_sums = summed_everywhere(
+        jnp.stack(
+            [per_channel_sum(first_sum * alive), per_channel_sum(first_sum * first_sum * alive)]
+        )
     )
     mean_two = second_sums[0] / pixel_count
     rstd_two = lax.rsqrt(second_sums[1] / pixel_count - mean_two * mean_two + epsilon)
@@ -165,9 +203,14 @@
     grad_kernel_three = kernel_grad(hidden_pad, grad_mixed, 3, 1)
     grad_normed_two = project_back(grad_hidden, fc_in)
     grad_fc_in = outer_sum(normed_two_low, grad_hidden)
-    grad_shift_two, grad_gain_two = lax.psum(
-        (per_channel_sum(grad_normed_two), per_channel_sum(grad_normed_two * yhat)), ("dp", "strip")
-    )
+    grad_shift_two, grad_gain_two = summed_everywhere(
+        jnp.stack(
+            [per_channel_sum(grad_normed_two), per_channel_sum(grad_normed_two * yhat)]
+        )
+    )
+    fc_grads = summed_by_halves(
+        jnp.concatenate([grad_fc_in, grad_fc_out.T]).reshape(-1, 128)
+    ).reshape(2, grad_fc_in.shape[0], -1)
     grad_first = grad_out + alive * rstd_two * gain_b * (
         grad_normed_two - (grad_shift_two + yhat * grad_gain_two) / pixel_count
     )
@@ -192,22 +235,47 @@
     grad_pre_low = gelu_grad(pre_gelu, grad_gelu).astype(jnp.bfloat16)
     normalized_gradient = grad_attn + project_back(grad_pre_low, proj_in)
     grad_proj_in = outer_sum(normed_low, grad_pre_low)
-    totals = lax.psum(
-        (
-            per_channel_sum(normalized_gradient),
-            per_channel_sum(normalized_gradient * centered_scaled_input),
-            grad_proj_in,
-            grad_kernel_five,
-            grad_kernel_seven,
-            grad_lka_proj,
-            grad_proj_out,
-            grad_scale_one,
-            grad_fc_in,
-            grad_kernel_three,
-            grad_fc_out,
-            grad_scale_two,
-        ),
-        ("dp", "strip"),
+    width = grad_proj_in.shape[0]
+    vectors = summed_everywhere(
+        jnp.stack(
+            [
+                per_channel_sum(normalized_gradient),
+                per_channel_sum(normalized_gradient * centered_scaled_input),
+                grad_scale_one,
+                grad_scale_two,
+            ]
+        )
+    )
+    matrices = summed_by_halves(
+        jnp.concatenate(
+            [
+                grad_proj_in,
+                grad_lka_proj,
+                grad_proj_out,
+                grad_kernel_five,
+                grad_kernel_seven,
+                grad_kernel_three.reshape(-1, width),
+                jnp.zeros((-(3 * width + 110) % 256, width), jnp.float32),
+            ]
+        )
+    )
+    ends = [0]
+    for count in (width, width, width, 25, 49, 36):
+        ends.append(ends[-1] + count)
+    pieces = [matrices[i:j] for i, j in zip(ends, ends[1:])]
+    totals = (
+        vectors[0],
+        vectors[1],
+        pieces[0],
+        pieces[3],
+        pieces[4],
+        pieces[1],
+        pieces[2],
+        vectors[2],
+        fc_grads[0],
+        pieces[5].reshape(9, -1),
+        fc_grads[1].T,
+        vectors[3],
     )
     gradient_first_shift = totals[0]
     gradient_first_gain = totals[1]

time: 1030 us -> 771 us (0.75)
  waiting for transfers between devices: 275 us -> 53.9 us
  blocking collectives: 140 us -> 0 us
  starting transfers between devices: 41.8 us -> 111 us
  local copies, waits for them, and re-layouts: 41.3 us -> 90.1 us
  matrix products: 164 us -> 148 us
  other arithmetic: 338 us -> 354 us
  between operations: 18.5 us -> 5.36 us
    psum x2 -> x0, waiting for transfers between devices: 274 us -> none  [body(): lax.psum((per_channel_sum(normalized_gradient), per_channel_sum(normalize...]
    psum x3 -> x0, blocking collectives: 140 us -> none  [the longest x1 57.5 us: body(): lax.psum((per_channel_sum(first_sum * alive), per_channel_sum(first_sum *...]
    ppermute x0 -> x40, starting transfers between devices: none -> 71.4 us  [swapped(): lax.ppermute(value, axis, [(i, i ^ bit) for i in range(lax.axis_size(axis...]
    ppermute x0 -> x40, waiting for transfers between devices: none -> 50.2 us  [swapped(): lax.ppermute(value, axis, [(i, i ^ bit) for i in range(lax.axis_size(axis...]
    another operation x86 -> x84, local copies, waits for them, and re-layouts: 21.5 us -> 54.3 us  [kernel_grad(): return jnp.stack(tap_sums)]
    unnamed x394 -> x389, local copies, waits for them, and re-layouts: 15.8 us -> 4.46 us
  transfers between devices with their start and end apart: 14 -> 52, of which waited for: 3 -> 27; matrix products, arithmetic and copies ran while one was open for 11% -> 45% of each run, Pallas kernels for 0% -> 0%
where the time goes in v1:
time: 771 us; the launch traced here: 762 us
  other arithmetic  354 us (46%)
  matrix products  148 us (19%)
  starting transfers between devices  111 us (14%)
  local copies, waits for them, and re-layouts  90.1 us (12%)
  waiting for transfers between devices  53.9 us (7%)
    reduce_sum x5, other arithmetic, kernel_grad(): tap_sums.append(jnp.sum(window * grad_out, axis=(0, 1, 2)))  157 us
    dot_general x5, matrix products, project_back(): jnp.einsum('bhwd,cd->bhwc', grads, matrix, preferred_element_type=jnp.flo...  97.9 us
    ppermute x40, starting transfers between devices, swapped(): lax.ppermute(value, axis, [(i, i ^ bit) for i in range(lax.axis_size(axis...  71.4 us
    another operation x84, local copies, waits for them, and re-layouts, kernel_grad(): return jnp.stack(tap_sums)  54.3 us
    ppermute x40, waiting for transfers between devices, swapped(): lax.ppermute(value, axis, [(i, i ^ bit) for i in range(lax.axis_size(axis...  50.2 us
    convert_element_type x1, other arithmetic, body(): active_low = jax.nn.gelu(mixed, approximate=False).astype(jnp.bfloat16)  50.1 us
    convert_element_type x1, other arithmetic, body(): depthwise(grad_mixed_pad, taps_three[::-1], 3, 1).astype(jnp.bfloat16)  35.6 us
    dot_general x5, matrix products, project(): jnp.einsum('bhwc,cd->bhwd', values, matrix, preferred_element_type=jnp.fl...  35 us
  transfers between devices with their start and end apart: 52, of which 27 were waited for; matrix products, arithmetic and copies ran while one was open for 45% of the time, Pallas kernels for 0%

profile of v1, /device:TPU:0, one launch (start us, length us, event | category | flops | bytes accessed | tf_op | source)
XLA Modules:
  0.0 762.0 jit_solution(14145066456031437482)
XLA Ops:
  26.4 10.5 %multiply_convert_fusion.3 = (bf16[6,9,36,320]{3,2,1,0:T(8,128)(2,1)S(1)}, f32[6,9,36,320]{3,2,1,0:T(8,128)}) fusion(bf16[320,320]{1,0:T(8,128)(2,1)} %param.21, bf16[6,9,36,320]{3,2,1,0:T(8,128)(2,1)} %param.17, f32[320]{0:T(512)} %convert_element_type.268, f32[320]{0:T(512)} %convert_element_type.267, f32[320]{0:T(512)S(1)} %add_rsqrt_fusion.1, ...), kind=kOutput, calls=%fused_computation.385 | convolution fusion | flops 442298880 | bytes 5186560 | tf_op jit(solution)/shard_map/bhwc,cd->bhwd/dot_general | solution.py:95
  43.5 11.9 %add_convert_fusion.3 = bf16[6,9,36,320]{3,2,1,0:T(8,128)(2,1)S(1)} fusion(f32[6,13,36,320]{3,2,1,0:T(8,128)S(1)} %maximum_convert_fusion.4, f32[320]{0:T(512)S(1)} %get-tuple-element.166, f32[320]{0:T(512)S(1)} %get-tuple-element.167, f32[320]{0:T(512)S(1)} %get-tuple-element.168, f32[320]{0:T(512)S(1)} %get-tuple-element.169, ...), kind=kLoop, calls=%fused_computation.384 | loop fusion | flops 31104000 | bytes 22676480 | tf_op jit(solution)/shard_map/convert_element_type | solution.py:168
  56.8 8.2 %collective-permute-start.7 = (bf16[6,9,36,320]{3,2,1,0:T(8,128)(2,1)S(1)}, bf16[6,9,36,320]{3,2,1,0:T(8,128)(2,1)}, u32[]{:S(2)}, u32[]{:S(2)}) collective-permute-start(bf16[6,9,36,320]{3,2,1,0:T(8,128)(2,1)S(1)} %add_convert_fusion.3), channel_id=1, source_target_pairs={{0,1},{1,2},{2,3},{4,5},{5,6},{6,7},{8,9},{9,10},{10,11},{12,13},{... | collective-permute-start | bytes 3732488 | tf_op jit(solution)/shard_map/ppermute | solution.py:52
  69.5 30.0 %add_convert_fusion.2 = bf16[6,9,36,320]{3,2,1,0:T(8,128)(2,1)} fusion(f32[6,27,36,320]{3,2,1,0:T(8,128)S(1)} %maximum_convert_fusion.2, f32[320]{0:T(512)S(1)} %get-tuple-element.108, f32[320]{0:T(512)S(1)} %get-tuple-element.109, f32[320]{0:T(512)S(1)} %get-tuple-element.110, f32[320]{0:T(512)S(1)} %get-tuple-element.111, f32[320]{0:T(512)S(1)} %get-tuple-element.112, ...), kind=kLoop, calls=%fused_computation.383 | loop fusion | flops 60963840 | bytes 34511360 | tf_op jit(solution)/shard_map/convert_element_type | solution.py:171
  102.6 5.3 multiply_reduce_fusion.87
  108.0 17.5 %collective-permute-start.9 = (f32[2,320]{1,0:T(2,128)S(1)}, f32[2,320]{1,0:T(2,128)S(1)}, u32[]{:S(2)}, u32[]{:S(2)}) collective-permute-start(f32[2,320]{1,0:T(2,128)S(1)} %pad_maximum_fusion.3), channel_id=1, source_target_pairs={{0,1},{1,0},{2,3},{3,2},{4,5},{5,4},{6,7},{7,6},{8,9},{9,8},{10,11... | collective-permute-start | bytes 7688 | tf_op jit(solution)/shard_map/ppermute | solution.py:18
  138.5 4.1 collective-permute-done.13
  152.2 5.3 maximum_convert_fusion
  157.5 50.1 %multiply_convert_fusion = (bf16[6,9,36,1280]{3,2,1,0:T(8,128)(2,1)}, f32[6,9,36,1280]{3,2,1,0:T(8,128)}, f32[6,9,36,1280]{3,2,1,0:T(8,128)}) fusion(f32[1280]{0:T(1024)S(1)} %get-tuple-element.157, f32[1280]{0:T(1024)S(1)} %get-tuple-element.158, f32[6,11,36,1280]{3,2,1,0:T(8,128)} %maximum_convert_fusion, f32[1280]{0:T(1024)S(1)} %get-tuple-element.159, ...), kind=kLoop, calls=%fused_computation.114 | loop fusion | flops 204042240 | bytes 71623680 | tf_op jit(solution)/shard_map/convert_element_type | solution.py:190
  207.6 53.7 %multiply_reduce_fusion = (bf16[1280]{0:T(1024)(128)(2,1)}, bf16[1280]{0:T(1024)(128)(2,1)}, bf16[1280]{0:T(1024)(128)(2,1)}, bf16[1280]{0:T(1024)(128)(2,1)}, b...) fusion(f32[6,11,36,1280]{3,2,1,0:T(8,128)} %maximum_convert_fus, ...), kind=kOutput, calls=%fused_computation.98 | convolution fusion | flops 1674627840 | bytes 75877632 | tf_op jit(solution)/shard_map/bhwd,cd->bhwc/dot_general | solution.py:99
  264.0 9.8 %collective-permute-start.16 = (bf16[6,1,36,1280]{3,2,1,0:T(8,128)(2,1)S(1)}, bf16[6,1,36,1280]{3,2,1,0:T(8,128)(2,1)S(1)}, u32[]{:S(2)}, u32[]{:S(2)}) collective-permute-start(bf16[6,1,36,1280]{3,2,1,0:T(8,128)(2,1)S(1)} %get-tuple-element.208), channel_id=1, source_target_pairs={{0,1},{1,2},{2,3},{4,5},{5,6},{6,7},{8,9},{9,10},{10,11},{12,13},{... | collective-permute-start | bytes 1658888 | tf_op jit(solution)/shard_map/ppermute | solution.py:52
  275.3 7.4 maximum_convert_fusion.1
  282.7 35.6 %fusion.3 = bf16[6,9,36,1280]{3,2,1,0:T(8,128)(2,1)} fusion(f32[6,11,36,1280]{3,2,1,0:T(8,128)} %maximum_convert_fusion.1, f32[1280]{0:T(1024)S(1)} %get-tuple-element.157, f32[1280]{0:T(1024)S(1)} %get-tuple-element.158, f32[1280]{0:T(1024)S(1)} %copy-done.31, f32[1280]{0:T(1024)S(1)} %copy-done.33, f32[1280]{0:T(1024)S(1)} %copy-done.35, ...), kind=kLoop, calls=%fused_computation.89 | loop fusion | flops 44789760 | bytes 51717120 | tf_op jit(solution)/shard_map/convert_element_type | solution.py:202
  318.4 8.7 %fusion.206 = (f32[320]{0:T(512)S(1)}, f32[320]{0:T(512)S(1)}, f32[6,9,36,320]{3,2,1,0:T(8,128)}) fusion(f32[320]{0:T(512)S(1)} %add_rsqrt_fusion, f32[6,9,36,320]{3,2,1,0:T(8,128)} %copy-done.22, f32[320]{0:T(512)S(1)} %get-tuple-element.196, bf16[6,9,36,1280]{3,2,1,0:T(8,128)(2,1)} %fusion.3, bf16[320,1280]{1,0:T(8,128)(2,1)S(1)} %copy-done.193), kind=kOutput, calls=%fused_computation.582 | convolution fusion | flops 1595634688 | bytes 10777600 | tf_op jit(solution)/shard_map/bhwd,cd->bhwc/dot_general | solution.py:99
  327.1 8.0 %collective-permute-start.18 = (f32[2,320]{1,0:T(2,128)S(1)}, f32[2,320]{1,0:T(2,128)S(1)}, u32[]{:S(2)}, u32[]{:S(2)}) collective-permute-start(f32[2,320]{1,0:T(2,128)S(1)} %pad_maximum_fusion.4), channel_id=1, source_target_pairs={{0,1},{1,0},{2,3},{3,2},{4,5},{5,4},{6,7},{7,6},{8,9},{9,8},{10,11... | collective-permute-start | bytes 7688 | tf_op jit(solution)/shard_map/ppermute | solution.py:18
  338.8 4.8 fusion.163
  346.4 5.7 fusion.162
  363.4 12.9 %multiply_reduce_fusion.83 = (f32[320]{0:T(512)}, bf16[6,9,36,320]{3,2,1,0:T(8,128)(2,1)}, f32[320]{0:T(512)}, f32[6,9,36,320]{3,2,1,0:T(8,128)S(1)}) fusion(bf16[6,9,36,320]{3,2,1,0:T(8,128)(2,1)} %param.33, f32[6]{0:T(128)} %compare_convert_fusion, f32[6,9,36,320]{3,2,1,0:T(8,128)} %copy-done.22, f32[320]{0:T(512)} %copy-done.184, ...), kind=kOutput, calls=%fused_computation.360 | convolution fusion | flops 1603721728 | bytes 18254108 | tf_op jit(solution)/shard_map/bhwc,cd->bhwd/dot_general | solution.py:95
  380.9 27.5 %multiply_reduce_fusion.9 = (bf16[320]{0:T(512)(128)(2,1)S(1)}, bf16[320]{0:T(512)(128)(2,1)S(1)}, bf16[320]{0:T(512)(128)(2,1)S(1)}, bf16[320]{0:T(512)(128)(2,...) fusion(f32[6,27,36,320]{3,2,1,0:T(8,128)} %copy-done.2, ...), kind=kOutput, calls=%fused_computation.286 | convolution fusion | flops 423008640 | bytes 28458240 | tf_op jit(solution)/shard_map/bhwd,cd->bhwc/dot_general | solution.py:99
  409.7 4.2 collective-permute-start.23
  414.0 29.3 %multiply_reduce_fusion.27 = (bf16[320]{0:T(512)(128)(2,1)S(1)}, bf16[320]{0:T(512)(128)(2,1)S(1)}, bf16[320]{0:T(512)(128)(2,1)S(1)}, bf16[320]{0:T(512)(128)(2...) fusion(f32[6,9,36,320]{3,2,1,0:T(8,128)} %get-tuple-element.236, ...), kind=kLoop, calls=%fused_computation.304 | loop fusion | flops 22389120 | bytes 19918080 | tf_op jit(solution)/shard_map/reduce_sum | solution.py:90
  443.3 22.3 %multiply_reduce_fusion.45 = (bf16[320]{0:T(512)(128)(2,1)S(1)}, bf16[320]{0:T(512)(128)(2,1)S(1)}, bf16[320]{0:T(512)(128)(2,1)S(1)}, bf16[320]{0:T(512)(128)(2...) fusion(f32[6,9,36,320]{3,2,1,0:T(8,128)} %get-tuple-element.236, ...), kind=kLoop, calls=%fused_computation.322 | loop fusion | flops 16169920 | bytes 19914880 | tf_op jit(solution)/shard_map/reduce_sum | solution.py:90
  506.2 6.9 maximum_convert_fusion.3
  513.4 78.5 %multiply_reduce_fusion.58 = (bf16[320]{0:T(512)(128)(2,1)S(1)}, bf16[320]{0:T(512)(128)(2,1)S(1)}, bf16[320]{0:T(512)(128)(2,1)S(1)}, bf16[320]{0:T(512)(128)(2...) fusion(f32[6,13,36,320]{3,2,1,0:T(8,128)} %copy-done.1, ...), kind=kLoop, calls=%fused_computation.335 | loop fusion | flops 72780160 | bytes 47173632 | tf_op jit(solution)/shard_map/reduce_sum | solution.py:90
  591.9 18.2 %multiply_reduce_fusion.68 = (bf16[320]{0:T(512)(128)(2,1)S(1)}, bf16[320]{0:T(512)(128)(2,1)S(1)}, bf16[320]{0:T(512)(128)(2,1)S(1)}, bf16[320]{0:T(512)(128)(2...) fusion(f32[6,9,36,320]{3,2,1,0:T(8,128)} %get-tuple-element.200, ...), kind=kLoop, calls=%fused_computation.345 | loop fusion | flops 13060480 | bytes 15996160 | tf_op jit(solution)/shard_map/reduce_sum | solution.py:90
  610.1 8.4 %multiply_reduce_fusion.78 = (bf16[320]{0:T(512)(128)(2,1)S(1)}, bf16[320]{0:T(512)(128)(2,1)S(1)}, bf16[320]{0:T(512)(128)(2,1)S(1)}, bf16[320]{0:T(512)(128)(2,1)S(1)}, bf16[320]{0:T(512)(128)(2,1)S(1)}) fusion(f32[6,9,36,320]{3,2,1,0:T(8,128)S(1)} %copy-done.12, f32[6,13,36,320]{3,2,1,0:T(8,128)} %copy-done.1), kind=kLoop, calls=%fused_computation.355 | loop fusion | flops 6219200 | bytes 10601600 | tf_op jit(solution)/shard_map/reduce_sum | solution.py:90
  645.3 23.0 %add_convert_fusion = bf16[6,9,36,320]{3,2,1,0:T(8,128)(2,1)} fusion(f32[6,13,36,320]{3,2,1,0:T(8,128)S(1)} %maximum_convert_fusion.5, f32[6,9,36,320]{3,2,1,0:T(8,128)S(1)} %copy-done.11, f32[6,9,36,320]{3,2,1,0:T(8,128)S(1)} %copy-done.9, f32[6,9,36,320]{3,2,1,0:T(8,128)} %get-tuple-element.232, f32[320]{0:T(512)S(1)} %copy-done.66, ...), kind=kLoop, calls=%fused_computation.362 | loop fusion | flops 76515840 | bytes 31788032 | tf_op jit(solution)/shard_map/convert_element_type | solution.py:235
  668.3 5.0 fusion.205
  675.9 7.8 %concatenate.92 = bf16[1280,320]{0,1:T(8,128)(2,1)} concatenate(bf16[320,320]{0,1:T(8,128)(2,1)} %fusion.166, bf16[320,320]{0,1:T(8,128)(2,1)S(1)} %fusion.167, bf16[320,320]{0,1:T(8,128)(2,1)S(1)} %fusion.168, bf16[1,320]{0,1:T(8,128)(2,1)} %stack.476, bf16[1,320]{0,1:T(8,128)(2,1)} %stack.477, bf16[1,320]{0,1:T(8,128)(2,1)} %stack.478, bf16[1,320]{0,1:T(8,128)(2,1)} %stack.479, ...), dimensions={0} | concatenate | bytes 1638400 | tf_op jit(solution)/shard_map/concatenate | solution.py:250
  695.4 5.3 collective-permute-done.33
  740.5 4.9 collective-permute-done.40
  745.7 4.7 fusion.36
  (687 shorter events, 221.0 us)
Async XLA Ops:
  18.8 7.5 collective-permute-start.4
  55.5 10.7 %collective-permute-start.8 = (bf16[6,9,36,320]{3,2,1,0:T(8,128)(2,1)S(1)}, bf16[6,9,36,320]{3,2,1,0:T(8,128)(2,1)S(1)}, u32[]{:S(2)}, u32[]{:S(2)}) collective-permute-start(bf16[6,9,36,320]{3,2,1,0:T(8,128)(2,1)S(1)} %add_convert_fusion.3), channel_id=1, source_target_pairs={{1,0},{2,1},{3,2},{5,4},{6,5},{7,6},{9,8},{10,9},{11,10},{13,12},{... | collective-permute-start | bytes 3732488 | tf_op jit(solution)/shard_map/ppermute | solution.py:53
  56.8 10.1 %collective-permute-start.7 = (bf16[6,9,36,320]{3,2,1,0:T(8,128)(2,1)S(1)}, bf16[6,9,36,320]{3,2,1,0:T(8,128)(2,1)}, u32[]{:S(2)}, u32[]{:S(2)}) collective-permute-start(bf16[6,9,36,320]{3,2,1,0:T(8,128)(2,1)S(1)} %add_convert_fusion.3), channel_id=1, source_target_pairs={{0,1},{1,2},{2,3},{4,5},{5,6},{6,7},{8,9},{9,10},{10,11},{12,13},{... | collective-permute-start | bytes 3732488 | tf_op jit(solution)/shard_map/ppermute | solution.py:52
  108.0 18.4 %collective-permute-start.9 = (f32[2,320]{1,0:T(2,128)S(1)}, f32[2,320]{1,0:T(2,128)S(1)}, u32[]{:S(2)}, u32[]{:S(2)}) collective-permute-start(f32[2,320]{1,0:T(2,128)S(1)} %pad_maximum_fusion.3), channel_id=1, source_target_pairs={{0,1},{1,0},{2,3},{3,2},{4,5},{5,4},{6,7},{7,6},{8,9},{9,8},{10,11... | collective-permute-start | bytes 7688 | tf_op jit(solution)/shard_map/ppermute | solution.py:18
  146.2 5.0 collective-permute-start.15
  262.7 11.3 %collective-permute-start.17 = (bf16[6,1,36,1280]{3,2,1,0:T(8,128)(2,1)S(1)}, bf16[6,1,36,1280]{3,2,1,0:T(8,128)(2,1)S(1)}, u32[]{:S(2)}, u32[]{:S(2)}) collective-permute-start(bf16[6,1,36,1280]{3,2,1,0:T(8,128)(2,1)S(1)} %get-tuple-element.209), channel_id=1, source_target_pairs={{1,0},{2,1},{3,2},{5,4},{6,5},{7,6},{9,8},{10,9},{11,10},{13,12},{... | collective-permute-start | bytes 1658888 | tf_op jit(solution)/shard_map/ppermute | solution.py:53
  264.0 11.3 %collective-permute-start.16 = (bf16[6,1,36,1280]{3,2,1,0:T(8,128)(2,1)S(1)}, bf16[6,1,36,1280]{3,2,1,0:T(8,128)(2,1)S(1)}, u32[]{:S(2)}, u32[]{:S(2)}) collective-permute-start(bf16[6,1,36,1280]{3,2,1,0:T(8,128)(2,1)S(1)} %get-tuple-element.208), channel_id=1, source_target_pairs={{0,1},{1,2},{2,3},{4,5},{5,6},{6,7},{8,9},{9,10},{10,11},{12,13},{... | collective-permute-start | bytes 1658888 | tf_op jit(solution)/shard_map/ppermute | solution.py:52
  327.1 8.8 %collective-permute-start.18 = (f32[2,320]{1,0:T(2,128)S(1)}, f32[2,320]{1,0:T(2,128)S(1)}, u32[]{:S(2)}, u32[]{:S(2)}) collective-permute-start(f32[2,320]{1,0:T(2,128)S(1)} %pad_maximum_fusion.4), channel_id=1, source_target_pairs={{0,1},{1,0},{2,3},{3,2},{4,5},{5,4},{6,7},{7,6},{8,9},{9,8},{10,11... | collective-permute-start | bytes 7688 | tf_op jit(solution)/shard_map/ppermute | solution.py:18
  336.0 8.8 %collective-permute-start.19 = (f32[2,320]{1,0:T(2,128)S(1)}, f32[2,320]{1,0:T(2,128)S(1)}, u32[]{:S(2)}, u32[]{:S(2)}) collective-permute-start(f32[2,320]{1,0:T(2,128)S(1)} %fusion.197), channel_id=1, source_target_pairs={{0,2},{1,3},{2,0},{3,1},{4,6},{5,7},{6,4},{7,5},{8,10},{9,11},{10,... | collective-permute-start | bytes 7688 | tf_op jit(solution)/shard_map/ppermute | solution.py:18
  344.8 7.3 collective-permute-start.20
  352.1 6.6 collective-permute-start.21
  359.2 106.4 %collective-permute-start.42 = (bf16[3200,128]{1,0:T(8,128)(2,1)S(1)}, bf16[3200,128]{1,0:T(8,128)(2,1)}, u32[]{:S(2)}, u32[]{:S(2)}) collective-permute-start(bf16[3200,128]{1,0:T(8,128)(2,1)S(1)} %dynamic-slice_bitcast_fusion), channel_id=1, source_target_pairs={{0,1},{1,0},{2,3},{3,2},{4,5},{5,4},{6,7},{7,6},{8,9},{9,8},{10,11... | collective-permute-start | bytes 2457608 | tf_op jit(solution)/shard_map/ppermute | solution.py:18
  408.4 97.7 %collective-permute-start.24 = (bf16[6,9,36,320]{3,2,1,0:T(8,128)(2,1)}, bf16[6,9,36,320]{3,2,1,0:T(8,128)(2,1)}, u32[]{:S(2)}, u32[]{:S(2)}) collective-permute-start(bf16[6,9,36,320]{3,2,1,0:T(8,128)(2,1)} %get-tuple-element.216), channel_id=1, source_target_pairs={{1,0},{2,1},{3,2},{5,4},{6,5},{7,6},{9,8},{10,9},{11,10},{13,12},{... | collective-permute-start | bytes 3732488 | tf_op jit(solution)/shard_map/ppermute | solution.py:53
  409.7 96.4 %collective-permute-start.23 = (bf16[6,9,36,320]{3,2,1,0:T(8,128)(2,1)}, bf16[6,9,36,320]{3,2,1,0:T(8,128)(2,1)}, u32[]{:S(2)}, u32[]{:S(2)}) collective-permute-start(bf16[6,9,36,320]{3,2,1,0:T(8,128)(2,1)} %get-tuple-element.216), channel_id=1, source_target_pairs={{0,1},{1,2},{2,3},{4,5},{5,6},{6,7},{8,9},{9,10},{10,11},{12,13},{... | collective-permute-start | bytes 3732488 | tf_op jit(solution)/shard_map/ppermute | solution.py:52
  467.1 37.9 %collective-permute-start.43 = (bf16[1600,128]{1,0:T(8,128)(2,1)S(1)}, bf16[1600,128]{1,0:T(8,128)(2,1)S(1)}, u32[]{:S(2)}, u32[]{:S(2)}) collective-permute-start(bf16[1600,128]{1,0:T(8,128)(2,1)S(1)} %dynamic-slice_bitcast_fusion.1), channel_id=1, source_target_pairs={{0,2},{1,3},{2,0},{3,1},{4,6},{5,7},{6,4},{7,5},{8,10},{9,11},{10,... | collective-permute-start | bytes 1228808 | tf_op jit(solution)/shard_map/ppermute | solution.py:18
  505.6 135.9 %collective-permute-start.44 = (bf16[800,128]{1,0:T(8,128)(2,1)S(1)}, bf16[800,128]{1,0:T(8,128)(2,1)S(1)}, u32[]{:S(2)}, u32[]{:S(2)}) collective-permute-start(bf16[800,128]{1,0:T(8,128)(2,1)S(1)} %dynamic-slice_bitcast_fusion.3), channel_id=1, source_target_pairs={{0,4},{4,0},{8,12},{12,8},{16,20},{20,16},{24,28},{28,24},{1,5},{5... | collective-permute-start | bytes 614408 | tf_op jit(solution)/shard_map/ppermute | solution.py:18
  618.6 24.2 %collective-permute-start.26 = (bf16[6,2,36,320]{3,2,1,0:T(8,128)(2,1)S(1)}, bf16[6,2,36,320]{3,2,1,0:T(8,128)(2,1)S(1)}, u32[]{:S(2)}, u32[]{:S(2)}) collective-permute-start(bf16[6,2,36,320]{3,2,1,0:T(8,128)(2,1)S(1)} %get-tuple-element.224), channel_id=1, source_target_pairs={{1,0},{2,1},{3,2},{5,4},{6,5},{7,6},{9,8},{10,9},{11,10},{13,12},{... | collective-permute-start | bytes 829448 | tf_op jit(solution)/shard_map/ppermute | solution.py:53
  619.9 22.9 %collective-permute-start.25 = (bf16[6,2,36,320]{3,2,1,0:T(8,128)(2,1)S(1)}, bf16[6,2,36,320]{3,2,1,0:T(8,128)(2,1)S(1)}, u32[]{:S(2)}, u32[]{:S(2)}) collective-permute-start(bf16[6,2,36,320]{3,2,1,0:T(8,128)(2,1)S(1)} %get-tuple-element.223), channel_id=1, source_target_pairs={{0,1},{1,2},{2,3},{4,5},{5,6},{6,7},{8,9},{9,10},{10,11},{12,13},{... | collective-permute-start | bytes 829448 | tf_op jit(solution)/shard_map/ppermute | solution.py:52
  642.3 47.9 %collective-permute-start.45 = (bf16[400,128]{1,0:T(8,128)(2,1)}, bf16[400,128]{1,0:T(8,128)(2,1)}, u32[]{:S(2)}, u32[]{:S(2)}) collective-permute-start(bf16[400,128]{1,0:T(8,128)(2,1)} %dynamic-slice_bitcast_fusion.5), channel_id=1, source_target_pairs={{0,8},{4,12},{8,0},{12,4},{16,24},{20,28},{24,16},{28,20},{1,9},{5... | collective-permute-start | bytes 307208 | tf_op jit(solution)/shard_map/ppermute | solution.py:18
  691.7 10.6 %collective-permute-start.46 = (bf16[200,128]{1,0:T(8,128)(2,1)}, bf16[200,128]{1,0:T(8,128)(2,1)S(1)}, u32[]{:S(2)}, u32[]{:S(2)}) collective-permute-start(bf16[200,128]{1,0:T(8,128)(2,1)} %dynamic-slice_bitcast_fusion.7), channel_id=1, source_target_pairs={{0,16},{4,20},{8,24},{12,28},{16,0},{20,4},{24,8},{28,12},{1,17},{... | collective-permute-start | bytes 153608 | tf_op jit(solution)/shard_map/ppermute | solution.py:18
  692.5 8.2 %collective-permute-start.33 = (bf16[320,320]{1,0:T(8,128)(2,1)S(1)}, bf16[320,320]{1,0:T(8,128)(2,1)S(1)}, u32[]{:S(2)}, u32[]{:S(2)}) collective-permute-start(bf16[320,320]{1,0:T(8,128)(2,1)S(1)} %dynamic-slice_bitcast_fusion.2), channel_id=1, source_target_pairs={{0,2},{1,3},{2,0},{3,1},{4,6},{5,7},{6,4},{7,5},{8,10},{9,11},{10,... | collective-permute-start | bytes 614408 | tf_op jit(solution)/shard_map/ppermute | solution.py:18
  694.2 27.3 %collective-permute-start.28 = (f32[4,320]{1,0:T(4,128)S(1)}, f32[4,320]{1,0:T(4,128)S(1)}, u32[]{:S(2)}, u32[]{:S(2)}) collective-permute-start(f32[4,320]{1,0:T(4,128)S(1)} %fusion.200), channel_id=1, source_target_pairs={{0,2},{1,3},{2,0},{3,1},{4,6},{5,7},{6,4},{7,5},{8,10},{9,11},{10,... | collective-permute-start | bytes 15368 | tf_op jit(solution)/shard_map/ppermute | solution.py:18
  700.8 4.9 collective-permute-start.34
  702.4 5.5 collective-permute-start.47
  710.3 5.6 collective-permute-start.36
  712.9 5.8 collective-permute-start.49
  715.9 5.1 collective-permute-start.37
  718.8 20.6 %collective-permute-start.50 = (bf16[1600,128]{1,0:T(8,128)(2,1)S(1)}, bf16[1600,128]{1,0:T(8,128)(2,1)S(1)}, u32[]{:S(2)}, u32[]{:S(2)}) collective-permute-start(bf16[1600,128]{1,0:T(8,128)(2,1)S(1)} %maximum_select_fusion.4), channel_id=1, source_target_pairs={{0,2},{1,3},{2,0},{3,1},{4,6},{5,7},{6,4},{7,5},{8,10},{9,11},{10,... | collective-permute-start | bytes 1228808 | tf_op jit(solution)/shard_map/ppermute | solution.py:18
  721.0 13.1 %collective-permute-start.38 = (bf16[80,320]{1,0:T(8,128)(2,1)S(1)}, bf16[80,320]{1,0:T(8,128)(2,1)S(1)}, u32[]{:S(2)}, u32[]{:S(2)}) collective-permute-start(bf16[80,320]{1,0:T(8,128)(2,1)S(1)} %maximum_select_fusion.9), channel_id=1, source_target_pairs={{0,8},{4,12},{8,0},{12,4},{16,24},{20,28},{24,16},{28,20},{1,9},{5... | collective-permute-start | bytes 153608 | tf_op jit(solution)/shard_map/ppermute | solution.py:18
  734.1 4.9 collective-permute-start.39
  739.2 6.3 collective-permute-start.40
  740.5 13.3 %collective-permute-start.51 = (bf16[3200,128]{1,0:T(8,128)(2,1)}, bf16[3200,128]{1,0:T(8,128)(2,1)}, u32[]{:S(2)}, u32[]{:S(2)}) collective-permute-start(bf16[3200,128]{1,0:T(8,128)(2,1)} %maximum_select_fusion.2), channel_id=1, source_target_pairs={{0,1},{1,0},{2,3},{3,2},{4,5},{5,4},{6,7},{7,6},{8,9},{9,8},{10,11... | collective-permute-start | bytes 2457608 | tf_op jit(solution)/shard_map/ppermute | solution.py:18
  (214 other events, 2952.1 us)

commit v2 on v1

v2 whole, which is shorter than its diff:
```python
import functools

import jax
import jax.numpy as jnp
from jax import lax
from jax.experimental import pallas as pl
from jax.experimental.pallas import tpu as pltpu
from jax.sharding import PartitionSpec as P

epsilon = 1e-05
lanes = 128
wide = jnp.float32
low = jnp.bfloat16


def exchange_steps():
    return [
        (axis, 1 << bit)
        for axis in ("strip", "dp")
        for bit in range(lax.axis_size(axis).bit_length() - 1)
    ]


def swapped(value, axis, bit):
    return lax.ppermute(value, axis, [(i, i ^ bit) for i in range(lax.axis_size(axis))])


def summed_everywhere(value):
    for axis, bit in exchange_steps():
        value = value + swapped(value, axis, bit)
    return value


def summed_by_halves(rows):
    steps = exchange_steps()
    part = rows.astype(low)
    for axis, bit in steps:
        upper = (lax.axis_index(axis) // bit) % 2
        halves = part.reshape((2, part.shape[0] // 2) + part.shape[1:])
        got = swapped(lax.dynamic_index_in_dim(halves, 1 - upper, 0, False), axis, bit)
        kept = lax.dynamic_index_in_dim(halves, upper, 0, False)
        part = (kept.astype(wide) + got.astype(wide)).astype(low)
    for axis, bit in reversed(steps):
        upper = (lax.axis_index(axis) // bit) % 2
        got = swapped(part, axis, bit)
        part = jnp.where(
            upper == 0, jnp.concatenate([part, got]), jnp.concatenate([got, part])
        )
    return part.astype(wide)


def neighbours(value, width):
    devices, length = lax.axis_size("strip"), value.shape[1]
    up = [(i, i + 1) for i in range(devices - 1)]
    down = [(j, i) for i, j in up]
    before = lax.ppermute(value[:, length - width :], "strip", up)
    after = lax.ppermute(value[:, :width], "strip", down)
    return before, after


def normal_parts(x):
    density = 0.3989422804014327 * jnp.exp(-0.5 * x * x)
    scale = 1.0 + 0.2316419 * jnp.abs(x)
    guess = pl.reciprocal(scale, approx=True)
    t = guess * (2.0 - scale * guess)
    poly = 1.781477937 + t * (-1.821255978 + t * 1.330274429)
    poly = t * (0.319381530 + t * (-0.356563782 + t * poly))
    tail = density * poly
    return jnp.where(x > 0, 1.0 - tail, tail), density


def window_sums(load, weight, across, spread, rows, back, center=None, add_tap=None):
    total = [None] * rows
    reach = spread * (across - 1)
    for j in range(across):
        shift = (j - across // 2) * spread * (-1 if back else 1)
        w = [weight(i * across + j) for i in range(across)]
        tap = [None] * across
        for r in range(rows + reach):
            v = load(r, shift)
            for i in range(across):
                o = r - reach + spread * i if back else r - spread * i
                if 0 <= o < rows:
                    term = v * w[i]
                    total[o] = term if total[o] is None else total[o] + term
                    if center is not None:
                        term = v * center[o]
                        tap[i] = term if tap[i] is None else tap[i] + term
        if center is not None:
            for i in range(across):
                add_tap(i * across + j, tap[i])
    return total


def lane_groups(width):
    return [(start, min(lanes, width - start)) for start in range(0, width, lanes)]


def fill_weights(weights, taps, width):
    weights[...] = jnp.zeros_like(weights)
    for g, (start, size) in enumerate(lane_groups(width)):
        for t in range(taps.shape[0]):
            weights[g, t, :, 0:size] = jnp.broadcast_to(
                taps[t : t + 1, start : start + size].astype(wide), (8, size)
            )


def store_taps(grad_taps, tap_sums, width):
    for g, (start, size) in enumerate(lane_groups(width)):
        for t in range(grad_taps.shape[0]):
            grad_taps[t : t + 1, start : start + size] = jnp.sum(
                tap_sums[g, t, :, 0:size], axis=0, keepdims=True
            )


def inside(rows, pitch, breadth, width):
    place = lax.broadcasted_iota(jnp.int32, (rows, pitch, width), 1)
    return jnp.where(place < breadth, 1.0, 0.0).reshape(rows * pitch, width)


def norm_of(stats, pixels):
    mean = stats[0:1, :] / pixels
    return mean, lax.rsqrt(stats[1:2, :] / pixels - mean * mean + epsilon)


def spec_image(*shape):
    return pl.BlockSpec((1,) + shape, lambda i: (i,) + (0,) * len(shape))


def spec_whole(*shape):
    return pl.BlockSpec(shape, lambda i: (0,) * len(shape))


def call(kernel, images, ins, outs, scratch, flops, moved, name, **sizes):
    return pl.pallas_call(
        functools.partial(kernel, **sizes),
        grid=(images,),
        in_specs=[spec for _, spec in ins],
        out_specs=[spec for _, _, spec in outs],
        out_shape=[jax.ShapeDtypeStruct(shape, dtype) for shape, dtype, _ in outs],
        scratch_shapes=[pltpu.VMEM(shape, dtype) for shape, dtype in scratch],
        compiler_params=pltpu.CompilerParams(vmem_limit_bytes=48 * 1024 * 1024),
        cost_estimate=pl.CostEstimate(flops=flops, bytes_accessed=moved, transcendentals=0),
        name=name,
    )(*[array for array, _ in ins])


def stats_kernel(flags, images, sums):
    image = pl.program_id(0)

    @pl.when(image == 0)
    def _():
        sums[...] = jnp.zeros_like(sums)

    alive = (image < flags[0]).astype(wide)
    total = jnp.zeros((images.shape[2], images.shape[3]), wide)
    square = total
    for r in range(images.shape[1]):
        value = images[0, r].astype(wide)
        total += value
        square += value * value
    sums[0:1, :] += jnp.sum(total, axis=0, keepdims=True) * alive
    sums[1:2, :] += jnp.sum(square, axis=0, keepdims=True) * alive


def front_kernel(
    flags,
    images,
    above,
    below,
    params,
    stats,
    proj_in,
    taps,
    gelu_low,
    pre_gelu,
    lka_mid,
    values,
    gelu,
    weights,
    mask,
    mid,
    *,
    rows,
    breadth,
    pitch,
    strips,
):
    width = images.shape[3]
    pixels = flags[3].astype(wide) * (rows * strips * breadth)
    mean, rstd = norm_of(stats, pixels)
    gain, shift = params[0:1, :], params[1:2, :]

    @pl.when(pl.program_id(0) == 0)
    def _():
        values[...] = jnp.zeros_like(values)
        gelu[...] = jnp.zeros_like(gelu)
        mid[...] = jnp.zeros_like(mid)
        fill_weights(weights, taps, width)
        mask[...] = inside(rows + 4, pitch, breadth, width)
        mask[0 : 2 * pitch, :] *= (flags[1] == 0).astype(wide)
        mask[(rows + 2) * pitch :, :] *= (flags[2] == 0).astype(wide)

    def place(at, value):
        values[at : at + breadth, :] = (value.astype(wide) - mean) * rstd * gain + shift

    for r in range(2):
        place(r * pitch, above[0, r])
        place((rows + 2 + r) * pitch, below[0, r])
    for r in range(rows):
        place((r + 2) * pitch, images[0, r])
    pre = jnp.dot(values[...].astype(low), proj_in[...], preferred_element_type=wide)
    pre_gelu[0] = pre[2 * pitch : (rows + 2) * pitch, :]
    cdf, _ = normal_parts(pre)
    rounded = (pre * cdf * mask[...]).astype(low).astype(wide)
    gelu_low[0] = rounded[2 * pitch : (rows + 2) * pitch, :].astype(low)
    for g, (start, size) in enumerate(lane_groups(width)):
        gelu[g, 8 : 8 + (rows + 4) * pitch, 0:size] = rounded[:, start : start + size]
    for g, (start, size) in enumerate(lane_groups(width)):

        def step(block, carry, g=g, start=start):
            base = pl.multiple_of(block * 8, 8)
            total = window_sums(
                lambda r, s: gelu[g, pl.ds(base + (8 + r * pitch + s), 8), :],
                lambda t: weights[g, t],
                5,
                1,
                rows,
                False,
            )
            for o in range(rows):
                mid[pl.ds(base + o * pitch, 8), start : start + lanes] = total[o]
            return carry

        lax.fori_loop(0, pitch // 8, step, 0)
    for r in range(rows):
        at = r * pitch
        lka_mid[0, r] = (
            mid[at : at + pitch, 0:width] * inside(1, pitch, breadth, width)
        ).astype(low)


def attend_kernel(
    flags,
    images,
    lka_mid,
    above,
    below,
    gelu_low,
    params,
    stats,
    lka_proj,
    proj_out,
    taps,
    lka_low,
    attend_out,
    attn_out,
    first_sum,
    sums,
    window,
    weights,
    lka,
    values,
    mask,
    *,
    rows,
    breadth,
    pitch,
    gap,
    strips,
):
    image = pl.program_id(0)
    width = images.shape[3]
    alive = (image < flags[0]).astype(wide)
    pixels = flags[3].astype(wide) * (rows * strips * breadth)
    mean, rstd = norm_of(stats, pixels)
    gain, shift, scale = params[0:1, :], params[1:2, :], params[2:3, :]

    @pl.when(image == 0)
    def _():
        window[...] = jnp.zeros_like(window)
        values[...] = jnp.zeros_like(values)
        lka[...] = jnp.zeros_like(lka)
        sums[...] = jnp.zeros_like(sums)
        fill_weights(weights, taps, width)
        mask[...] = inside(rows, pitch, breadth, width)

    for part, source in enumerate((above, lka_mid, below)):
        for r in range(rows):
            at = 16 + (part * rows + r) * gap
            for g, (start, size) in enumerate(lane_groups(width)):
                window[g, at : at + pitch, 0:size] = source[0, r, :, start : start + size].astype(
                    wide
                )
    for g, (start, size) in enumerate(lane_groups(width)):

        def step(block, carry, g=g, start=start):
            base = pl.multiple_of(block * 8, 8)
            total = window_sums(
                lambda r, s: window[g, pl.ds(base + (16 + r * gap + s), 8), :],
                lambda t: weights[g, t],
                7,
                3,
                rows,
                False,
            )
            for o in range(rows):
                lka[pl.ds(base + o * pitch, 8), start : start + lanes] = total[o]
            return carry

        lax.fori_loop(0, pitch // 8, step, 0)
    for r in range(rows):
        values[r * pitch : r * pitch + breadth, :] = images[0, r].astype(wide)
    low_lka = lka[:, 0:width].astype(low)
    lka_low[0] = low_lka
    attend = jnp.dot(low_lka, lka_proj[...], preferred_element_type=wide)
    attend_out[0] = attend
    gated = (gelu_low[0].astype(wide) * attend).astype(low)
    branch = jnp.dot(gated, proj_out[...], preferred_element_type=wide)
    attn = (branch + ((values[...] - mean) * rstd * gain + shift)) * mask[...]
    attn_out[0] = attn
    first = values[...] + scale * attn
    first_sum[0] = first
    sums[0:1, :] += jnp.sum(first, axis=0, keepdims=True) * alive
    sums[1:2, :] += jnp.sum(first * first, axis=0, keepdims=True) * alive


def gate_kernel(
    flags,
    first_sum,
    attn,
    cot,
    grad_normed,
    lka_low,
    attend,
    gelu_low,
    params,
    stats,
    grad_stats,
    lka_proj,
    proj_out,
    grad_first,
    grad_lka,
    grad_direct,
    grad_lka_proj,
    grad_proj_out,
    sums,
    values,
    mask,
    *,
    rows,
    breadth,
    pitch,
    strips,
):
    image = pl.program_id(0)
    width = cot.shape[3]
    alive = (image < flags[0]).astype(wide)
    pixels = flags[3].astype(wide) * (rows * strips * breadth)
    mean, rstd = norm_of(stats, pixels)
    scale, gain = params[2:3, :], params[3:4, :]

    @pl.when(image == 0)
    def _():
        values[...] = jnp.zeros_like(values)
        mask[...] = inside(rows, pitch, breadth, width)
        sums[...] = jnp.zeros_like(sums)
        grad_lka_proj[...] = jnp.zeros_like(grad_lka_proj)
        grad_proj_out[...] = jnp.zeros_like(grad_proj_out)

    for r in range(rows):
        values[r * pitch : r * pitch + breadth, :] = cot[0, r].astype(wide)
    yhat = (first_sum[0] - mean) * rstd
    inner = grad_normed[0] - (grad_stats[0:1, :] + yhat * grad_stats[1:2, :]) / pixels
    first = alive * (values[...] + rstd * gain * inner) * mask[...]
    grad_first[0] = first
    sums[0:1, :] += jnp.sum(first * attn[0], axis=0, keepdims=True)
    branch = (first * scale).astype(low)
    gated_back = lax.dot_general(
        branch, proj_out[...], (((1,), (1,)), ((), ())), preferred_element_type=wide
    )
    gelu = gelu_low[0].astype(wide)
    gated = gelu * attend[0]
    grad_proj_out[...] += jnp.dot(
        gated.T.astype(low), branch, preferred_element_type=wide
    )
    grad_direct[0] = gated_back * attend[0]
    back = (gated_back * gelu).astype(low)
    lka = lax.dot_general(
        back, lka_proj[...], (((1,), (1,)), ((), ())), preferred_element_type=wide
    )
    grad_lka_proj[...] += jnp.dot(
        lka_low[0].astype(wide).T.astype(low), back, preferred_element_type=wide
    )
    for r in range(rows):
        grad_lka[0, r] = lka[r * pitch : (r + 1) * pitch, :].astype(low)


def seven_kernel(
    grad_lka,
    above,
    below,
    lka_mid,
    taps,
    grad_mid,
    grad_taps,
    window,
    middle,
    out,
    weights,
    tap_sums,
    *,
    rows,
    breadth,
    pitch,
    gap,
):
    image = pl.program_id(0)
    width = grad_lka.shape[3]

    @pl.when(image == 0)
    def _():
        window[...] = jnp.zeros_like(window)
        middle[...] = jnp.zeros_like(middle)
        tap_sums[...] = jnp.zeros_like(tap_sums)
        fill_weights(weights, taps, width)

    for g, (start, size) in enumerate(lane_groups(width)):
        for part, source in enumerate((above, grad_lka, below)):
            for r in range(rows):
                at = 16 + (part * rows + r) * gap
                window[g, at : at + pitch, 0:size] = source[0, r, :, start : start + size].astype(
                    wide
                )
        for r in range(rows):
            middle[g, r * pitch : (r + 1) * pitch, 0:size] = lka_mid[
                0, r, :, start : start + size
            ].astype(wide)
    for g, (start, size) in enumerate(lane_groups(width)):

        def step(block, carry, g=g, start=start):
            base = pl.multiple_of(block * 8, 8)

            def add_tap(t, value):
                tap_sums[g, t] += value

            total = window_sums(
                lambda r, s: window[g, pl.ds(base + (16 + r * gap + s), 8), :],
                lambda t: weights[g, t],
                7,
                3,
                rows,
                True,
                [middle[g, pl.ds(base + p * pitch, 8), :] for p in range(rows)],
                add_tap,
            )
            for o in range(rows):
                out[pl.ds(base + o * pitch, 8), start : start + lanes] = total[o]
            return carry

        lax.fori_loop(0, pitch // 8, step, 0)
    for r in range(rows):
        at = r * pitch
        grad_mid[0, r] = (
            out[at : at + pitch, 0:width] * inside(1, pitch, breadth, width)
        ).astype(low)

    @pl.when(image == pl.num_programs(0) - 1)
    def _():
        store_taps(grad_taps, tap_sums, width)


def five_kernel(
    flags,
    images,
    grad_mid,
    above,
    below,
    gelu_low,
    pre_gelu,
    grad_direct,
    grad_first,
    params,
    stats,
    proj_in,
    taps,
    grad_partial,
    grad_proj_in,
    grad_taps,
    sums,
    window,
    middle,
    out,
    weights,
    tap_sums,
    values,
    mask,
    *,
    rows,
    breadth,
    pitch,
    strips,
):
    image = pl.program_id(0)
    width = images.shape[3]
    alive = (image < flags[0]).astype(wide)
    pixels = flags[3].astype(wide) * (rows * strips * breadth)
    mean, rstd = norm_of(stats, pixels)
    gain, shift, scale = params[0:1, :], params[1:2, :], params[2:3, :]

    @pl.when(image == 0)
    def _():
        window[...] = jnp.zeros_like(window)
        middle[...] = jnp.zeros_like(middle)
        tap_sums[...] = jnp.zeros_like(tap_sums)
        values[...] = jnp.zeros_like(values)
        sums[...] = jnp.zeros_like(sums)
        grad_proj_in[...] = jnp.zeros_like(grad_proj_in)
        mask[...] = inside(rows, pitch, breadth, width)
        fill_weights(weights, taps, width)

    for g, (start, size) in enumerate(lane_groups(width)):
        for r in range(2):
            at = 8 + r * pitch
            window[g, at : at + pitch, 0:size] = above[0, r, :, start : start + size].astype(wide)
            at = 8 + (rows + 2 + r) * pitch
            window[g, at : at + pitch, 0:size] = below[0, r, :, start : start + size].astype(wide)
        for r in range(rows):
            at = 8 + (r + 2) * pitch
            window[g, at : at + pitch, 0:size] = grad_mid[0, r, :, start : start + size].astype(
                wide
            )
        middle[g, :, 0:size] = gelu_low[0, :, start : start + size].astype(wide)
    for g, (start, size) in enumerate(lane_groups(width)):

        def step(block, carry, g=g, start=start):
            base = pl.multiple_of(block * 8, 8)

            def add_tap(t, value):
                tap_sums[g, t] += value

            total = window_sums(
                lambda r, s: window[g, pl.ds(base + (8 + r * pitch + s), 8), :],
                lambda t: weights[g, t],
                5,
                1,
                rows,
                True,
                [middle[g, pl.ds(base + p * pitch, 8), :] for p in range(rows)],
                add_tap,
            )
            for o in range(rows):
                out[pl.ds(base + o * pitch, 8), start : start + lanes] = total[o]
            return carry

        lax.fori_loop(0, pitch // 8, step, 0)
    for r in range(rows):
        values[r * pitch : r * pitch + breadth, :] = images[0, r].astype(wide)
    pre = pre_gelu[0]
    cdf, density = normal_parts(pre)
    grad_pre = ((grad_direct[0] + out[:, 0:width]) * (cdf + pre * density)).astype(low)
    xhat = (values[...] - mean) * rstd
    normed = (xhat * gain + shift) * mask[...]
    grad_proj_in[...] += jnp.dot(normed.T.astype(low), grad_pre, preferred_element_type=wide)
    back = lax.dot_general(
        grad_pre, proj_in[...], (((1,), (1,)), ((), ())), preferred_element_type=wide
    )
    first = grad_first[0]
    grad_normed = (first * scale + back) * mask[...]
    sums[0:1, :] += jnp.sum(grad_normed, axis=0, keepdims=True)
    sums[1:2, :] += jnp.sum(grad_normed * xhat, axis=0, keepdims=True)
    grad_partial[0] = first + alive * rstd * gain * grad_normed

    @pl.when(image == pl.num_programs(0) - 1)
    def _():
        store_taps(grad_taps, tap_sums, width)


def last_kernel(
    flags, images, grad_partial, params, stats, grad_stats, grad_images, *, rows, breadth, pitch, strips
):
    alive = (pl.program_id(0) < flags[0]).astype(wide)
    pixels = flags[3].astype(wide) * (rows * strips * breadth)
    mean, rstd = norm_of(stats, pixels)
    factor = alive * rstd * params[0:1, :] / pixels
    for r in range(rows):
        xhat = (images[0, r].astype(wide) - mean) * rstd
        part = grad_partial[0, r * pitch : r * pitch + breadth, :]
        grad_images[0, r] = part - factor * (grad_stats[0:1, :] + xhat * grad_stats[1:2, :])


def mlp_kernel(
    flags,
    first_sum,
    above,
    below,
    cot,
    cot_above,
    cot_below,
    params,
    stats,
    fc_in,
    fc_out,
    taps,
    out_image,
    grad_normed,
    sums,
    grad_in,
    grad_out,
    grad_taps,
    normed_wide,
    mlp_wide,
    normed_low,
    normed_turned,
    grads_low,
    grads_turned,
    hidden,
    from_active,
    grad_mixed,
    active,
    grad_hidden,
    mlp_sum,
    normed_sum,
    weights,
    tap_sums,
    in_sum,
    out_sum,
    *,
    rows,
    breadth,
    pitch,
    strips,
):
    image = pl.program_id(0)
    alive = (image < flags[0]).astype(jnp.float32)
    upper = (flags[1] == 0).astype(jnp.float32)
    lower = (flags[2] == 0).astype(jnp.float32)
    groups = fc_in.shape[1] // (2 * lanes)
    blocks = pitch // 8
    pixels = flags[3].astype(wide) * (rows * strips * breadth)
    mean_two, rstd_two = norm_of(stats, pixels)
    gain_two, shift_two, scale_two = params[3:4, :], params[4:5, :], params[5:6, :]

    @pl.when(image == 0)
    def _():
        normed_wide[...] = jnp.zeros_like(normed_wide)
        mlp_wide[...] = jnp.zeros_like(mlp_wide)
        hidden[...] = jnp.zeros_like(hidden)
        grad_mixed[...] = jnp.zeros_like(grad_mixed)
        tap_sums[...] = jnp.zeros_like(tap_sums)
        in_sum[...] = jnp.zeros_like(in_sum)
        out_sum[...] = jnp.zeros_like(out_sum)
        sums[...] = jnp.zeros_like(sums)
        fill_weights(weights, taps, taps.shape[1])

    def normalized(value):
        return (value - mean_two) * rstd_two * gain_two + shift_two

    for r in range(2):
        normed_wide[r * pitch : r * pitch + breadth, :] = upper * normalized(
            above[0, r, 0:breadth, :]
        )
        at = (rows + 2 + r) * pitch
        normed_wide[at : at + breadth, :] = lower * normalized(below[0, r, 0:breadth, :])
    for r in range(rows):
        at = (r + 2) * pitch
        normed_wide[at : at + breadth, :] = normalized(first_sum[0, r, 0:breadth, :])
        at = (r + 1) * pitch
        mlp_wide[at : at + breadth, :] = cot[0, r].astype(jnp.float32) * alive * scale_two
    mlp_wide[0:breadth, :] = cot_above[0, 0].astype(jnp.float32) * alive * scale_two
    at = (rows + 1) * pitch
    mlp_wide[at : at + breadth, :] = cot_below[0, 0].astype(jnp.float32) * alive * scale_two
    normed_low[...] = normed_wide[...].astype(jnp.bfloat16)
    grads_low[...] = mlp_wide[...].astype(jnp.bfloat16)
    inner = normed_wide[2 * pitch : (rows + 2) * pitch, :]
    normed_turned[...] = inner.T.astype(jnp.bfloat16)
    grads_turned[...] = mlp_wide[pitch : (rows + 1) * pitch, :].T.astype(jnp.bfloat16)
    mlp_sum[...] = jnp.zeros_like(mlp_sum)
    normed_sum[...] = jnp.zeros_like(normed_sum)

    def group_step(group, carry):
        columns = pl.ds(pl.multiple_of(group * (2 * lanes), 2 * lanes), 2 * lanes)
        in_part = fc_in[:, columns]
        out_part = fc_out[columns, :]
        hid = jnp.dot(normed_low[...], in_part, preferred_element_type=jnp.float32)
        hid = hid.astype(jnp.bfloat16).astype(jnp.float32)
        act = lax.dot_general(
            grads_low[...],
            out_part,
            (((1,), (1,)), ((), ())),
            preferred_element_type=jnp.float32,
        )
        for half in range(2):
            lane = slice(half * lanes, (half + 1) * lanes)
            hidden[half, 8 : 8 + (rows + 4) * pitch, :] = hid[:, lane]
            from_active[half] = act[:, lane]

        for half in range(2):
            lane = slice(half * lanes, (half + 1) * lanes)
            place = group * 2 + half

            def forward(block, carry, half=half, lane=lane, place=place):
                base = pl.multiple_of(block * 8, 8)
                mixed = window_sums(
                    lambda r, s: hidden[half, pl.ds(base + (8 + r * pitch + s), 8), :],
                    lambda t: weights[place, t],
                    3,
                    1,
                    rows + 2,
                    False,
                )
                for o in range(rows + 2):
                    x = mixed[o]
                    cdf, density = normal_parts(x)
                    slope = cdf + x * density
                    grad_mixed[half, pl.ds(base + (8 + o * pitch), 8), :] = (
                        from_active[half, pl.ds(base + o * pitch, 8), :] * slope
                    )
                    if 1 <= o <= rows:
                        active[pl.ds(base + (o - 1) * pitch, 8), lane] = x * cdf
                return carry

            lax.fori_loop(0, blocks, forward, 0)

            def backward(block, carry, half=half, lane=lane, place=place):
                base = pl.multiple_of(block * 8, 8)

                def add_tap(t, value):
                    tap_sums[place, t] += value

                total = window_sums(
                    lambda r, s: grad_mixed[half, pl.ds(base + (8 + r * pitch + s), 8), :],
                    lambda t: weights[place, t],
                    3,
                    1,
                    rows,
                    True,
                    [hidden[half, pl.ds(base + (8 + (p + 2) * pitch), 8), :] for p in range(rows)],
                    add_tap,
                )
                for p in range(rows):
                    grad_hidden[pl.ds(base + p * pitch, 8), lane] = total[p]
                return carry

            lax.fori_loop(0, blocks, backward, 0)

        act_low = active[...].astype(jnp.bfloat16)
        hid_low = grad_hidden[...].astype(jnp.bfloat16)
        mlp_sum[...] += jnp.dot(act_low, out_part, preferred_element_type=jnp.float32)
        normed_sum[...] += lax.dot_general(
            hid_low, in_part, (((1,), (1,)), ((), ())), preferred_element_type=jnp.float32
        )
        part_in = jnp.dot(normed_turned[...], hid_low, preferred_element_type=jnp.float32)
        part_out = jnp.dot(grads_turned[...], act_low, preferred_element_type=jnp.float32)
        for half in range(2):
            lane = slice(half * lanes, (half + 1) * lanes)
            in_sum[group * 2 + half] += part_in[:, lane]
            out_sum[group * 2 + half] += part_out[:, lane]
        return carry

    lax.fori_loop(0, groups, group_step, 0)

    scale_grad = jnp.zeros_like(scale_two)
    shift_grad = jnp.zeros_like(scale_two)
    gain_grad = jnp.zeros_like(scale_two)
    for r in range(rows):
        mlp = mlp_sum[r * pitch : r * pitch + breadth, :]
        back = normed_sum[r * pitch : r * pitch + breadth, :]
        first = first_sum[0, r, 0:breadth, :]
        out_image[0, r] = (alive * (first + scale_two * mlp)).astype(jnp.bfloat16)
        grad_normed[0, r * pitch : r * pitch + breadth, :] = back
        grad_normed[0, r * pitch + breadth : (r + 1) * pitch, :] = jnp.zeros(
            (pitch - breadth, back.shape[1]), wide
        )
        grad = cot[0, r].astype(jnp.float32) * alive
        scale_grad += jnp.sum(grad * mlp, axis=0, keepdims=True)
        shift_grad += jnp.sum(back, axis=0, keepdims=True)
        gain_grad += jnp.sum(back * (first - mean_two) * rstd_two, axis=0, keepdims=True)
    sums[0:1, :] += shift_grad
    sums[1:2, :] += gain_grad
    sums[2:3, :] += scale_grad

    @pl.when(image == pl.num_programs(0) - 1)
    def _():
        grad_in[...] = in_sum[...].astype(jnp.bfloat16)
        grad_out[...] = out_sum[...].astype(jnp.bfloat16)
        store_taps(grad_taps, tap_sums, taps.shape[1])


def mlp_block(
    flags, first_sum, above, below, cot, cot_above, cot_below, params, stats, fc_in, fc_out, taps
):
    images, rows, breadth, width = cot.shape
    pitch = first_sum.shape[2]
    deep = fc_in.shape[1]
    groups = deep // lanes
    count = images * rows * breadth
    return call(
        mlp_kernel,
        images,
        [
            (flags, pl.BlockSpec(memory_space=pltpu.SMEM)),
            (first_sum, spec_image(rows, pitch, width)),
            (above, spec_image(2, pitch, width)),
            (below, spec_image(2, pitch, width)),
            (cot, spec_image(rows, breadth, width)),
            (cot_above, spec_image(1, breadth, width)),
            (cot_below, spec_image(1, breadth, width)),
            (params, spec_whole(8, width)),
            (stats, spec_whole(2, width)),
            (fc_in, spec_whole(width, deep)),
            (fc_out, spec_whole(deep, width)),
            (taps, spec_whole(9, deep)),
        ],
        [
            (cot.shape, low, spec_image(rows, breadth, width)),
            ((images, rows * pitch, width), wide, spec_image(rows * pitch, width)),
            ((8, width), wide, spec_whole(8, width)),
            ((groups, width, lanes), low, spec_whole(groups, width, lanes)),
            ((groups, width, lanes), low, spec_whole(groups, width, lanes)),
            ((9, deep), wide, spec_whole(9, deep)),
        ],
        [
            (((rows + 4) * pitch, width), wide),
            (((rows + 2) * pitch, width), wide),
            (((rows + 4) * pitch, width), low),
            ((width, rows * pitch), low),
            (((rows + 2) * pitch, width), low),
            ((width, rows * pitch), low),
            ((2, (rows + 4) * pitch + 16, lanes), wide),
            ((2, (rows + 2) * pitch, lanes), wide),
            ((2, (rows + 2) * pitch + 16, lanes), wide),
            ((rows * pitch, 2 * lanes), wide),
            ((rows * pitch, 2 * lanes), wide),
            ((rows * pitch, width), wide),
            ((rows * pitch, width), wide),
            ((groups, 9, 8, lanes), wide),
            ((groups, 9, 8, lanes), wide),
            ((groups, width, lanes), wide),
            ((groups, width, lanes), wide),
        ],
        12 * count * width * deep,
        16 * count * width,
        "mlp",
        rows=rows,
        breadth=breadth,
        pitch=pitch,
        strips=lax.axis_size("strip"),
    )


def body(
    images,
    counts,
    gain_one,
    shift_one,
    proj_in,
    kernel_five,
    kernel_seven,
    lka_proj,
    proj_out,
    scale_one,
    gain_two,
    shift_two,
    fc_in,
    kernel_three,
    fc_out,
    scale_two,
    cotangent,
):
    slots, rows, breadth, width = images.shape
    strips = lax.axis_size("strip")
    strip = lax.axis_index("strip")
    pitch = -(-(breadth + 2) // 8) * 8
    gap = -(-(breadth + 9) // 8) * 8
    flat = rows * pitch
    flags = jnp.stack(
        [
            counts[lax.axis_index("dp")],
            (strip == 0).astype(jnp.int32),
            (strip == strips - 1).astype(jnp.int32),
            jnp.sum(counts),
        ]
    )
    blank = jnp.zeros_like(gain_one)
    params = jnp.stack(
        [gain_one, shift_one, scale_one, gain_two, shift_two, scale_two, blank, blank]
    ).astype(wide)
    sizes = dict(rows=rows, breadth=breadth, pitch=pitch)
    smem = pl.BlockSpec(memory_space=pltpu.SMEM)
    vec = spec_whole(8, width)
    two = spec_whole(2, width)
    square = spec_whole(width, width)
    image_spec = spec_image(rows, breadth, width)
    flat_spec = spec_image(flat, width)
    row_spec = spec_image(rows, pitch, width)
    flat_shape = (slots, flat, width)
    row_shape = (slots, rows, pitch, width)
    groups = len(lane_groups(width))
    area = slots * rows * breadth
    matmul = 2 * area * width * width

    image_above, image_below = neighbours(images, 2)
    cot_above, cot_below = neighbours(cotangent, 1)
    (first_part,) = call(
        stats_kernel,
        slots,
        [(flags, smem), (images, image_spec)],
        [((2, width), wide, two)],
        [],
        3 * area * width,
        2 * area * width,
        "input_sums",
    )
    first_stats = summed_everywhere(first_part)
    gelu_low, pre_gelu, lka_mid = call(
        front_kernel,
        slots,
        [
            (flags, smem),
            (images, image_spec),
            (image_above, spec_image(2, breadth, width)),
            (image_below, spec_image(2, breadth, width)),
            (params, vec),
            (first_stats, two),
            (proj_in, square),
            (kernel_five, spec_whole(*kernel_five.shape)),
        ],
        [
            (flat_shape, low, flat_spec),
            (flat_shape, wide, flat_spec),
            (row_shape, low, row_spec),
        ],
        [
            (((rows + 4) * pitch, width), wide),
            ((groups, (rows + 4) * pitch + 16, lanes), wide),
            ((groups, 25, 8, lanes), wide),
            (((rows + 4) * pitch, width), wide),
            ((flat, groups * lanes), wide),
        ],
        matmul + 50 * area * width,
        10 * area * width,
        "normed_to_five",
        strips=strips,
        **sizes,
    )
    mid_above, mid_below = neighbours(lka_mid, rows)
    lka_low, attend, attn, first_sum, second_part = call(
        attend_kernel,
        slots,
        [
            (flags, smem),
            (images, image_spec),
            (lka_mid, row_spec),
            (mid_above, row_spec),
            (mid_below, row_spec),
            (gelu_low, flat_spec),
            (params, vec),
            (first_stats, two),
            (lka_proj, square),
            (proj_out, square),
            (kernel_seven, spec_whole(*kernel_seven.shape)),
        ],
        [
            (flat_shape, low, flat_spec),
            (flat_shape, wide, flat_spec),
            (flat_shape, wide, flat_spec),
            (flat_shape, wide, flat_spec),
            ((2, width), wide, two),
        ],
        [
            ((groups, 3 * rows * gap + 48, lanes), wide),
            ((groups, 49, 8, lanes), wide),
            ((flat, groups * lanes), wide),
            ((flat, width), wide),
            ((flat, width), wide),
        ],
        2 * matmul + 98 * area * width,
        22 * area * width,
        "seven_to_first_sum",
        strips=strips,
        gap=gap,
        **sizes,
    )
    first_rows = first_sum.reshape(row_shape)
    sum_above, sum_below = neighbours(first_rows, 2)
    second_stats = summed_everywhere(second_part)
    out_image, grad_normed_two, mlp_sums, fc_in_part, fc_out_part, grad_kernel_three = mlp_block(
        flags,
        first_rows,
        sum_above,
        sum_below,
        cotangent,
        cot_above,
        cot_below,
        params,
        second_stats,
        fc_in,
        fc_out,
        kernel_three,
    )
    grad_second = summed_everywhere(mlp_sums[:2])
    fc_grads = summed_by_halves(
        jnp.concatenate([fc_in_part.reshape(-1, lanes), fc_out_part.reshape(-1, lanes)])
    ).reshape((2,) + fc_in_part.shape)
    fc_grads = fc_grads.transpose(0, 2, 1, 3).reshape(2, width, fc_in.shape[1])
    grad_first, grad_lka, grad_direct, grad_lka_proj, grad_proj_out, scale_sums = call(
        gate_kernel,
        slots,
        [
            (flags, smem),
            (first_sum, flat_spec),
            (attn, flat_spec),
            (cotangent, image_spec),
            (grad_normed_two, flat_spec),
            (lka_low, flat_spec),
            (attend, flat_spec),
            (gelu_low, flat_spec),
            (params, vec),
            (second_stats, two),
            (grad_second, two),
            (lka_proj, square),
            (proj_out, square),
        ],
        [
            (flat_shape, wide, flat_spec),
            (row_shape, low, row_spec),
            (flat_shape, wide, flat_spec),
            ((width, width), wide, square),
            ((width, width), wide, square),
            ((8, width), wide, vec),
        ],
        [((flat, width), wide), ((flat, width), wide)],
        4 * matmul,
        30 * area * width,
        "gate_backward",
        strips=strips,
        **sizes,
    )
    lka_above, lka_below = neighbours(grad_lka, rows)
    grad_mid, grad_kernel_seven = call(
        seven_kernel,
        slots,
        [
            (grad_lka, row_spec),
            (lka_above, row_spec),
            (lka_below, row_spec),
            (lka_mid, row_spec),
            (kernel_seven, spec_whole(*kernel_seven.shape)),
        ],
        [
            (row_shape, low, row_spec),
            (kernel_seven.shape, wide, spec_whole(*kernel_seven.shape)),
        ],
        [
            ((groups, 3 * rows * gap + 48, lanes), wide),
            ((groups, flat, lanes), wide),
            ((flat, groups * lanes), wide),
            ((groups, 49, 8, lanes), wide),
            ((groups, 49, 8, lanes), wide),
        ],
        200 * area * width,
        10 * area * width,
        "seven_backward",
        gap=gap,
        **sizes,
    )
    five_above, five_below = neighbours(grad_mid, 2)
    grad_partial, grad_proj_in, grad_kernel_five, last_sums = call(
        five_kernel,
        slots,
        [
            (flags, smem),
            (images, image_spec),
            (grad_mid, row_spec),
            (five_above, spec_image(2, pitch, width)),
            (five_below, spec_image(2, pitch, width)),
            (gelu_low, flat_spec),
            (pre_gelu, flat_spec),
            (grad_direct, flat_spec),
            (grad_first, flat_spec),
            (params, vec),
            (first_stats, two),
            (proj_in, square),
            (kernel_five, spec_whole(*kernel_five.shape)),
        ],
        [
            (flat_shape, wide, flat_spec),
            ((width, width), wide, square),
            (kernel_five.shape, wide, spec_whole(*kernel_five.shape)),
            ((8, width), wide, vec),
        ],
        [
            ((groups, (rows + 4) * pitch + 16, lanes), wide),
            ((groups, flat, lanes), wide),
            ((flat, groups * lanes), wide),
            ((groups, 25, 8, lanes), wide),
            ((groups, 25, 8, lanes), wide),
            ((flat, width), wide),
            ((flat, width), wide),
        ],
        2 * matmul + 100 * area * width,
        24 * area * width,
        "five_backward",
        strips=strips,
        **sizes,
    )
    vectors = summed_everywhere(
        jnp.concatenate([last_sums[0:2], scale_sums[0:1], mlp_sums[2:3]])
    )
    matrices = summed_by_halves(
        jnp.concatenate(
            [
                grad_proj_in,
                grad_lka_proj,
                grad_proj_out,
                grad_kernel_five,
                grad_kernel_seven,
                grad_kernel_three.reshape(-1, width),
                jnp.zeros((-(3 * width + 110) % 256, width), wide),
            ]
        )
    )
    ends = [0]
    for count in (width, width, width, 25, 49, 36):
        ends.append(ends[-1] + count)
    pieces = [matrices[i:j] for i, j in zip(ends, ends[1:])]
    (grad_images,) = call(
        last_kernel,
        slots,
        [
            (flags, smem),
            (images, image_spec),
            (grad_partial, flat_spec),
            (params, vec),
            (first_stats, two),
            (vectors, spec_whole(4, width)),
        ],
        [(images.shape, wide, image_spec)],
        [],
        6 * area * width,
        10 * area * width,
        "input_gradient",
        strips=strips,
        **sizes,
    )
    return (
        out_image,
        grad_images,
        vectors[1],
        vectors[0],
        pieces[0],
        pieces[3],
        pieces[4],
        pieces[1],
        pieces[2],
        vectors[2],
        grad_second[1],
        grad_second[0],
        fc_grads[0],
        pieces[5].reshape(9, -1),
        fc_grads[1].T,
        vectors[3],
    )


def solution(mesh):
    split = P("dp", "strip", None, None)
    return jax.shard_map(
        body,
        mesh=mesh,
        in_specs=(split,) + (P(),) * 15 + (split,),
        out_specs=(split, split) + (P(),) * 14,
        check_vma=False,
    )
```

time: 771 us -> 428 us (0.56); the launches traced: 762 us -> 427 us
  other arithmetic: 354 us -> 16.9 us
  Pallas kernels: 0 us -> 186 us
  matrix products: 148 us -> 0 us
  local copies, waits for them, and re-layouts: 90.1 us -> 44.7 us
  waiting for transfers between devices: 53.9 us -> 81 us
  starting transfers between devices: 111 us -> 96.4 us
    pallas_call x0 -> x8, Pallas kernels: none -> 186 us  [call(): pl.pallas_call(functools.partial(kernel, **sizes), grid=(images,), in_spe...]
    convert_element_type x33 -> x12, other arithmetic: 183 us -> 6.58 us  [the longest x10 4.84 us: summed_by_halves(): part = (kept.astype(wide) + got.astype(wide)).astype(low)]
    reduce_sum x7 -> x1, other arithmetic: 160 us -> 1.29 us  [body(): jnp.sum(counts)]
    dot_general x15 -> x0, matrix products: 148 us -> none  [the longest x5 97.9 us: project_back(): jnp.einsum('bhwd,cd->bhwc', grads, matrix, preferred_element_type=jnp.flo...]
    another operation x95 -> x8, local copies, waits for them, and re-layouts: 54.3 us -> 0.07 us  [body(): jnp.stack([gain_one, shift_one, scale_one, gain_two, shift_two, scale_two...]
    ppermute x40, waiting for transfers between devices: 50.2 us -> 74.8 us  [swapped(): lax.ppermute(value, axis, [(i, i ^ bit) for i in range(lax.axis_size(axis...]
    unnamed x389 -> x73, local copies, waits for them, and re-layouts: 4.46 us -> 22.3 us
    ppermute x40, starting transfers between devices: 71.4 us -> 58.2 us  [swapped(): lax.ppermute(value, axis, [(i, i ^ bit) for i in range(lax.axis_size(axis...]
  transfers between devices with their start and end apart: 52 -> 52, of which waited for: 27 -> 30; matrix products, arithmetic and copies ran while one was open for 45% -> 8% of each run, Pallas kernels for 0% -> 16%
where the time goes in v2:
time: 428 us; the launch traced here: 427 us
  Pallas kernels  186 us (43%)
  starting transfers between devices  96.4 us (23%)
  waiting for transfers between devices  81 us (19%)
  local copies, waits for them, and re-layouts  44.7 us (10%)
  other arithmetic  16.9 us (4%)
    pallas_call x8, Pallas kernels, call(): pl.pallas_call(functools.partial(kernel, **sizes), grid=(images,), in_spe...  186 us
    ppermute x40, waiting for transfers between devices, swapped(): lax.ppermute(value, axis, [(i, i ^ bit) for i in range(lax.axis_size(axis...  74.8 us
    ppermute x40, starting transfers between devices, swapped(): lax.ppermute(value, axis, [(i, i ^ bit) for i in range(lax.axis_size(axis...  58.2 us
    ppermute x6, starting transfers between devices, neighbours(): before = lax.ppermute(value[:, length - width:], 'strip', up)  30.3 us
    unnamed x73, local copies, waits for them, and re-layouts  22.3 us
  transfers between devices with their start and end apart: 52, of which 30 were waited for; matrix products, arithmetic and copies ran while one was open for 8% of the time, Pallas kernels for 16%

profile of v2, /device:TPU:0, one launch (start us, length us, event | category | flops | bytes accessed | tf_op | source)
XLA Modules:
  0.0 426.8 jit_solution(10574525748404712732)
XLA Ops:
  1.9 2.4 collective-permute-start
  12.1 3.3 collective-permute-start.2
  27.0 2.6 collective-permute-start.6
  32.5 15.3 %normed_to_five.1 = (bf16[6,360,320]{2,1,0:T(8,128)(2,1)S(1)}, f32[6,360,320]{2,1,0:T(8,128)}, bf16[6,9,40,320]{3,2,1,0:T(8,128)(2,1)S(1)}) custom-call(s32[4]{0:T(128)S(1)} %pad_add_fusion.flags, bf16[6,9,36,320]{3,2,1,0:T(8,128)(2,1)S(1)} %copy-done.1, bf16[6,2,36,320]{3,2,1,0:T(8,128)(2,1)S(1)} %collective-permute-done.above, ...), custom_call_target="tpu_custom_call" | custom-call | flops 429235200 | bytes 6220800 | tf_op jit(solution)/shard_map/normed_to_five/pallas_call | solution.py:135
  53.5 4.5 %collective-permute-done.8.below = bf16[6,9,40,320]{3,2,1,0:T(8,128)(2,1)S(1)} collective-permute-done((bf16[6,9,40,320]{3,2,1,0:T(8,128)(2,1)S(1)}, bf16[6,9,40,320]{3,2,1,0:T(8,128)(2,1)S(1)}, u32[]{:S(2)}, u32[]{:S(2)}) %collective-permute-start.8) | collective-permute-done | bytes 1382432 | tf_op jit(solution)/shard_map/ppermute | solution.py:57
  61.1 22.1 %seven_to_first_sum.1 = (bf16[6,360,320]{2,1,0:T(8,128)(2,1)S(1)}, f32[6,360,320]{2,1,0:T(8,128)}, f32[6,360,320]{2,1,0:T(8,128)}, f32[6,360,320]{2,1,0:T(8,128)}, f32[2,320]{1,0:T(2,128)S(1)}) custom-call(s32[4]{0:T(128)S(1)} %pad_add_fusion.flags, bf16[6,9,36,320]{3,2,1,0:T(8,128)(2,1)S(1)} %copy-done.1, ...), custom_call_target="tpu_custom_call" | custom-call | flops 857226240 | bytes 13685760 | tf_op jit(solution)/shard_map/seven_to_first_sum/pallas_call | solution.py:135
  83.2 3.1 fusion.12
  86.3 20.7 %collective-permute-start.9 = (f32[6,2,40,320]{3,2,1,0:T(8,128)}, f32[6,2,40,320]{3,2,1,0:T(8,128)}, u32[]{:S(2)}, u32[]{:S(2)}) collective-permute-start(f32[6,2,40,320]{3,2,1,0:T(8,128)} %get-tuple-element.91), channel_id=1, source_target_pairs={{0,1},{1,2},{2,3},{4,5},{5,6},{6,7},{8,9},{9,10},{10,11},{12,13},{... | collective-permute-start | bytes 1843208 | tf_op jit(solution)/shard_map/ppermute | solution.py:56
  110.0 3.0 collective-permute-start.11
  118.2 3.1 collective-permute-done.14
  122.8 2.1 collective-permute-done.15
  128.5 2.6 collective-permute-start.17
  134.2 79.5 %mlp.1 = (bf16[6,9,36,320]{3,2,1,0:T(8,128)(2,1)}, f32[6,360,320]{2,1,0:T(8,128)}, f32[8,320]{1,0:T(8,128)S(1)}, bf16[10,320,128]{2,1,0:T(8,128)(2,1)S(1)}, bf16...) custom-call(s32[4]{0:T(128)S(1)} %pad_add_fusion.flags, f32[6,9,40,320]{3,2,1,0:T(8,128)} %bitcast.79, ...), custom_call_target="tpu_custom_call" | custom-call | flops 9555148800 | bytes 9953280 | tf_op jit(solution)/shard_map/mlp/pallas_call | solution.py:135
  218.4 3.1 collective-permute-done.19
  228.7 2.6 collective-permute-start.22
  235.1 12.2 %gate_backward.1 = (f32[6,360,320]{2,1,0:T(8,128)}, bf16[6,9,40,320]{3,2,1,0:T(8,128)(2,1)}, f32[6,360,320]{2,1,0:T(8,128)}, f32[320,320]{1,0:T(8,128)S(1)}, f32...) custom-call(s32[4]{0:T(128)S(1)} %pad_add_fusion.flags, f32[6,360,320]{2,1,0:T(8,128)} %get-tuple-element.44.first_sum, ...), custom_call_target="tpu_custom_call" | custom-call | flops 1592524800 | bytes 18662400 | tf_op jit(solution)/shard_map/gate_backward/pallas_call | solution.py:135
  254.8 3.3 collective-permute-start.43
  263.8 19.4 %collective-permute-done.43 = bf16[1600,128]{1,0:T(8,128)(2,1)} collective-permute-done((bf16[1600,128]{1,0:T(8,128)(2,1)}, bf16[1600,128]{1,0:T(8,128)(2,1)}, u32[]{:S(2)}, u32[]{:S(2)}) %collective-permute-start.43) | collective-permute-done | bytes 409632 | tf_op jit(solution)/shard_map/ppermute | solution.py:25
  286.0 28.4 %seven_backward.1 = (bf16[6,9,40,320]{3,2,1,0:T(8,128)(2,1)S(1)}, f32[49,320]{1,0:T(8,128)S(1)}) custom-call(bf16[6,9,40,320]{3,2,1,0:T(8,128)(2,1)} %get-tuple-element.52.grad_lka, bf16[6,9,40,320]{3,2,1,0:T(8,128)(2,1)S(1)} %collective-permute-done.23.above, bf16[6,9,40,320]{3,2,1,0:T(8,128)(2,1)} %collective-permute-done.24.below, ...), custom_call_target="tpu_custom_call" | custom-call | flops 124416000 | bytes 6220800 | tf_op jit(solution)/shard_map/seven_backward/pallas_call | solution.py:135
  319.7 24.2 %five_backward.1 = (f32[6,360,320]{2,1,0:T(8,128)}, f32[320,320]{1,0:T(8,128)S(1)}, f32[25,320]{1,0:T(8,128)S(1)}, f32[8,320]{1,0:T(8,128)S(1)}) custom-call(s32[4]{0:T(128)S(1)} %pad_add_fusion.flags, bf16[6,9,36,320]{3,2,1,0:T(8,128)(2,1)S(1)} %copy-done.1, bf16[6,9,40,320]{3,2,1,0:T(8,128)(2,1)S(1)} %get-tuple-element.53.grad_mid, ...), custom_call_target="tpu_custom_call" | custom-call | flops 858470400 | bytes 14929920 | tf_op jit(solution)/shard_map/five_backward/pallas_call | solution.py:135
  346.7 5.4 %collective-permute-start.32 = (bf16[640,320]{1,0:T(8,128)(2,1)S(1)}, bf16[640,320]{1,0:T(8,128)(2,1)}, u32[]{:S(2)}, u32[]{:S(2)}) collective-permute-start(bf16[640,320]{1,0:T(8,128)(2,1)S(1)} %dynamic-slice_bitcast_fusion.1), channel_id=1, source_target_pairs={{0,1},{1,0},{2,3},{3,2},{4,5},{5,4},{6,7},{7,6},{8,9},{9,8},{10,11... | collective-permute-start | bytes 1228808 | tf_op jit(solution)/shard_map/ppermute | solution.py:25
  353.2 2.7 collective-permute-start.46
  357.1 2.2 collective-permute-done.46
  360.9 3.8 collective-permute-done.33
  367.1 2.7 collective-permute-done.34
  380.4 3.6 collective-permute-done.37
  384.0 2.3 collective-permute-start.38
  389.9 3.1 collective-permute-done.28
  394.3 2.4 collective-permute-done.29
  406.8 3.6 input_gradient.1
  414.7 2.7 copy.37
  419.2 2.7 copy.38
  (245 shorter events, 130.6 us)
Async XLA Ops:
  1.9 29.6 %collective-permute-start = (bf16[6,2,36,320]{3,2,1,0:T(8,128)(2,1)S(1)}, bf16[6,2,36,320]{3,2,1,0:T(8,128)(2,1)S(1)}, u32[]{:S(2)}, u32[]{:S(2)}) collective-permute-start(bf16[6,2,36,320]{3,2,1,0:T(8,128)(2,1)S(1)} %get-tuple-element.102), channel_id=1, source_target_pairs={{0,1},{1,2},{2,3},{4,5},{5,6},{6,7},{8,9},{9,10},{10,11},{12,13},{... | collective-permute-start | bytes 829448 | tf_op jit(solution)/shard_map/ppermute | solution.py:56
  4.3 27.2 %collective-permute-start.1 = (bf16[6,2,36,320]{3,2,1,0:T(8,128)(2,1)S(1)}, bf16[6,2,36,320]{3,2,1,0:T(8,128)(2,1)S(1)}, u32[]{:S(2)}, u32[]{:S(2)}) collective-permute-start(bf16[6,2,36,320]{3,2,1,0:T(8,128)(2,1)S(1)} %get-tuple-element.101), channel_id=1, source_target_pairs={{1,0},{2,1},{3,2},{5,4},{6,5},{7,6},{9,8},{10,9},{11,10},{13,12},{... | collective-permute-start | bytes 829448 | tf_op jit(solution)/shard_map/ppermute | solution.py:57
  27.0 4.5 %collective-permute-start.6 = (f32[2,320]{1,0:T(2,128)S(1)}, f32[2,320]{1,0:T(2,128)S(1)}, u32[]{:S(2)}, u32[]{:S(2)}) collective-permute-start(f32[2,320]{1,0:T(2,128)S(1)} %add.188), channel_id=1, source_target_pairs={{0,16},{4,20},{8,24},{12,28},{16,0},{20,4},{24,8},{28,12},{1,17},{... | collective-permute-start | bytes 7688 | tf_op jit(solution)/shard_map/ppermute | solution.py:25
  50.4 7.5 %collective-permute-start.8 = (bf16[6,9,40,320]{3,2,1,0:T(8,128)(2,1)S(1)}, bf16[6,9,40,320]{3,2,1,0:T(8,128)(2,1)S(1)}, u32[]{:S(2)}, u32[]{:S(2)}) collective-permute-start(bf16[6,9,40,320]{3,2,1,0:T(8,128)(2,1)S(1)} %get-tuple-element.42.lka_mid), channel_id=1, source_target_pairs={{1,0},{2,1},{3,2},{5,4},{6,5},{7,6},{9,8},{10,9},{11,10},{13,12},{... | collective-permute-start | bytes 4147208 | tf_op jit(solution)/shard_map/ppermute | solution.py:57
  86.3 46.7 %collective-permute-start.9 = (f32[6,2,40,320]{3,2,1,0:T(8,128)}, f32[6,2,40,320]{3,2,1,0:T(8,128)}, u32[]{:S(2)}, u32[]{:S(2)}) collective-permute-start(f32[6,2,40,320]{3,2,1,0:T(8,128)} %get-tuple-element.91), channel_id=1, source_target_pairs={{0,1},{1,2},{2,3},{4,5},{5,6},{6,7},{8,9},{9,10},{10,11},{12,13},{... | collective-permute-start | bytes 1843208 | tf_op jit(solution)/shard_map/ppermute | solution.py:56
  107.0 26.0 %collective-permute-start.10 = (f32[6,2,40,320]{3,2,1,0:T(8,128)}, f32[6,2,40,320]{3,2,1,0:T(8,128)}, u32[]{:S(2)}, u32[]{:S(2)}) collective-permute-start(f32[6,2,40,320]{3,2,1,0:T(8,128)} %get-tuple-element.90), channel_id=1, source_target_pairs={{1,0},{2,1},{3,2},{5,4},{6,5},{7,6},{9,8},{10,9},{11,10},{13,12},{... | collective-permute-start | bytes 1843208 | tf_op jit(solution)/shard_map/ppermute | solution.py:57
  110.0 23.0 %collective-permute-start.11 = (bf16[6,1,36,320]{3,2,1,0:T(8,128)(2,1)}, bf16[6,1,36,320]{3,2,1,0:T(8,128)(2,1)S(1)}, u32[]{:S(2)}, u32[]{:S(2)}) collective-permute-start(bf16[6,1,36,320]{3,2,1,0:T(8,128)(2,1)} %get-tuple-element.100), channel_id=1, source_target_pairs={{0,1},{1,2},{2,3},{4,5},{5,6},{6,7},{8,9},{9,10},{10,11},{12,13},{... | collective-permute-start | bytes 414728 | tf_op jit(solution)/shard_map/ppermute | solution.py:56
  113.1 20.0 %collective-permute-start.12 = (bf16[6,1,36,320]{3,2,1,0:T(8,128)(2,1)S(1)}, bf16[6,1,36,320]{3,2,1,0:T(8,128)(2,1)S(1)}, u32[]{:S(2)}, u32[]{:S(2)}) collective-permute-start(bf16[6,1,36,320]{3,2,1,0:T(8,128)(2,1)S(1)} %get-tuple-element.99), channel_id=1, source_target_pairs={{1,0},{2,1},{3,2},{5,4},{6,5},{7,6},{9,8},{10,9},{11,10},{13,12},{... | collective-permute-start | bytes 414728 | tf_op jit(solution)/shard_map/ppermute | solution.py:57
  116.4 4.9 %collective-permute-start.14 = (f32[2,320]{1,0:T(2,128)S(1)}, f32[2,320]{1,0:T(2,128)S(1)}, u32[]{:S(2)}, u32[]{:S(2)}) collective-permute-start(f32[2,320]{1,0:T(2,128)S(1)} %add.190), channel_id=1, source_target_pairs={{0,2},{1,3},{2,0},{3,1},{4,6},{5,7},{6,4},{7,5},{8,10},{9,11},{10,... | collective-permute-start | bytes 7688 | tf_op jit(solution)/shard_map/ppermute | solution.py:25
  215.9 35.8 %collective-permute-start.42 = (bf16[3200,128]{1,0:T(8,128)(2,1)}, bf16[3200,128]{1,0:T(8,128)(2,1)}, u32[]{:S(2)}, u32[]{:S(2)}) collective-permute-start(bf16[3200,128]{1,0:T(8,128)(2,1)} %dynamic-slice_bitcast_fusion), channel_id=1, source_target_pairs={{0,1},{1,0},{2,3},{3,2},{4,5},{5,4},{6,7},{7,6},{8,9},{9,8},{10,11... | collective-permute-start | bytes 2457608 | tf_op jit(solution)/shard_map/ppermute | solution.py:25
  248.9 37.1 %collective-permute-start.23 = (bf16[6,9,40,320]{3,2,1,0:T(8,128)(2,1)}, bf16[6,9,40,320]{3,2,1,0:T(8,128)(2,1)S(1)}, u32[]{:S(2)}, u32[]{:S(2)}) collective-permute-start(bf16[6,9,40,320]{3,2,1,0:T(8,128)(2,1)} %get-tuple-element.52.grad_lka), channel_id=1, source_target_pairs={{0,1},{1,2},{2,3},{4,5},{5,6},{6,7},{8,9},{9,10},{10,11},{12,13},{... | collective-permute-start | bytes 4147208 | tf_op jit(solution)/shard_map/ppermute | solution.py:56
  250.2 35.8 %collective-permute-start.24 = (bf16[6,9,40,320]{3,2,1,0:T(8,128)(2,1)}, bf16[6,9,40,320]{3,2,1,0:T(8,128)(2,1)}, u32[]{:S(2)}, u32[]{:S(2)}) collective-permute-start(bf16[6,9,40,320]{3,2,1,0:T(8,128)(2,1)} %get-tuple-element.52.grad_lka), channel_id=1, source_target_pairs={{1,0},{2,1},{3,2},{5,4},{6,5},{7,6},{9,8},{10,9},{11,10},{13,12},{... | collective-permute-start | bytes 4147208 | tf_op jit(solution)/shard_map/ppermute | solution.py:57
  254.8 28.5 %collective-permute-start.43 = (bf16[1600,128]{1,0:T(8,128)(2,1)}, bf16[1600,128]{1,0:T(8,128)(2,1)}, u32[]{:S(2)}, u32[]{:S(2)}) collective-permute-start(bf16[1600,128]{1,0:T(8,128)(2,1)} %dynamic-slice_bitcast_fusion.2), channel_id=1, source_target_pairs={{0,2},{1,3},{2,0},{3,1},{4,6},{5,7},{6,4},{7,5},{8,10},{9,11},{10,... | collective-permute-start | bytes 1228808 | tf_op jit(solution)/shard_map/ppermute | solution.py:25
  284.4 32.8 %collective-permute-start.44 = (bf16[800,128]{1,0:T(8,128)(2,1)S(1)}, bf16[800,128]{1,0:T(8,128)(2,1)S(1)}, u32[]{:S(2)}, u32[]{:S(2)}) collective-permute-start(bf16[800,128]{1,0:T(8,128)(2,1)S(1)} %dynamic-slice_bitcast_fusion.4), channel_id=1, source_target_pairs={{0,4},{4,0},{8,12},{12,8},{16,20},{20,16},{24,28},{28,24},{1,5},{5... | collective-permute-start | bytes 614408 | tf_op jit(solution)/shard_map/ppermute | solution.py:25
  314.5 5.2 %collective-permute-start.25 = (bf16[6,2,40,320]{3,2,1,0:T(8,128)(2,1)S(1)}, bf16[6,2,40,320]{3,2,1,0:T(8,128)(2,1)S(1)}, u32[]{:S(2)}, u32[]{:S(2)}) collective-permute-start(bf16[6,2,40,320]{3,2,1,0:T(8,128)(2,1)S(1)} %get-tuple-element.98), channel_id=1, source_target_pairs={{0,1},{1,2},{2,3},{4,5},{5,6},{6,7},{8,9},{9,10},{10,11},{12,13},{... | collective-permute-start | bytes 921608 | tf_op jit(solution)/shard_map/ppermute | solution.py:56
  318.0 34.1 %collective-permute-start.45 = (bf16[400,128]{1,0:T(8,128)(2,1)}, bf16[400,128]{1,0:T(8,128)(2,1)}, u32[]{:S(2)}, u32[]{:S(2)}) collective-permute-start(bf16[400,128]{1,0:T(8,128)(2,1)} %dynamic-slice_bitcast_fusion.6), channel_id=1, source_target_pairs={{0,8},{4,12},{8,0},{12,4},{16,24},{20,28},{24,16},{28,20},{1,9},{5... | collective-permute-start | bytes 307208 | tf_op jit(solution)/shard_map/ppermute | solution.py:25
  346.7 9.1 %collective-permute-start.32 = (bf16[640,320]{1,0:T(8,128)(2,1)S(1)}, bf16[640,320]{1,0:T(8,128)(2,1)}, u32[]{:S(2)}, u32[]{:S(2)}) collective-permute-start(bf16[640,320]{1,0:T(8,128)(2,1)S(1)} %dynamic-slice_bitcast_fusion.1), channel_id=1, source_target_pairs={{0,1},{1,0},{2,3},{3,2},{4,5},{5,4},{6,7},{7,6},{8,9},{9,8},{10,11... | collective-permute-start | bytes 1228808 | tf_op jit(solution)/shard_map/ppermute | solution.py:25
  353.2 6.2 %collective-permute-start.46 = (bf16[200,128]{1,0:T(8,128)(2,1)S(1)}, bf16[200,128]{1,0:T(8,128)(2,1)S(1)}, u32[]{:S(2)}, u32[]{:S(2)}) collective-permute-start(bf16[200,128]{1,0:T(8,128)(2,1)S(1)} %dynamic-slice_bitcast_fusion.8), channel_id=1, source_target_pairs={{0,16},{4,20},{8,24},{12,28},{16,0},{20,4},{24,8},{28,12},{1,17},{... | collective-permute-start | bytes 153608 | tf_op jit(solution)/shard_map/ppermute | solution.py:25
  357.0 7.7 %collective-permute-start.33 = (bf16[320,320]{1,0:T(8,128)(2,1)S(1)}, bf16[320,320]{1,0:T(8,128)(2,1)S(1)}, u32[]{:S(2)}, u32[]{:S(2)}) collective-permute-start(bf16[320,320]{1,0:T(8,128)(2,1)S(1)} %dynamic-slice_bitcast_fusion.3), channel_id=1, source_target_pairs={{0,2},{1,3},{2,0},{3,1},{4,6},{5,7},{6,4},{7,5},{8,10},{9,11},{10,... | collective-permute-start | bytes 614408 | tf_op jit(solution)/shard_map/ppermute | solution.py:25
  359.3 6.1 %collective-permute-start.47 = (bf16[200,128]{1,0:T(8,128)(2,1)S(1)}, bf16[200,128]{1,0:T(8,128)(2,1)S(1)}, u32[]{:S(2)}, u32[]{:S(2)}) collective-permute-start(bf16[200,128]{1,0:T(8,128)(2,1)S(1)} %fusion.9), channel_id=1, source_target_pairs={{0,16},{4,20},{8,24},{12,28},{16,0},{20,4},{24,8},{28,12},{1,17},{... | collective-permute-start | bytes 153608 | tf_op jit(solution)/shard_map/ppermute | solution.py:25
  364.9 4.9 %collective-permute-start.34 = (bf16[160,320]{1,0:T(8,128)(2,1)S(1)}, bf16[160,320]{1,0:T(8,128)(2,1)S(1)}, u32[]{:S(2)}, u32[]{:S(2)}) collective-permute-start(bf16[160,320]{1,0:T(8,128)(2,1)S(1)} %dynamic-slice_bitcast_fusion.5), channel_id=1, source_target_pairs={{0,4},{4,0},{8,12},{12,8},{16,20},{20,16},{24,28},{28,24},{1,5},{5... | collective-permute-start | bytes 307208 | tf_op jit(solution)/shard_map/ppermute | solution.py:25
  365.5 6.0 %collective-permute-start.48 = (bf16[400,128]{1,0:T(8,128)(2,1)S(1)}, bf16[400,128]{1,0:T(8,128)(2,1)S(1)}, u32[]{:S(2)}, u32[]{:S(2)}) collective-permute-start(bf16[400,128]{1,0:T(8,128)(2,1)S(1)} %maximum_select_fusion.8), channel_id=1, source_target_pairs={{0,8},{4,12},{8,0},{12,4},{16,24},{20,28},{24,16},{28,20},{1,9},{5... | collective-permute-start | bytes 307208 | tf_op jit(solution)/shard_map/ppermute | solution.py:25
  371.6 5.8 %collective-permute-start.49 = (bf16[800,128]{1,0:T(8,128)(2,1)S(1)}, bf16[800,128]{1,0:T(8,128)(2,1)S(1)}, u32[]{:S(2)}, u32[]{:S(2)}) collective-permute-start(bf16[800,128]{1,0:T(8,128)(2,1)S(1)} %maximum_select_fusion.6), channel_id=1, source_target_pairs={{0,4},{4,0},{8,12},{12,8},{16,20},{20,16},{24,28},{28,24},{1,5},{5... | collective-permute-start | bytes 614408 | tf_op jit(solution)/shard_map/ppermute | solution.py:25
  374.2 4.9 %collective-permute-start.36 = (bf16[40,320]{1,0:T(8,128)(2,1)S(1)}, bf16[40,320]{1,0:T(8,128)(2,1)S(1)}, u32[]{:S(2)}, u32[]{:S(2)}) collective-permute-start(bf16[40,320]{1,0:T(8,128)(2,1)S(1)} %dynamic-slice_bitcast_fusion.9), channel_id=1, source_target_pairs={{0,16},{4,20},{8,24},{12,28},{16,0},{20,4},{24,8},{28,12},{1,17},{... | collective-permute-start | bytes 76808 | tf_op jit(solution)/shard_map/ppermute | solution.py:25
  377.5 8.7 %collective-permute-start.50 = (bf16[1600,128]{1,0:T(8,128)(2,1)S(1)}, bf16[1600,128]{1,0:T(8,128)(2,1)S(1)}, u32[]{:S(2)}, u32[]{:S(2)}) collective-permute-start(bf16[1600,128]{1,0:T(8,128)(2,1)S(1)} %maximum_select_fusion.4), channel_id=1, source_target_pairs={{0,2},{1,3},{2,0},{3,1},{4,6},{5,7},{6,4},{7,5},{8,10},{9,11},{10,... | collective-permute-start | bytes 1228808 | tf_op jit(solution)/shard_map/ppermute | solution.py:25
  379.1 4.9 %collective-permute-start.37 = (bf16[40,320]{1,0:T(8,128)(2,1)S(1)}, bf16[40,320]{1,0:T(8,128)(2,1)S(1)}, u32[]{:S(2)}, u32[]{:S(2)}) collective-permute-start(bf16[40,320]{1,0:T(8,128)(2,1)S(1)} %fusion.10), channel_id=1, source_target_pairs={{0,16},{4,20},{8,24},{12,28},{16,0},{20,4},{24,8},{28,12},{1,17},{... | collective-permute-start | bytes 76808 | tf_op jit(solution)/shard_map/ppermute | solution.py:25
  380.3 9.1 %collective-permute-start.27 = (f32[4,320]{1,0:T(4,128)S(1)}, f32[4,320]{1,0:T(4,128)S(1)}, u32[]{:S(2)}, u32[]{:S(2)}) collective-permute-start(f32[4,320]{1,0:T(4,128)S(1)} %pad_maximum_fusion.1), channel_id=1, source_target_pairs={{0,1},{1,0},{2,3},{3,2},{4,5},{5,4},{6,7},{7,6},{8,9},{9,8},{10,11... | collective-permute-start | bytes 15368 | tf_op jit(solution)/shard_map/ppermute | solution.py:25
  386.5 25.5 %collective-permute-start.51 = (bf16[3200,128]{1,0:T(8,128)(2,1)S(1)}, bf16[3200,128]{1,0:T(8,128)(2,1)S(1)}, u32[]{:S(2)}, u32[]{:S(2)}) collective-permute-start(bf16[3200,128]{1,0:T(8,128)(2,1)S(1)} %maximum_select_fusion.2), channel_id=1, source_target_pairs={{0,1},{1,0},{2,3},{3,2},{4,5},{5,4},{6,7},{7,6},{8,9},{9,8},{10,11... | collective-permute-start | bytes 2457608 | tf_op jit(solution)/shard_map/ppermute | solution.py:25
  388.5 12.7 %collective-permute-start.39 = (bf16[160,320]{1,0:T(8,128)(2,1)S(1)}, bf16[160,320]{1,0:T(8,128)(2,1)}, u32[]{:S(2)}, u32[]{:S(2)}) collective-permute-start(bf16[160,320]{1,0:T(8,128)(2,1)S(1)} %maximum_select_fusion.7), channel_id=1, source_target_pairs={{0,4},{4,0},{8,12},{12,8},{16,20},{20,16},{24,28},{28,24},{1,5},{5... | collective-permute-start | bytes 307208 | tf_op jit(solution)/shard_map/ppermute | solution.py:25
  400.3 4.5 %collective-permute-start.31 = (f32[4,320]{1,0:T(4,128)S(1)}, f32[4,320]{1,0:T(4,128)S(1)}, u32[]{:S(2)}, u32[]{:S(2)}) collective-permute-start(f32[4,320]{1,0:T(4,128)S(1)} %add.203), channel_id=1, source_target_pairs={{0,16},{4,20},{8,24},{12,28},{16,0},{20,4},{24,8},{28,12},{1,17},{... | collective-permute-start | bytes 15368 | tf_op jit(solution)/shard_map/ppermute | solution.py:25
  402.2 8.8 %collective-permute-start.40 = (bf16[320,320]{1,0:T(8,128)(2,1)S(1)}, bf16[320,320]{1,0:T(8,128)(2,1)S(1)}, u32[]{:S(2)}, u32[]{:S(2)}) collective-permute-start(bf16[320,320]{1,0:T(8,128)(2,1)S(1)} %maximum_select_fusion.5), channel_id=1, source_target_pairs={{0,2},{1,3},{2,0},{3,1},{4,6},{5,7},{6,4},{7,5},{8,10},{9,11},{10,... | collective-permute-start | bytes 614408 | tf_op jit(solution)/shard_map/ppermute | solution.py:25
  411.9 10.0 %collective-permute-start.41 = (bf16[640,320]{1,0:T(8,128)(2,1)}, bf16[640,320]{1,0:T(8,128)(2,1)}, u32[]{:S(2)}, u32[]{:S(2)}) collective-permute-start(bf16[640,320]{1,0:T(8,128)(2,1)} %maximum_select_fusion.3), channel_id=1, source_target_pairs={{0,1},{1,0},{2,3},{3,2},{4,5},{5,4},{6,7},{7,6},{8,9},{9,8},{10,11... | collective-permute-start | bytes 1228808 | tf_op jit(solution)/shard_map/ppermute | solution.py:25
  (55 other events, 615.2 us)

commit v3 on v2

v3 whole, which is shorter than its diff:
```python
import functools

import jax
import jax.numpy as jnp
from jax import lax
from jax.experimental import pallas as pl
from jax.experimental.pallas import tpu as pltpu
from jax.sharding import PartitionSpec as P

epsilon = 1e-05
lanes = 128
smem = pl.BlockSpec(memory_space=pltpu.SMEM)
wide = jnp.float32
low = jnp.bfloat16


def exchange_steps():
    return [
        (axis, 1 << bit)
        for axis in ("strip", "dp")
        for bit in range(lax.axis_size(axis).bit_length() - 1)
    ]


def swapped(value, axis, bit):
    return lax.ppermute(value, axis, [(i, i ^ bit) for i in range(lax.axis_size(axis))])


def device_count():
    return lax.axis_size("dp") * lax.axis_size("strip")


def from_all(copies):
    return lax.all_to_all(copies, ("dp", "strip"), 0, 0)


def split_sums(rows, whole):
    size = whole.shape[0]
    part = jnp.concatenate([rows, whole])
    for place, (axis, bit) in enumerate(exchange_steps()):
        length = part.shape[0] - size
        if place < 3:
            upper = (lax.axis_index(axis) // bit) % 2
            tail = part[length:]
            halves = part[:length].reshape((2, length // 2) + part.shape[1:])
            sent = lax.dynamic_index_in_dim(halves, 1 - upper, 0, False)
            kept = lax.dynamic_index_in_dim(halves, upper, 0, False)
            sent, part = jnp.concatenate([sent, tail]), jnp.concatenate([kept, tail])
        else:
            sent = part
        got = swapped(sent, axis, bit)
        part = (part.astype(wide) + got.astype(wide)).astype(low)
    return part[: part.shape[0] - size], part[part.shape[0] - size :]


def joined(part):
    for axis, bit in reversed(exchange_steps()[:3]):
        upper = (lax.axis_index(axis) // bit) % 2
        got = swapped(part, axis, bit)
        part = jnp.where(
            upper == 0, jnp.concatenate([part, got]), jnp.concatenate([got, part])
        )
    return part.astype(wide)


def shifted(last, first):
    up = [(i, i + 1) for i in range(lax.axis_size("strip") - 1)]
    return (
        lax.ppermute(last, "strip", up),
        lax.ppermute(first, "strip", [(j, i) for i, j in up]),
    )


def neighbours(value, width):
    return shifted(value[:, value.shape[1] - width :], value[:, :width])


def normal_parts(x):
    density = 0.3989422804014327 * jnp.exp(-0.5 * x * x)
    scale = 1.0 + 0.2316419 * jnp.abs(x)
    guess = pl.reciprocal(scale, approx=True)
    t = guess * (2.0 - scale * guess)
    poly = 1.781477937 + t * (-1.821255978 + t * 1.330274429)
    poly = t * (0.319381530 + t * (-0.356563782 + t * poly))
    tail = density * poly
    return jnp.where(x > 0, 1.0 - tail, tail), density


def window_sums(load, weight, across, spread, rows, back, center=None, add_tap=None):
    total = [None] * rows
    reach = spread * (across - 1)
    for j in range(across):
        shift = (j - across // 2) * spread * (-1 if back else 1)
        w = [weight(i * across + j) for i in range(across)]
        tap = [None] * across
        for r in range(rows + reach):
            v = load(r, shift)
            for i in range(across):
                o = r - reach + spread * i if back else r - spread * i
                if 0 <= o < rows:
                    term = v * w[i]
                    total[o] = term if total[o] is None else total[o] + term
                    if center is not None:
                        term = v * center[o]
                        tap[i] = term if tap[i] is None else tap[i] + term
        if center is not None:
            for i in range(across):
                add_tap(i * across + j, tap[i])
    return total


def lane_groups(width):
    return [(start, min(lanes, width - start)) for start in range(0, width, lanes)]


def fill_weights(weights, taps, width):
    weights[...] = jnp.zeros_like(weights)
    for g, (start, size) in enumerate(lane_groups(width)):
        for t in range(taps.shape[0]):
            weights[g, t, :, 0:size] = jnp.broadcast_to(
                taps[t : t + 1, start : start + size].astype(wide), (8, size)
            )


def store_taps(grad_taps, tap_sums, width):
    for g, (start, size) in enumerate(lane_groups(width)):
        for t in range(grad_taps.shape[0]):
            grad_taps[t : t + 1, start : start + size] = jnp.sum(
                tap_sums[g, t, :, 0:size], axis=0, keepdims=True
            )


def inside(rows, pitch, breadth, width):
    place = lax.broadcasted_iota(jnp.int32, (rows, pitch, width), 1)
    return jnp.where(place < breadth, 1.0, 0.0).reshape(rows * pitch, width)


def live_here(counts):
    return counts[lax.axis_index("dp")]


def pixels_of(counts, area):
    total = counts[0]
    for k in range(1, counts.shape[0]):
        total += counts[k]
    return total.astype(wide) * (area * lax.axis_size("strip"))


def norm_of(blocks, pixels):
    stats = jnp.sum(blocks[...], axis=0) / pixels
    mean = stats[0:1, :]
    return mean, lax.rsqrt(stats[1:2, :] - mean * mean + epsilon)


def spec_image(*shape):
    return pl.BlockSpec((1,) + shape, lambda i: (i,) + (0,) * len(shape))


def spec_from(start, *shape):
    return pl.BlockSpec((1,) + shape, lambda i: (i + start,) + (0,) * len(shape))


def spec_two(start, *shape):
    return pl.BlockSpec((2,) + shape, lambda i: (i + start,) + (0,) * len(shape))


def spec_whole(*shape):
    return pl.BlockSpec(shape, lambda i: (0,) * len(shape))


def call(kernel, steps, ins, outs, scratch, flops, moved, name, vmem=20, **sizes):
    earlier = [out[3] for out in outs if len(out) > 3 and out[3] is not None]
    aliases, at = {}, len(ins)
    for place, out in enumerate(outs):
        if len(out) > 3 and out[3] is not None:
            aliases[at] = place
            at += 1

    def run(*refs):
        kernel(*refs[: len(ins)], *refs[at:], **sizes)

    return pl.pallas_call(
        run,
        grid=(steps,),
        in_specs=[spec for _, spec in ins] + [pl.BlockSpec(memory_space=pl.ANY)] * len(earlier),
        out_specs=[out[2] for out in outs],
        out_shape=[jax.ShapeDtypeStruct(out[0], out[1]) for out in outs],
        scratch_shapes=[pltpu.VMEM(shape, dtype) for shape, dtype in scratch],
        input_output_aliases=aliases,
        compiler_params=pltpu.CompilerParams(vmem_limit_bytes=vmem * 1024 * 1024),
        cost_estimate=pl.CostEstimate(flops=flops, bytes_accessed=moved, transcendentals=0),
        name=name,
    )(*[array for array, _ in ins], *earlier)


def paired(value):
    return pair_lanes(value, value)


def pair_lanes(left, right):
    main = left.shape[-1] // lanes * lanes
    tails = jnp.concatenate([left[..., main:], right[..., main:]], axis=-1)
    return jnp.concatenate([left[..., :main], right[..., :main], tails], axis=-1)


def split_lanes(value):
    width = value.shape[-1] // 2
    main = width // lanes * lanes
    left = jnp.concatenate([value[..., :main], value[..., 2 * main : main + width]], axis=-1)
    right = jnp.concatenate([value[..., main : 2 * main], value[..., main + width :]], axis=-1)
    return left, right


def folded(value):
    left, right = split_lanes(value)
    return left + right


def folded_square(value):
    width = value.shape[0] // 2
    main = width // lanes * lanes
    left = split_lanes(jnp.concatenate([value[:main], value[2 * main : main + width]], axis=0))[0]
    right = split_lanes(jnp.concatenate([value[main : 2 * main], value[main + width :]], axis=0))[1]
    return left + right


def pair_matrix(matrix):
    blank = jnp.zeros_like(matrix)
    left = jnp.concatenate([matrix, blank], axis=1)
    right = jnp.concatenate([blank, matrix], axis=1)
    width = matrix.shape[0]
    main = width // lanes * lanes

    def columns(value):
        return jnp.concatenate(
            [
                value[:, :main],
                value[:, width : width + main],
                value[:, main:width],
                value[:, width + main :],
            ],
            axis=1,
        )

    left, right = columns(left), columns(right)
    return jnp.concatenate([left[:main], right[:main], left[main:], right[main:]])


def pair_groups(width):
    main = width // lanes
    return [(g * lanes, g % main) for g in range(2 * main)] + [(2 * main * lanes, main)]


def fill_pair_weights(weights, taps, width):
    main = width // lanes * lanes
    for t in range(taps.shape[0]):
        row = taps[t : t + 1, :].astype(wide)
        tail = row[:, main:]
        for g in range(main // lanes):
            weights[g, t] = jnp.broadcast_to(row[:, g * lanes : (g + 1) * lanes], (8, lanes))
        weights[main // lanes, t] = jnp.broadcast_to(
            jnp.concatenate([tail, tail], axis=1), (8, lanes)
        )


def store_pair_taps(grad_taps, tap_sums, width):
    main = width // lanes * lanes
    for t in range(grad_taps.shape[0]):
        for g in range(main // lanes):
            grad_taps[t : t + 1, g * lanes : (g + 1) * lanes] = jnp.sum(
                tap_sums[g, t], axis=0, keepdims=True
            )
        tail = jnp.sum(tap_sums[main // lanes, t], axis=0, keepdims=True)
        grad_taps[t : t + 1, main:width] = tail[:, : width - main] + tail[:, width - main :]


def alive_lanes(counts, start, width):
    main = width // lanes * lanes
    image = 2 * (pl.program_id(0) + start)
    at = lax.broadcasted_iota(jnp.int32, (1, 2 * width), 1)
    second = ((at >= main) & (at < 2 * main)) | (at >= main + width)
    return jnp.where(image + second.astype(jnp.int32) < live_here(counts), 1.0, 0.0)


def stats_kernel(counts, images, copies, sums):
    image = pl.program_id(0)

    @pl.when(image == 0)
    def _():
        sums[...] = jnp.zeros_like(sums)

    alive = (image < live_here(counts)).astype(wide)
    total = jnp.zeros((images.shape[2], images.shape[3]), wide)
    square = total
    for r in range(images.shape[1]):
        value = images[0, r].astype(wide)
        total += value
        square += value * value
    sums[0:1, :] += jnp.sum(total, axis=0, keepdims=True) * alive
    sums[1:2, :] += jnp.sum(square, axis=0, keepdims=True) * alive

    @pl.when(image == pl.num_programs(0) - 1)
    def _():
        copies[...] = jnp.broadcast_to(sums[...][None], copies.shape)


def front_kernel(
    counts,
    images,
    above,
    below,
    params,
    stats,
    proj_in,
    taps,
    gelu_low,
    pre_gelu,
    lka_mid,
    values,
    gelu,
    weights,
    mask,
    mid,
    *,
    rows,
    breadth,
    pitch,
):
    width = images.shape[3]
    pixels = pixels_of(counts, rows * breadth)
    mean, rstd = norm_of(stats, pixels)
    mean, rstd = paired(mean), paired(rstd)
    gain, shift = paired(params[0:1, :]), paired(params[1:2, :])

    @pl.when(pl.program_id(0) == 0)
    def _():
        values[...] = jnp.zeros_like(values)
        gelu[...] = jnp.zeros_like(gelu)
        fill_pair_weights(weights, taps, width)
        mask[...] = inside(rows + 4, pitch, breadth, lanes)
        mask[0 : 2 * pitch, :] *= (lax.axis_index("strip") > 0).astype(wide)
        mask[(rows + 2) * pitch :, :] *= (lax.axis_index("strip") < lax.axis_size("strip") - 1).astype(wide)

    def place(at, source, r):
        value = pair_lanes(source[0, r].astype(wide), source[1, r].astype(wide))
        values[at : at + breadth, :] = (value - mean) * rstd * gain + shift

    for r in range(2):
        place(r * pitch, above, r)
        place((rows + 2 + r) * pitch, below, r)
    for r in range(rows):
        place((r + 2) * pitch, images, r)
    pre = jnp.dot(values[...].astype(low), proj_in[...], preferred_element_type=wide)
    pre_gelu[0] = pre[2 * pitch : (rows + 2) * pitch, :].astype(low)
    for g, (start, _) in enumerate(pair_groups(width)):
        part = pre[:, start : start + lanes]
        cdf, _ = normal_parts(part)
        rounded = (part * cdf * mask[...]).astype(low).astype(wide)
        gelu_low[0, :, start : start + lanes] = rounded[2 * pitch : (rows + 2) * pitch].astype(low)
        gelu[g, 8 : 8 + (rows + 4) * pitch, :] = rounded
    for g, (start, which) in enumerate(pair_groups(width)):

        def step(block, carry, g=g, start=start, which=which):
            base = pl.multiple_of(block * 8, 8)
            total = window_sums(
                lambda r, s: gelu[g, pl.ds(base + (8 + r * pitch + s), 8), :],
                lambda t: weights[which, t],
                5,
                1,
                rows,
                False,
            )
            for o in range(rows):
                mid[pl.ds(base + o * pitch, 8), start : start + lanes] = total[o]
            return carry

        lax.fori_loop(0, pitch // 8, step, 0)
    for r in range(rows):
        at = r * pitch
        lka_mid[0, r] = (
            mid[at : at + pitch, :] * inside(1, pitch, breadth, 2 * width)
        ).astype(low)


def attend_kernel(
    counts,
    images,
    lka_mid,
    above,
    below,
    gelu_low,
    params,
    stats,
    earlier_sums,
    lka_proj,
    proj_out,
    taps,
    lka_low,
    attend_out,
    attn_out,
    first_sum,
    copies,
    sums,
    window,
    weights,
    lka,
    values,
    mask,
    *,
    rows,
    breadth,
    pitch,
    gap,
    start_pair,
):
    width = images.shape[3]
    alive = alive_lanes(counts, start_pair, width)
    pixels = pixels_of(counts, rows * breadth)
    mean, rstd = norm_of(stats, pixels)
    mean, rstd = paired(mean), paired(rstd)
    gain, shift, scale = (paired(params[k : k + 1, :]) for k in range(3))

    @pl.when(pl.program_id(0) == 0)
    def _():
        window[...] = jnp.zeros_like(window)
        values[...] = jnp.zeros_like(values)
        sums[...] = earlier_sums[0]
        fill_pair_weights(weights, taps, width)
        mask[...] = inside(rows, pitch, breadth, 2 * width)

    for part, source in enumerate((above, lka_mid, below)):
        for r in range(rows):
            at = 16 + (part * rows + r) * gap
            for g, (start, _) in enumerate(pair_groups(width)):
                window[g, at : at + pitch, :] = source[0, r, :, start : start + lanes].astype(wide)
    for g, (start, which) in enumerate(pair_groups(width)):

        def step(block, carry, g=g, start=start, which=which):
            base = pl.multiple_of(block * 8, 8)
            total = window_sums(
                lambda r, s: window[g, pl.ds(base + (16 + r * gap + s), 8), :],
                lambda t: weights[which, t],
                7,
                3,
                rows,
                False,
            )
            for o in range(rows):
                lka[pl.ds(base + o * pitch, 8), start : start + lanes] = total[o]
            return carry

        lax.fori_loop(0, pitch // 8, step, 0)
    for r in range(rows):
        values[r * pitch : r * pitch + breadth, :] = pair_lanes(
            images[0, r].astype(wide), images[1, r].astype(wide)
        )
    low_lka = lka[...].astype(low)
    lka_low[0] = low_lka
    attend = jnp.dot(low_lka, lka_proj[...], preferred_element_type=wide)
    attend_out[0] = attend.astype(low)
    gated = (gelu_low[0].astype(wide) * attend).astype(low)
    branch = jnp.dot(gated, proj_out[...], preferred_element_type=wide)
    attn = (branch + ((values[...] - mean) * rstd * gain + shift)) * mask[...]
    attn_out[0] = attn.astype(low)
    first = values[...] + scale * attn
    first_sum[0], first_sum[1] = split_lanes(first)
    sums[0:1, :] += folded(jnp.sum(first, axis=0, keepdims=True) * alive)
    sums[1:2, :] += folded(jnp.sum(first * first, axis=0, keepdims=True) * alive)

    @pl.when(pl.program_id(0) == pl.num_programs(0) - 1)
    def _():
        copies[...] = jnp.broadcast_to(sums[...][None], copies.shape)


def gate_kernel(
    counts,
    first_sum,
    attn,
    cot,
    grad_normed,
    lka_low,
    attend,
    gelu_low,
    params,
    stats,
    grad_stats,
    lka_proj,
    proj_out,
    grad_first,
    grad_direct,
    grad_lka,
    grad_lka_proj,
    grad_proj_out,
    sums,
    values,
    mask,
    *,
    rows,
    breadth,
    pitch,
    start_pair,
):
    width = cot.shape[3]
    alive = alive_lanes(counts, start_pair, width)
    pixels = pixels_of(counts, rows * breadth)
    mean, rstd = norm_of(stats, pixels)
    mean, rstd = paired(mean), paired(rstd)
    scale, gain = paired(params[2:3, :]), paired(params[3:4, :])
    grad_sums = jnp.sum(grad_stats[...], axis=0)
    shift_sum, gain_sum = paired(grad_sums[0:1, :]), paired(grad_sums[1:2, :])

    @pl.when(pl.program_id(0) == 0)
    def _():
        values[...] = jnp.zeros_like(values)
        mask[...] = inside(rows, pitch, breadth, 2 * width)
        sums[...] = jnp.zeros_like(sums)
        grad_lka_proj[...] = jnp.zeros_like(grad_lka_proj)
        grad_proj_out[...] = jnp.zeros_like(grad_proj_out)

    for r in range(rows):
        values[r * pitch : r * pitch + breadth, :] = pair_lanes(
            cot[0, r].astype(wide), cot[1, r].astype(wide)
        )
    yhat = (pair_lanes(first_sum[0], first_sum[1]) - mean) * rstd
    inner = pair_lanes(grad_normed[0], grad_normed[1]) - (shift_sum + yhat * gain_sum) / pixels
    first = alive * (values[...] + rstd * gain * inner) * mask[...]
    grad_first[0] = first
    sums[0:1, :] += folded(jnp.sum(first * attn[0].astype(wide), axis=0, keepdims=True))
    branch = (first * scale).astype(low)
    gated_back = lax.dot_general(
        branch, proj_out[...], (((1,), (1,)), ((), ())), preferred_element_type=wide
    )
    gelu = gelu_low[0].astype(wide)
    attended = attend[0].astype(wide)
    gated = gelu * attended
    grad_proj_out[...] += folded_square(
        jnp.dot(gated.T.astype(low), branch, preferred_element_type=wide)
    )
    grad_direct[0] = (gated_back * attended).astype(low)
    back = (gated_back * gelu).astype(low)
    lka = lax.dot_general(
        back, lka_proj[...], (((1,), (1,)), ((), ())), preferred_element_type=wide
    )
    grad_lka_proj[...] += folded_square(
        jnp.dot(lka_low[0].astype(wide).T.astype(low), back, preferred_element_type=wide)
    )
    for r in range(rows):
        grad_lka[0, r] = lka[r * pitch : (r + 1) * pitch, :].astype(low)


def seven_kernel(
    grad_lka,
    above,
    below,
    lka_mid,
    taps,
    grad_mid,
    grad_taps,
    window,
    middle,
    out,
    weights,
    tap_sums,
    *,
    rows,
    breadth,
    pitch,
    gap,
):
    width = taps.shape[1]

    @pl.when(pl.program_id(0) == 0)
    def _():
        window[...] = jnp.zeros_like(window)
        tap_sums[...] = jnp.zeros_like(tap_sums)
        fill_pair_weights(weights, taps, width)

    for g, (start, _) in enumerate(pair_groups(width)):
        for part, source in enumerate((above, grad_lka, below)):
            for r in range(rows):
                at = 16 + (part * rows + r) * gap
                window[g, at : at + pitch, :] = source[0, r, :, start : start + lanes].astype(wide)
        for r in range(rows):
            middle[g, r * pitch : (r + 1) * pitch, :] = lka_mid[
                0, r, :, start : start + lanes
            ].astype(wide)
    for g, (start, which) in enumerate(pair_groups(width)):

        def step(block, carry, g=g, start=start, which=which):
            base = pl.multiple_of(block * 8, 8)

            def add_tap(t, value):
                tap_sums[which, t] += value

            total = window_sums(
                lambda r, s: window[g, pl.ds(base + (16 + r * gap + s), 8), :],
                lambda t: weights[which, t],
                7,
                3,
                rows,
                True,
                [middle[g, pl.ds(base + p * pitch, 8), :] for p in range(rows)],
                add_tap,
            )
            for o in range(rows):
                out[pl.ds(base + o * pitch, 8), start : start + lanes] = total[o]
            return carry

        lax.fori_loop(0, pitch // 8, step, 0, unroll=True)
    for r in range(rows):
        at = r * pitch
        grad_mid[0, r] = (
            out[at : at + pitch, :] * inside(1, pitch, breadth, 2 * width)
        ).astype(low)

    @pl.when(pl.program_id(0) == pl.num_programs(0) - 1)
    def _():
        store_pair_taps(grad_taps, tap_sums, width)


def five_kernel(
    counts,
    images,
    grad_mid,
    above,
    below,
    gelu_low,
    pre_gelu,
    grad_direct,
    grad_first,
    params,
    stats,
    proj_in,
    taps,
    grad_partial,
    grad_proj_in,
    grad_taps,
    sums,
    window,
    middle,
    out,
    weights,
    tap_sums,
    values,
    mask,
    *,
    rows,
    breadth,
    pitch,
):
    width = images.shape[3]
    alive = alive_lanes(counts, 0, width)
    pixels = pixels_of(counts, rows * breadth)
    mean, rstd = norm_of(stats, pixels)
    mean, rstd = paired(mean), paired(rstd)
    gain, shift, scale = (paired(params[k : k + 1, :]) for k in range(3))

    @pl.when(pl.program_id(0) == 0)
    def _():
        window[...] = jnp.zeros_like(window)
        tap_sums[...] = jnp.zeros_like(tap_sums)
        values[...] = jnp.zeros_like(values)
        sums[...] = jnp.zeros_like(sums)
        grad_proj_in[...] = jnp.zeros_like(grad_proj_in)
        mask[...] = inside(rows, pitch, breadth, 2 * width)
        fill_pair_weights(weights, taps, width)

    for g, (start, _) in enumerate(pair_groups(width)):
        for r in range(2):
            at = 8 + r * pitch
            window[g, at : at + pitch, :] = above[0, r, :, start : start + lanes].astype(wide)
            at = 8 + (rows + 2 + r) * pitch
            window[g, at : at + pitch, :] = below[0, r, :, start : start + lanes].astype(wide)
        for r in range(rows):
            at = 8 + (r + 2) * pitch
            window[g, at : at + pitch, :] = grad_mid[0, r, :, start : start + lanes].astype(wide)
        middle[g] = gelu_low[0, :, start : start + lanes].astype(wide)
    for g, (start, which) in enumerate(pair_groups(width)):

        def step(block, carry, g=g, start=start, which=which):
            base = pl.multiple_of(block * 8, 8)

            def add_tap(t, value):
                tap_sums[which, t] += value

            total = window_sums(
                lambda r, s: window[g, pl.ds(base + (8 + r * pitch + s), 8), :],
                lambda t: weights[which, t],
                5,
                1,
                rows,
                True,
                [middle[g, pl.ds(base + p * pitch, 8), :] for p in range(rows)],
                add_tap,
            )
            for o in range(rows):
                out[pl.ds(base + o * pitch, 8), start : start + lanes] = total[o]
            return carry

        lax.fori_loop(0, pitch // 8, step, 0, unroll=True)
    for r in range(rows):
        values[r * pitch : r * pitch + breadth, :] = pair_lanes(
            images[0, r].astype(wide), images[1, r].astype(wide)
        )
    pre = pre_gelu[0].astype(wide)
    cdf, density = normal_parts(pre)
    grad_pre = ((grad_direct[0].astype(wide) + out[...]) * (cdf + pre * density)).astype(low)
    xhat = (values[...] - mean) * rstd
    normed = (xhat * gain + shift) * mask[...]
    grad_proj_in[...] += folded_square(
        jnp.dot(normed.T.astype(low), grad_pre, preferred_element_type=wide)
    )
    back = lax.dot_general(
        grad_pre, proj_in[...], (((1,), (1,)), ((), ())), preferred_element_type=wide
    )
    first = grad_first[0]
    grad_normed = (first * scale + back) * mask[...]
    sums[0:1, :] += folded(jnp.sum(grad_normed, axis=0, keepdims=True))
    sums[1:2, :] += folded(jnp.sum(grad_normed * xhat, axis=0, keepdims=True))
    grad_partial[0], grad_partial[1] = split_lanes(first + alive * rstd * gain * grad_normed)

    @pl.when(pl.program_id(0) == pl.num_programs(0) - 1)
    def _():
        store_pair_taps(grad_taps, tap_sums, width)


def last_kernel(
    counts, images, grad_partial, params, stats, grad_stats, grad_images, *, rows, breadth, pitch
):
    alive = (pl.program_id(0) < live_here(counts)).astype(wide)
    pixels = pixels_of(counts, rows * breadth)
    mean, rstd = norm_of(stats, pixels)
    factor = alive * rstd * params[0:1, :] / pixels
    grad_sums = grad_stats[...].astype(wide)
    shift_sum, gain_sum = grad_sums[0:1, :], grad_sums[1:2, :]
    for r in range(rows):
        xhat = (images[0, r].astype(wide) - mean) * rstd
        part = grad_partial[0, r * pitch : r * pitch + breadth, :]
        grad_images[0, r] = part - factor * (shift_sum + xhat * gain_sum)


def mlp_kernel(
    counts,
    first_sum,
    above,
    below,
    cot,
    cot_above,
    cot_below,
    params,
    stats,
    fc_in,
    fc_out,
    taps,
    out_image,
    grad_normed,
    copies,
    scale_sum,
    grad_fc,
    grad_taps,
    sums,
    normed_wide,
    mlp_wide,
    normed_low,
    normed_turned,
    grads_low,
    grads_turned,
    hidden_even,
    hidden_odd,
    active_even,
    active_odd,
    grad_mixed,
    low_even,
    low_odd,
    back_even,
    back_odd,
    mlp_sum,
    normed_sum,
    weights,
    tap_sums,
    in_sum,
    out_sum,
    *,
    rows,
    breadth,
    pitch,
):
    image = pl.program_id(0)
    alive = (image < live_here(counts)).astype(jnp.float32)
    upper = (lax.axis_index("strip") > 0).astype(jnp.float32)
    lower = (lax.axis_index("strip") < lax.axis_size("strip") - 1).astype(jnp.float32)
    groups = fc_in.shape[1] // (2 * lanes)
    blocks = pitch // 8
    pixels = pixels_of(counts, rows * breadth)
    mean_two, rstd_two = norm_of(stats, pixels)
    gain_two, shift_two, scale_two = params[3:4, :], params[4:5, :], params[5:6, :]

    @pl.when(image == 0)
    def _():
        normed_wide[...] = jnp.zeros_like(normed_wide)
        mlp_wide[...] = jnp.zeros_like(mlp_wide)
        hidden_even[...] = jnp.zeros_like(hidden_even)
        hidden_odd[...] = jnp.zeros_like(hidden_odd)
        grad_mixed[...] = jnp.zeros_like(grad_mixed)
        tap_sums[...] = jnp.zeros_like(tap_sums)
        in_sum[...] = jnp.zeros_like(in_sum)
        out_sum[...] = jnp.zeros_like(out_sum)
        sums[...] = jnp.zeros_like(sums)
        scale_sum[...] = jnp.zeros_like(scale_sum)
        fill_weights(weights, taps, taps.shape[1])

    def normalized(value):
        return (value - mean_two) * rstd_two * gain_two + shift_two

    for r in range(2):
        normed_wide[r * pitch : r * pitch + breadth, :] = upper * normalized(
            above[0, r, 0:breadth, :]
        )
        at = (rows + 2 + r) * pitch
        normed_wide[at : at + breadth, :] = lower * normalized(below[0, r, 0:breadth, :])
    for r in range(rows):
        at = (r + 2) * pitch
        normed_wide[at : at + breadth, :] = normalized(first_sum[0, r, 0:breadth, :])
        at = (r + 1) * pitch
        mlp_wide[at : at + breadth, :] = cot[0, r].astype(jnp.float32) * alive * scale_two
    mlp_wide[0:breadth, :] = cot_above[0, 2].astype(jnp.float32) * alive * scale_two
    at = (rows + 1) * pitch
    mlp_wide[at : at + breadth, :] = cot_below[0, 2].astype(jnp.float32) * alive * scale_two
    normed_low[...] = normed_wide[...].astype(jnp.bfloat16)
    grads_low[...] = mlp_wide[...].astype(jnp.bfloat16)
    inner = normed_wide[2 * pitch : (rows + 2) * pitch, :]
    normed_turned[...] = inner.T.astype(jnp.bfloat16)
    grads_turned[...] = mlp_wide[pitch : (rows + 1) * pitch, :].T.astype(jnp.bfloat16)
    mlp_sum[...] = jnp.zeros_like(mlp_sum)
    normed_sum[...] = jnp.zeros_like(normed_sum)

    hiddens, sources = (hidden_even, hidden_odd), (active_even, active_odd)
    actives, backs = (low_even, low_odd), (back_even, back_odd)

    def columns(group):
        return slice(group * 2 * lanes, (group + 1) * 2 * lanes)

    def enter(group):
        hid = jnp.dot(normed_low[...], fc_in[:, columns(group)], preferred_element_type=wide)
        hid = hid.astype(low).astype(wide)
        act = jnp.dot(grads_low[...], fc_out[:, columns(group)], preferred_element_type=wide)
        for half in range(2):
            lane = slice(half * lanes, (half + 1) * lanes)
            hiddens[group % 2][half, 8 : 8 + (rows + 4) * pitch, :] = hid[:, lane]
            sources[group % 2][half] = act[:, lane]

    def forward(group, half, block):
        hidden, source, active = (refs[group % 2] for refs in (hiddens, sources, actives))
        lane = slice(half * lanes, (half + 1) * lanes)
        place, base = group * 2 + half, block * 8
        mixed = window_sums(
            lambda r, s: hidden[half, pl.ds(base + (8 + r * pitch + s), 8), :],
            lambda t: weights[place, t],
            3,
            1,
            rows + 2,
            False,
        )
        for o in range(rows + 2):
            x = mixed[o]
            cdf, density = normal_parts(x)
            slope = cdf + x * density
            grad_mixed[half, pl.ds(base + (8 + o * pitch), 8), :] = (
                source[half, pl.ds(base + o * pitch, 8), :] * slope
            )
            if 1 <= o <= rows:
                active[pl.ds(base + (o - 1) * pitch, 8), lane] = x * cdf

    def backward(group, half, block):
        hidden, back = hiddens[group % 2], backs[group % 2]
        lane = slice(half * lanes, (half + 1) * lanes)
        place, base = group * 2 + half, block * 8

        def add_tap(t, value):
            tap_sums[place, t] += value

        total = window_sums(
            lambda r, s: grad_mixed[half, pl.ds(base + (8 + r * pitch + s), 8), :],
            lambda t: weights[place, t],
            3,
            1,
            rows,
            True,
            [hidden[half, pl.ds(base + (8 + (p + 2) * pitch), 8), :] for p in range(rows)],
            add_tap,
        )
        for p in range(rows):
            back[pl.ds(base + p * pitch, 8), lane] = total[p]

    def leave(group):
        act_low = actives[group % 2][...].astype(low)
        hid_low = backs[group % 2][...].astype(low)
        mlp_sum[...] += lax.dot_general(
            act_low,
            fc_out[:, columns(group)],
            (((1,), (1,)), ((), ())),
            preferred_element_type=wide,
        )
        normed_sum[...] += lax.dot_general(
            hid_low,
            fc_in[:, columns(group)],
            (((1,), (1,)), ((), ())),
            preferred_element_type=wide,
        )
        part_in = jnp.dot(normed_turned[...], hid_low, preferred_element_type=wide)
        part_out = jnp.dot(grads_turned[...], act_low, preferred_element_type=wide)
        for half in range(2):
            lane = slice(half * lanes, (half + 1) * lanes)
            in_sum[group * 2 + half] += part_in[:, lane]
            out_sum[group * 2 + half] += part_out[:, lane]

    enter(0)
    for group in range(groups):
        if group + 1 < groups:
            enter(group + 1)
        if group > 0:
            leave(group - 1)
        for half in range(2):
            for block in range(blocks):
                forward(group, half, block)
        for half in range(2):
            for block in range(blocks):
                backward(group, half, block)
    leave(groups - 1)

    scale_grad = jnp.zeros_like(scale_two)
    shift_grad = jnp.zeros_like(scale_two)
    gain_grad = jnp.zeros_like(scale_two)
    for r in range(rows):
        mlp = mlp_sum[r * pitch : r * pitch + breadth, :]
        back = normed_sum[r * pitch : r * pitch + breadth, :]
        first = first_sum[0, r, 0:breadth, :]
        out_image[0, r] = (alive * (first + scale_two * mlp)).astype(jnp.bfloat16)
        grad_normed[0, r * pitch : r * pitch + breadth, :] = back
        grad_normed[0, r * pitch + breadth : (r + 1) * pitch, :] = jnp.zeros(
            (pitch - breadth, back.shape[1]), wide
        )
        grad = cot[0, r].astype(jnp.float32) * alive
        scale_grad += jnp.sum(grad * mlp, axis=0, keepdims=True)
        shift_grad += jnp.sum(back, axis=0, keepdims=True)
        gain_grad += jnp.sum(back * (first - mean_two) * rstd_two, axis=0, keepdims=True)
    sums[0:1, :] += shift_grad
    sums[1:2, :] += gain_grad
    scale_sum[...] += scale_grad

    @pl.when(image == pl.num_programs(0) - 1)
    def _():
        copies[...] = jnp.broadcast_to(sums[...][None], copies.shape)
        grad_fc[0 : 2 * groups] = in_sum[...].astype(low)
        grad_fc[2 * groups :] = out_sum[...].astype(low)
        store_taps(grad_taps, tap_sums, taps.shape[1])


def unpack_kernel(packed, grad_in, grad_out):
    groups = packed.shape[0] // 2
    for g in range(groups):
        grad_in[:, g * lanes : (g + 1) * lanes] = packed[g].astype(wide)
        grad_out[:, g * lanes : (g + 1) * lanes] = packed[groups + g].astype(wide)


def mlp_block(
    counts, first_sum, above, below, cot, cot_above, cot_below, params, stats, fc_in, fc_out, taps
):
    images, rows, breadth, width = cot.shape
    pitch = first_sum.shape[2]
    deep = fc_in.shape[1]
    groups = deep // lanes
    count = images * rows * breadth
    return call(
        mlp_kernel,
        images,
        [
            (counts, smem),
            (first_sum, spec_image(rows, pitch, width)),
            (above, spec_image(2, pitch, width)),
            (below, spec_image(2, pitch, width)),
            (cot, spec_image(rows, breadth, width)),
            (cot_above, spec_image(3, breadth, width)),
            (cot_below, spec_image(3, breadth, width)),
            (params, spec_whole(8, width)),
            (stats, spec_whole(*stats.shape)),
            (fc_in, spec_whole(width, deep)),
            (fc_out.T, spec_whole(width, deep)),
            (taps, spec_whole(9, deep)),
        ],
        [
            (cot.shape, low, spec_image(rows, breadth, width)),
            ((images, rows * pitch, width), wide, spec_image(rows * pitch, width)),
            (stats.shape, wide, spec_whole(*stats.shape)),
            ((1, width), wide, spec_whole(1, width)),
            ((2 * groups, width, lanes), low, spec_whole(2 * groups, width, lanes)),
            ((9, deep), wide, spec_whole(9, deep)),
        ],
        [
            ((2, width), wide),
            (((rows + 4) * pitch, width), wide),
            (((rows + 2) * pitch, width), wide),
            (((rows + 4) * pitch, width), low),
            ((width, rows * pitch), low),
            (((rows + 2) * pitch, width), low),
            ((width, rows * pitch), low),
            ((2, (rows + 4) * pitch + 16, lanes), wide),
            ((2, (rows + 4) * pitch + 16, lanes), wide),
            ((2, (rows + 2) * pitch, lanes), wide),
            ((2, (rows + 2) * pitch, lanes), wide),
            ((2, (rows + 2) * pitch + 16, lanes), wide),
            ((rows * pitch, 2 * lanes), wide),
            ((rows * pitch, 2 * lanes), wide),
            ((rows * pitch, 2 * lanes), wide),
            ((rows * pitch, 2 * lanes), wide),
            ((rows * pitch, width), wide),
            ((rows * pitch, width), wide),
            ((groups, 9, 8, lanes), wide),
            ((groups, 9, 8, lanes), wide),
            ((groups, width, lanes), wide),
            ((groups, width, lanes), wide),
        ],
        12 * count * width * deep,
        16 * count * width,
        "mlp",
        vmem=36,
        rows=rows,
        breadth=breadth,
        pitch=pitch,
    )


def body(
    images,
    counts,
    gain_one,
    shift_one,
    proj_in,
    kernel_five,
    kernel_seven,
    lka_proj,
    proj_out,
    scale_one,
    gain_two,
    shift_two,
    fc_in,
    kernel_three,
    fc_out,
    scale_two,
    cotangent,
):
    slots, rows, breadth, width = images.shape
    pitch = -(-(breadth + 2) // 8) * 8
    gap = -(-(breadth + 9) // 8) * 8
    flat = rows * pitch
    blank = jnp.zeros_like(gain_one)
    params = jnp.stack(
        [gain_one, shift_one, scale_one, gain_two, shift_two, scale_two, blank, blank]
    ).astype(wide)
    sizes = dict(rows=rows, breadth=breadth, pitch=pitch)
    vec = spec_whole(8, width)
    devices = device_count()
    blocks = (devices, 2, width)
    two = spec_whole(*blocks)
    square = spec_whole(width, width)
    image_spec = spec_image(rows, breadth, width)
    pairs = slots // 2
    chunks = [(0, pairs - 1), (pairs - 1, 1)]
    pair_width = 2 * width
    pair_square = spec_whole(pair_width, pair_width)
    pair_flat = (pairs, flat, pair_width)
    flat_spec = spec_image(flat, width)
    flat_shape = (slots, flat, width)
    row_shape = (slots, rows, pitch, width)
    groups = len(pair_groups(width))
    kinds = width // lanes + 1
    area = slots * rows * breadth
    matmul = 2 * area * width * width
    five_spec = spec_whole(*kernel_five.shape)
    seven_spec = spec_whole(*kernel_seven.shape)

    (first_part,) = call(
        stats_kernel,
        slots,
        [(counts, smem), (images, image_spec)],
        [(blocks, wide, two)],
        [((2, width), wide)],
        3 * area * width,
        2 * area * width,
        "input_sums",
    )
    pair_in, pair_lka, pair_out = (pair_matrix(m) for m in (proj_in, lka_proj, proj_out))
    last = jnp.concatenate([images[:, rows - 2 :], cotangent[:, rows - 1 :]], axis=1)
    first = jnp.concatenate([images[:, :2], cotangent[:, :1]], axis=1)
    first_part, last, first = lax.optimization_barrier((first_part, last, first))
    image_above, image_below = shifted(last, first)
    first_stats = from_all(first_part)
    gelu_low = pre_gelu = None
    mids, rims = [], []
    for start, count in chunks:
        part = matmul * count // pairs
        gelu_low, pre_gelu, mid = call(
            front_kernel,
            count,
            [
                (counts, smem),
                (images, spec_two(start, rows, breadth, width)),
                (image_above, spec_two(start, 3, breadth, width)),
                (image_below, spec_two(start, 3, breadth, width)),
                (params, vec),
                (first_stats, two),
                (pair_in, pair_square),
                (kernel_five, five_spec),
            ],
            [
                (pair_flat, low, spec_from(start, flat, pair_width), gelu_low),
                (pair_flat, low, spec_from(start, flat, pair_width), pre_gelu),
                ((count, rows, pitch, pair_width), low, spec_image(rows, pitch, pair_width)),
            ],
            [
                (((rows + 4) * pitch, pair_width), wide),
                ((groups, (rows + 4) * pitch + 16, lanes), wide),
                ((kinds, 25, 8, lanes), wide),
                (((rows + 4) * pitch, lanes), wide),
                ((flat, pair_width), wide),
            ],
            part,
            part // 40,
            f"normed_to_five_{start}",
            **sizes,
        )
        mids.append(mid)
        rims.append(neighbours(mid, rows))
    lka_low = attend = attn = first_sum = None
    second_part = jnp.zeros(blocks, wide)
    for (start, count), mid, (mid_above, mid_below) in zip(chunks, mids, rims):
        part = matmul * count // pairs
        rim_spec = spec_image(rows, pitch, pair_width)
        pair_spec = spec_from(start, flat, pair_width)
        lka_low, attend, attn, first_sum, second_part = call(
            attend_kernel,
            count,
            [
                (counts, smem),
                (images, spec_two(start, rows, breadth, width)),
                (mid, rim_spec),
                (mid_above, rim_spec),
                (mid_below, rim_spec),
                (gelu_low, pair_spec),
                (params, vec),
                (first_stats, two),
                (second_part, two),
                (pair_lka, pair_square),
                (pair_out, pair_square),
                (kernel_seven, seven_spec),
            ],
            [
                (pair_flat, low, pair_spec, lka_low),
                (pair_flat, low, pair_spec, attend),
                (pair_flat, low, pair_spec, attn),
                (flat_shape, wide, spec_two(start, flat, width), first_sum),
                (blocks, wide, two),
            ],
            [
                ((2, width), wide),
                ((groups, 3 * rows * gap + 48, lanes), wide),
                ((kinds, 49, 8, lanes), wide),
                ((flat, pair_width), wide),
                ((flat, pair_width), wide),
                ((flat, pair_width), wide),
            ],
            2 * part,
            part // 20,
            f"seven_to_first_sum_{start}",
            gap=gap,
            start_pair=start,
            **sizes,
        )
    first_rows = first_sum.reshape(row_shape)
    sum_above, sum_below = neighbours(first_rows, 2)
    second_stats = from_all(second_part)
    out_image, grad_normed_two, third_part, scale_two_part, grad_fc, grad_kernel_three = mlp_block(
        counts,
        first_rows,
        sum_above,
        sum_below,
        cotangent,
        image_above,
        image_below,
        params,
        second_stats,
        fc_in,
        fc_out,
        kernel_three,
    )
    grad_second = from_all(third_part)
    grad_first = grad_direct = None
    gates, rims = [], []
    lka_parts, out_parts, scale_parts = [], [], []
    for start, count in chunks:
        part = matmul * count // pairs
        pair_spec = spec_from(start, flat, pair_width)
        grad_first, grad_direct, grad_lka, lka_part, out_part, scale_part = call(
            gate_kernel,
            count,
            [
                (counts, smem),
                (first_sum, spec_two(start, flat, width)),
                (attn, pair_spec),
                (cotangent, spec_two(start, rows, breadth, width)),
                (grad_normed_two, spec_two(start, flat, width)),
                (lka_low, pair_spec),
                (attend, pair_spec),
                (gelu_low, pair_spec),
                (params, vec),
                (second_stats, two),
                (grad_second, two),
                (pair_lka, pair_square),
                (pair_out, pair_square),
            ],
            [
                (pair_flat, wide, pair_spec, grad_first),
                (pair_flat, low, pair_spec, grad_direct),
                ((count, rows, pitch, pair_width), low, spec_image(rows, pitch, pair_width)),
                ((width, width), wide, square),
                ((width, width), wide, square),
                ((1, width), wide, spec_whole(1, width)),
            ],
            [
                ((flat, pair_width), wide),
                ((flat, pair_width), wide),
            ],
            0,
            0,
            f"gate_backward_{start}",
            start_pair=start,
            **sizes,
        )
        gates.append(grad_lka)
        rims.append(neighbours(grad_lka, rows))
        lka_parts.append(lka_part)
        out_parts.append(out_part)
        scale_parts.append(scale_part)
    packed_shape = grad_fc.shape
    grad_fc = grad_fc.reshape(devices, -1, lanes)
    grad_fc, rims[-1] = lax.optimization_barrier((grad_fc, rims[-1]))
    fc_share = jnp.sum(from_all(grad_fc).astype(wide), axis=0).astype(low)
    grad_mid = None
    seven_parts = []
    for (start, count), grad_lka, mid, (lka_above, lka_below) in zip(chunks, gates, mids, rims):
        part = matmul * count // pairs
        rim_spec = spec_image(rows, pitch, pair_width)
        grad_mid, seven_part = call(
            seven_kernel,
            count,
            [
                (grad_lka, rim_spec),
                (lka_above, rim_spec),
                (lka_below, rim_spec),
                (mid, rim_spec),
                (kernel_seven, seven_spec),
            ],
            [
                (
                    (pairs, rows, pitch, pair_width),
                    low,
                    spec_from(start, rows, pitch, pair_width),
                    grad_mid,
                ),
                (kernel_seven.shape, wide, seven_spec),
            ],
            [
                ((groups, 3 * rows * gap + 48, lanes), wide),
                ((groups, flat, lanes), wide),
                ((flat, pair_width), wide),
                ((kinds, 49, 8, lanes), wide),
                ((kinds, 49, 8, lanes), wide),
            ],
            0,
            0,
            f"seven_backward_{start}",
            gap=gap,
            **sizes,
        )
        seven_parts.append(seven_part)
    five_above, five_below = neighbours(grad_mid, 2)
    fc_whole = lax.all_gather(fc_share, ("dp", "strip"), tiled=True)
    pair_spec = spec_image(flat, pair_width)
    grad_partial, grad_proj_in, grad_kernel_five, last_sums = call(
        five_kernel,
        pairs,
        [
            (counts, smem),
            (images, spec_two(0, rows, breadth, width)),
            (grad_mid, spec_image(rows, pitch, pair_width)),
            (five_above, spec_image(2, pitch, pair_width)),
            (five_below, spec_image(2, pitch, pair_width)),
            (gelu_low, pair_spec),
            (pre_gelu, pair_spec),
            (grad_direct, pair_spec),
            (grad_first, pair_spec),
            (params, vec),
            (first_stats, two),
            (pair_in, pair_square),
            (kernel_five, five_spec),
        ],
        [
            (flat_shape, wide, spec_two(0, flat, width)),
            ((width, width), wide, square),
            (kernel_five.shape, wide, five_spec),
            ((2, width), wide, spec_whole(2, width)),
        ],
        [
            ((groups, (rows + 4) * pitch + 16, lanes), wide),
            ((groups, flat, lanes), wide),
            ((flat, pair_width), wide),
            ((kinds, 25, 8, lanes), wide),
            ((kinds, 25, 8, lanes), wide),
            ((flat, pair_width), wide),
            ((flat, pair_width), wide),
        ],
        0,
        0,
        "five_backward",
        **sizes,
    )
    blank = jnp.zeros((4, width), wide)
    share, vectors = split_sums(
        jnp.concatenate(
            [
                grad_proj_in,
                sum(lka_parts),
                sum(out_parts),
                grad_kernel_five,
                sum(seven_parts),
                grad_kernel_three.reshape(-1, width),
                jnp.zeros((-(3 * width + 110) % 64, width), wide),
            ]
        ).astype(low),
        jnp.concatenate([last_sums, sum(scale_parts), scale_two_part, blank]).astype(low),
    )
    matrices = joined(share)
    ends = [0]
    for count in (width, width, width, 25, 49, 36):
        ends.append(ends[-1] + count)
    pieces = [matrices[i:j] for i, j in zip(ends, ends[1:])]
    (grad_images,) = call(
        last_kernel,
        slots,
        [
            (counts, smem),
            (images, image_spec),
            (grad_partial, flat_spec),
            (params, vec),
            (first_stats, two),
            (vectors, spec_whole(8, width)),
        ],
        [(images.shape, wide, image_spec)],
        [],
        6 * area * width,
        10 * area * width,
        "input_gradient",
        **sizes,
    )
    deep = fc_in.shape[1]
    grad_fc_in, grad_fc_out = call(
        unpack_kernel,
        1,
        [(fc_whole.reshape(packed_shape), spec_whole(*packed_shape))],
        [
            ((width, deep), wide, spec_whole(width, deep)),
            ((width, deep), wide, spec_whole(width, deep)),
        ],
        [],
        0,
        6 * width * deep,
        "weight_gradients",
    )
    vectors = vectors.astype(wide)
    grad_second = jnp.sum(grad_second, axis=0)
    return (
        out_image,
        grad_images,
        vectors[1],
        vectors[0],
        pieces[0],
        pieces[3],
        pieces[4],
        pieces[1],
        pieces[2],
        vectors[2],
        grad_second[1],
        grad_second[0],
        grad_fc_in,
        pieces[5].reshape(9, -1),
        grad_fc_out.T,
        vectors[3],
    )


def solution(mesh):
    split = P("dp", "strip", None, None)
    return jax.shard_map(
        body,
        mesh=mesh,
        in_specs=(split,) + (P(),) * 15 + (split,),
        out_specs=(split, split) + (P(),) * 14,
        check_vma=False,
    )
```

time: 428 us -> 364 us (0.85); the launches traced: 427 us -> 358 us
  Pallas kernels: 186 us -> 141 us
  waiting for transfers between devices: 81 us -> 41.8 us
  blocking collectives: 0 us -> 23 us
  between operations: 1.39 us -> 15.7 us
  starting transfers between devices: 96.4 us -> 84.2 us
  local copies, waits for them, and re-layouts: 44.7 us -> 39.8 us
  other arithmetic: 16.9 us -> 12 us
    ppermute x40 -> x8, waiting for transfers between devices: 74.8 us -> 27.2 us  [swapped(): lax.ppermute(value, axis, [(i, i ^ bit) for i in range(lax.axis_size(axis...]
    pallas_call x8 -> x13, Pallas kernels: 186 us -> 141 us  [call(): pl.pallas_call(run, grid=(steps,), in_specs=[spec for _, spec in ins] + [...]
    ppermute x40 -> x8, starting transfers between devices: 58.2 us -> 15.2 us  [swapped(): lax.ppermute(value, axis, [(i, i ^ bit) for i in range(lax.axis_size(axis...]
    all_to_all x0 -> x2, blocking collectives: none -> 23 us  [from_all(): return lax.all_to_all(copies, ('dp', 'strip'), 0, 0)]
    all_to_all x0 -> x2, starting transfers between devices: none -> 17.7 us  [from_all(): return lax.all_to_all(copies, ('dp', 'strip'), 0, 0)]
    ppermute x12 -> x14, starting transfers between devices: 38.2 us -> 51.3 us  [the longest x7 42.1 us: shifted(): lax.ppermute(last, 'strip', up)]
    all_gather x0 -> x1, waiting for transfers between devices: none -> 10.8 us  [body(): fc_whole = lax.all_gather(fc_share, ('dp', 'strip'), tiled=True)]
    slice x11 -> x33, local copies, waits for them, and re-layouts: 9.93 us -> 4.82 us  [the longest x2 2.23 us: body(): first = jnp.concatenate([images[:, :2], cotangent[:, :1]], axis=1)]
  transfers between devices with their start and end apart: 52 -> 25, of which waited for: 30 -> 10; matrix products, arithmetic and copies ran while one was open for 8% -> 6% of each run, Pallas kernels for 16% -> 17%
where the time goes in v3:
time: 364 us; the launch traced here: 358 us
  Pallas kernels  141 us (39%)
  starting transfers between devices  84.2 us (23%)
  waiting for transfers between devices  41.8 us (11%)
  local copies, waits for them, and re-layouts  39.8 us (11%)
  blocking collectives  23 us (6%)
  between operations  15.7 us (4%)
  other arithmetic  12 us (3%)
    pallas_call x13, Pallas kernels, call(): pl.pallas_call(run, grid=(steps,), in_specs=[spec for _, spec in ins] + [...  141 us
    ppermute x7, starting transfers between devices, shifted(): lax.ppermute(last, 'strip', up)  42.1 us
    ppermute x8, waiting for transfers between devices, swapped(): lax.ppermute(value, axis, [(i, i ^ bit) for i in range(lax.axis_size(axis...  27.2 us
    all_to_all x2, blocking collectives, from_all(): return lax.all_to_all(copies, ('dp', 'strip'), 0, 0)  23 us
    unnamed x104, local copies, waits for them, and re-layouts  22.7 us
    all_to_all x2, starting transfers between devices, from_all(): return lax.all_to_all(copies, ('dp', 'strip'), 0, 0)  17.7 us
    ppermute x8, starting transfers between devices, swapped(): lax.ppermute(value, axis, [(i, i ^ bit) for i in range(lax.axis_size(axis...  15.2 us
    all_gather x1, waiting for transfers between devices, body(): fc_whole = lax.all_gather(fc_share, ('dp', 'strip'), tiled=True)  10.8 us
  transfers between devices with their start and end apart: 25, of which 10 were waited for; matrix products, arithmetic and copies ran while one was open for 6% of the time, Pallas kernels for 17%

profile of v3, /device:TPU:0, one launch (start us, length us, event | category | flops | bytes accessed | tf_op | source)
XLA Modules:
  0.0 357.6 jit_solution(5220841747182961897)
XLA Ops:
  18.2 9.2 %all-to-all-start = ((f32[32,2,320]{2,1,0:T(2,128)}), f32[32,2,320]{2,1,0:T(2,128)S(1)}, u32[]{:S(2)}, u32[]{:S(2)}) async-start(f32[32,2,320]{2,1,0:T(2,128)} %input_sums.1), calls=%async_computation | async-start | bytes 196608 | tf_op jit(solution)/shard_map/all_to_all | solution.py:34
  40.1 8.6 %normed_to_five_0.1 = (bf16[3,360,640]{2,1,0:T(8,128)(2,1)S(1)}, bf16[3,360,640]{2,1,0:T(8,128)(2,1)S(1)}, bf16[2,9,40,640]{3,2,1,0:T(8,128)(2,1)S(1)}) custom-call(s32[8]{0:T(128)S(1)} %copy-done.40, bf16[6,9,36,320]{3,2,1,0:T(8,128)(2,1)S(1)} %copy-done.1, bf16[6,3,36,320]{3,2,1,0:T(8,128)(2,1)S(1)} %copy-done.16, bf16[6,3,36,320]{3,2,1,0:T(8,128)(2,1)S(1)} %copy-done.19, ...), custom_call_target="tpu_custom_call" | custom-call | flops 265420800 | bytes 6635520 | tf_op jit(solution)/shard_map/normed_to_five_0/pallas_call | solution.py:182
  50.1 3.1 collective-permute-start.4
  53.2 4.5 %normed_to_five_2.1 = (bf16[3,360,640]{2,1,0:T(8,128)(2,1)S(1)}, bf16[3,360,640]{2,1,0:T(8,128)(2,1)S(1)}, bf16[1,9,40,640]{3,2,1,0:T(8,128)(2,1)S(1)}) custom-call(s32[8]{0:T(128)S(1)} %copy-done.40, bf16[6,9,36,320]{3,2,1,0:T(8,128)(2,1)S(1)} %copy-done.1, bf16[6,3,36,320]{3,2,1,0:T(8,128)(2,1)S(1)} %copy-done.16, ...), custom_call_target="tpu_custom_call", output_to_operand_aliasing={{0}: (8, {}), {1}: (9, {})} | custom-call | flops 132710400 | bytes 3317760 | tf_op jit(solution)/shard_map/normed_to_five_2/pallas_call | solution.py:182
  59.0 4.1 %collective-permute-start.2 = (bf16[1,9,40,640]{3,2,1,0:T(8,128)(2,1)S(1)}, bf16[1,9,40,640]{3,2,1,0:T(8,128)(2,1)S(1)}, u32[]{:S(2)}, u32[]{:S(2)}) collective-permute-start(bf16[1,9,40,640]{3,2,1,0:T(8,128)(2,1)S(1)} %get-tuple-element.71.refs_2_.refs_3_), channel_id=1, source_target_pairs={{0,1},{1,2},{2,3},{4,5},{5,6},{6,7},{8,9},{9,10},{10,11},{12,13},{... | collective-permute-start | bytes 1382408 | tf_op jit(solution)/shard_map/ppermute | solution.py:69
  64.4 12.1 %seven_to_first_sum_0.1 = (bf16[3,360,640]{2,1,0:T(8,128)(2,1)S(1)}, bf16[3,360,640]{2,1,0:T(8,128)(2,1)S(1)}, bf16[3,360,640]{2,1,0:T(8,128)(2,1)S(1)}, f32[6,360,320]{2,1,0:T(8,128)S(1)}, f32[32,2,320]{2,1,0:T(2,128)S(1)}) custom-call(s32[8]{0:T(128)S(1)} %copy-done.40, bf16[6,9,36,320]{3,2,1,0:T(8,128)(2,1)S(1)} %copy-done.1, ...), custom_call_target="tpu_custom_call" | custom-call | flops 530841600 | bytes 13271040 | tf_op jit(solution)/shard_map/seven_to_first_sum_0/pallas_call | solution.py:182
  76.7 6.3 %seven_to_first_sum_2.1 = (bf16[3,360,640]{2,1,0:T(8,128)(2,1)S(1)}, bf16[3,360,640]{2,1,0:T(8,128)(2,1)S(1)}, bf16[3,360,640]{2,1,0:T(8,128)(2,1)S(1)}, f32[6,360,320]{2,1,0:T(8,128)S(1)}, f32[32,2,320]{2,1,0:T(2,128)S(1)}) custom-call(s32[8]{0:T(128)S(1)} %copy-done.40, ...), custom_call_target="tpu_custom_call", output_to_operand_aliasing={{0}: (12, {}), {1}: (13, {}), {2}: (14, {}), {3}: (15, {})} | custom-call | flops 265420800 | bytes 6635520 | tf_op jit(solution)/shard_map/seven_to_first_sum_2/pallas_call | solution.py:182
  84.6 4.3 %collective-permute-start.6 = (f32[6,2,40,320]{3,2,1,0:T(8,128)S(1)}, f32[6,2,40,320]{3,2,1,0:T(8,128)S(1)}, u32[]{:S(2)}, u32[]{:S(2)}) collective-permute-start(f32[6,2,40,320]{3,2,1,0:T(8,128)S(1)} %get-tuple-element.123), channel_id=1, source_target_pairs={{0,1},{1,2},{2,3},{4,5},{5,6},{6,7},{8,9},{9,10},{10,11},{12,13},{... | collective-permute-start | bytes 1843208 | tf_op jit(solution)/shard_map/ppermute | solution.py:69
  88.9 11.8 %all_to_all.20.refs_8_.refs_9_ = f32[32,2,320]{2,1,0:T(2,128)S(1)} all-to-all(f32[32,2,320]{2,1,0:T(2,128)S(1)} %get-tuple-element.80), channel_id=1, replica_groups=mesh['dp'=8,'strip'=4] {'dp','strip'}, dimensions={0} | all-to-all | bytes 163840 | tf_op jit(solution)/shard_map/all_to_all | solution.py:34
  100.7 53.7 %mlp.1 = (bf16[6,9,36,320]{3,2,1,0:T(8,128)(2,1)}, f32[6,360,320]{2,1,0:T(8,128)S(1)}, f32[32,2,320]{2,1,0:T(2,128)S(1)}, f32[1,320]{1,0:T(1,128)S(1)}, bf16[20,...) custom-call(s32[8]{0:T(128)S(1)} %copy-done.40, f32[6,9,40,320]{3,2,1,0:T(8,128)S(1)} %bitcast.21, ...), custom_call_target="tpu_custom_call" | custom-call | flops 9555148800 | bytes 9953280 | tf_op jit(solution)/shard_map/mlp/pallas_call | solution.py:182
  155.6 11.2 %all_to_all.21.refs_10_ = f32[32,2,320]{2,1,0:T(2,128)S(1)} all-to-all(f32[32,2,320]{2,1,0:T(2,128)S(1)} %get-tuple-element.86), channel_id=1, replica_groups=mesh['dp'=8,'strip'=4] {'dp','strip'}, dimensions={0} | all-to-all | bytes 163840 | tf_op jit(solution)/shard_map/all_to_all | solution.py:34
  166.8 6.2 %gate_backward_0.1 = (f32[3,360,640]{2,1,0:T(8,128)S(1)}, bf16[3,360,640]{2,1,0:T(8,128)(2,1)S(1)}, bf16[2,9,40,640]{3,2,1,0:T(8,128)(2,1)S(1)}, f32[320,320]{1,...) custom-call(s32[8]{0:T(128)S(1)} %copy-done.40, f32[6,360,320]{2,1,0:T(8,128)S(1)} %get-tuple-element.79.refs_1_, ...), custom_call_target="tpu_custom_call" | custom-call | tf_op jit(solution)/shard_map/gate_backward_0/pallas_call | solution.py:182
  174.8 3.2 gate_backward_2.1
  183.4 3.1 collective-permute-start.8
  188.9 8.5 %all-to-all-start.3 = ((bf16[32,200,128]{2,1,0:T(8,128)(2,1)}), bf16[32,200,128]{2,1,0:T(8,128)(2,1)}, u32[]{:S(2)}, u32[]{:S(2)}) async-start(bf16[32,200,128]{2,1,0:T(8,128)(2,1)} %bitcast.22), calls=%async_computation.3 | async-start | bytes 3276800 | tf_op jit(solution)/shard_map/all_to_all | solution.py:34
  198.8 4.2 %collective-permute-start.10 = (bf16[2,9,40,640]{3,2,1,0:T(8,128)(2,1)}, bf16[2,9,40,640]{3,2,1,0:T(8,128)(2,1)}, u32[]{:S(2)}, u32[]{:S(2)}) collective-permute-start(bf16[2,9,40,640]{3,2,1,0:T(8,128)(2,1)} %copy-done.25), channel_id=1, source_target_pairs={{0,1},{1,2},{2,3},{4,5},{5,6},{6,7},{8,9},{9,10},{10,11},{12,13},{... | collective-permute-start | bytes 2764808 | tf_op jit(solution)/shard_map/ppermute | solution.py:69
  207.2 14.4 %seven_backward_0.1 = (bf16[3,9,40,640]{3,2,1,0:T(8,128)(2,1)S(1)}, f32[49,320]{1,0:T(8,128)S(1)}) custom-call(bf16[2,9,40,640]{3,2,1,0:T(8,128)(2,1)S(1)} %copy-done.26, bf16[2,9,40,640]{3,2,1,0:T(8,128)(2,1)} %collective-permute-done.10.refs_1_, bf16[2,9,40,640]{3,2,1,0:T(8,128)(2,1)} %collective-permute-done.11.refs_2_, ...), custom_call_target="tpu_custom_call" | custom-call | tf_op jit(solution)/shard_map/seven_backward_0/pallas_call | solution.py:182
  221.7 6.4 %seven_backward_2.1 = (bf16[3,9,40,640]{3,2,1,0:T(8,128)(2,1)S(1)}, f32[49,320]{1,0:T(8,128)S(1)}) custom-call(bf16[1,9,40,640]{3,2,1,0:T(8,128)(2,1)S(1)} %copy-done.33, bf16[1,9,40,640]{3,2,1,0:T(8,128)(2,1)S(1)} %copy-done.37, bf16[1,9,40,640]{3,2,1,0:T(8,128)(2,1)S(1)} %copy-done.35, ...), custom_call_target="tpu_custom_call", output_to_operand_aliasing={{0}: (5, {})} | custom-call | tf_op jit(solution)/shard_map/seven_backward_2/pallas_call | solution.py:182
  229.4 21.0 %collective-permute-start.12 = (bf16[3,2,40,640]{3,2,1,0:T(8,128)(2,1)S(1)}, bf16[3,2,40,640]{3,2,1,0:T(8,128)(2,1)S(1)}, u32[]{:S(2)}, u32[]{:S(2)}) collective-permute-start(bf16[3,2,40,640]{3,2,1,0:T(8,128)(2,1)S(1)} %get-tuple-element.132), channel_id=1, source_target_pairs={{0,1},{1,2},{2,3},{4,5},{5,6},{6,7},{8,9},{9,10},{10,11},{12,13},{... | collective-permute-start | bytes 921608 | tf_op jit(solution)/shard_map/ppermute | solution.py:69
  251.7 18.1 %five_backward.1 = (f32[6,360,320]{2,1,0:T(8,128)S(1)}, f32[320,320]{1,0:T(8,128)S(1)}, f32[25,320]{1,0:T(8,128)S(1)}, f32[2,320]{1,0:T(2,128)S(1)}) custom-call(s32[8]{0:T(128)S(1)} %copy-done.40, bf16[6,9,36,320]{3,2,1,0:T(8,128)(2,1)S(1)} %copy-done.1, bf16[3,9,40,640]{3,2,1,0:T(8,128)(2,1)S(1)} %get-tuple-element.95.refs_2_, ...), custom_call_target="tpu_custom_call" | custom-call | tf_op jit(solution)/shard_map/five_backward/pallas_call | solution.py:182
  275.3 3.7 %concatenate.90 = bf16[552,320]{1,0:T(8,128)(2,1)} concatenate(bf16[544,320]{1,0:T(8,128)(2,1)} %get-tuple-element.134, bf16[2,320]{1,0:T(2,128)(2,1)S(1)} %convert.39, bf16[1,320]{1,0:T(2,128)(2,1)S(1)} %add_convert_fusion.8, bf16[1,320]{1,0:T(2,128)(2,1)S(1)} %convert.41, bf16[4,320]{1,0:T(4,128)(2,1)S(1)} %broadcast_in_dim.11), dimensions={0} | concatenate | bytes 706560 | tf_op jit(solution)/shard_map/concatenate | solution.py:48
  279.0 4.3 %collective-permute-start.14 = (bf16[552,320]{1,0:T(8,128)(2,1)}, bf16[552,320]{1,0:T(8,128)(2,1)}, u32[]{:S(2)}, u32[]{:S(2)}) collective-permute-start(bf16[552,320]{1,0:T(8,128)(2,1)} %concatenate.90), channel_id=1, source_target_pairs={{0,1},{1,0},{2,3},{3,2},{4,5},{5,4},{6,7},{7,6},{8,9},{9,8},{10,11... | collective-permute-start | bytes 1059848 | tf_op jit(solution)/shard_map/ppermute | solution.py:26
  288.6 2.8 collective-permute-start.15
  291.5 5.6 %collective-permute-done.15 = bf16[280,320]{1,0:T(8,128)(2,1)S(1)} collective-permute-done((bf16[280,320]{1,0:T(8,128)(2,1)S(1)}, bf16[280,320]{1,0:T(8,128)(2,1)S(1)}, u32[]{:S(2)}, u32[]{:S(2)}) %collective-permute-start.15) | collective-permute-done | bytes 179232 | tf_op jit(solution)/shard_map/ppermute | solution.py:26
  297.9 4.1 %collective-permute-done.16 = bf16[144,320]{1,0:T(8,128)(2,1)S(1)} collective-permute-done((bf16[144,320]{1,0:T(8,128)(2,1)S(1)}, bf16[144,320]{1,0:T(8,128)(2,1)S(1)}, u32[]{:S(2)}, u32[]{:S(2)}) %collective-permute-start.16) | collective-permute-done | bytes 92192 | tf_op jit(solution)/shard_map/ppermute | solution.py:26
  303.3 3.8 %collective-permute-done.17 = bf16[144,320]{1,0:T(8,128)(2,1)S(1)} collective-permute-done((bf16[144,320]{1,0:T(8,128)(2,1)S(1)}, bf16[144,320]{1,0:T(8,128)(2,1)S(1)}, u32[]{:S(2)}, u32[]{:S(2)}) %collective-permute-start.17) | collective-permute-done | bytes 92192 | tf_op jit(solution)/shard_map/ppermute | solution.py:26
  307.2 3.0 collective-permute-start.18
  310.1 3.9 %collective-permute-done.18 = bf16[144,320]{1,0:T(8,128)(2,1)S(1)} collective-permute-done((bf16[144,320]{1,0:T(8,128)(2,1)S(1)}, bf16[144,320]{1,0:T(8,128)(2,1)S(1)}, u32[]{:S(2)}, u32[]{:S(2)}) %collective-permute-start.18) | collective-permute-done | bytes 92192 | tf_op jit(solution)/shard_map/ppermute | solution.py:26
  315.3 4.4 %collective-permute-done.19 = bf16[136,320]{1,0:T(8,128)(2,1)S(1)} collective-permute-done((bf16[136,320]{1,0:T(8,128)(2,1)S(1)}, bf16[136,320]{1,0:T(8,128)(2,1)S(1)}, u32[]{:S(2)}, u32[]{:S(2)}) %collective-permute-start.19) | collective-permute-done | bytes 87072 | tf_op jit(solution)/shard_map/ppermute | solution.py:26
  321.7 3.9 %collective-permute-done.20 = bf16[272,320]{1,0:T(8,128)(2,1)S(1)} collective-permute-done((bf16[272,320]{1,0:T(8,128)(2,1)S(1)}, bf16[272,320]{1,0:T(8,128)(2,1)S(1)}, u32[]{:S(2)}, u32[]{:S(2)}) %collective-permute-start.20) | collective-permute-done | bytes 174112 | tf_op jit(solution)/shard_map/ppermute | solution.py:26
  328.3 3.8 %input_gradient.1 = f32[6,9,36,320]{3,2,1,0:T(8,128)} custom-call(s32[8]{0:T(128)S(1)} %copy-done.40, bf16[6,9,36,320]{3,2,1,0:T(8,128)(2,1)S(1)} %copy-done.1, f32[6,360,320]{2,1,0:T(8,128)S(1)} %copy-done.14, f32[8,320]{1,0:T(8,128)S(1)} %convert_element_type.62.refs_4_.refs_6_.refs_7_.refs_8_.refs_9_.refs_3_, ...), custom_call_target="tpu_custom_call" | custom-call | flops 3732480 | bytes 6220800 | tf_op jit(solution)/shard_map/input_gradient/pallas_call | solution.py:182
  336.1 10.8 %all-gather.2.cloned.1.call-done = bf16[6400,128]{1,0:T(8,128)(2,1)} async-done(((bf16[200,128]{1,0:T(8,128)(2,1)}), bf16[6400,128]{1,0:T(8,128)(2,1)}) %all-gather.2.cloned.1.call-update) | async-done | bytes 1638416 | tf_op jit(solution)/shard_map/all_gather | solution.py:1287
  (226 shorter events, 73.7 us)
Async XLA Ops:
  14.5 20.7 %collective-permute-start = (bf16[6,3,36,320]{3,2,1,0:T(8,128)(2,1)}, bf16[6,3,36,320]{3,2,1,0:T(8,128)(2,1)S(1)}, u32[]{:S(2)}, u32[]{:S(2)}) collective-permute-start(bf16[6,3,36,320]{3,2,1,0:T(8,128)(2,1)} %get-tuple-element.66), channel_id=1, source_target_pairs={{0,1},{1,2},{2,3},{4,5},{5,6},{6,7},{8,9},{9,10},{10,11},{12,13},{... | collective-permute-start | bytes 1244168 | tf_op jit(solution)/shard_map/ppermute | solution.py:69
  16.9 19.1 %collective-permute-start.1 = (bf16[6,3,36,320]{3,2,1,0:T(8,128)(2,1)}, bf16[6,3,36,320]{3,2,1,0:T(8,128)(2,1)S(1)}, u32[]{:S(2)}, u32[]{:S(2)}) collective-permute-start(bf16[6,3,36,320]{3,2,1,0:T(8,128)(2,1)} %get-tuple-element.67), channel_id=1, source_target_pairs={{1,0},{2,1},{3,2},{5,4},{6,5},{7,6},{9,8},{10,9},{11,10},{13,12},{... | collective-permute-start | bytes 1244168 | tf_op jit(solution)/shard_map/ppermute | solution.py:70
  18.2 17.0 %all-to-all-start = ((f32[32,2,320]{2,1,0:T(2,128)}), f32[32,2,320]{2,1,0:T(2,128)S(1)}, u32[]{:S(2)}, u32[]{:S(2)}) async-start(f32[32,2,320]{2,1,0:T(2,128)} %input_sums.1), calls=%async_computation | async-start | bytes 196608 | tf_op jit(solution)/shard_map/all_to_all | solution.py:34
  48.8 15.1 %collective-permute-start.5 = (bf16[2,9,40,640]{3,2,1,0:T(8,128)(2,1)S(1)}, bf16[2,9,40,640]{3,2,1,0:T(8,128)(2,1)S(1)}, u32[]{:S(2)}, u32[]{:S(2)}) collective-permute-start(bf16[2,9,40,640]{3,2,1,0:T(8,128)(2,1)S(1)} %get-tuple-element.73.refs_2_.refs_3_), channel_id=1, source_target_pairs={{1,0},{2,1},{3,2},{5,4},{6,5},{7,6},{9,8},{10,9},{11,10},{13,12},{... | collective-permute-start | bytes 2764808 | tf_op jit(solution)/shard_map/ppermute | solution.py:70
  50.1 13.8 %collective-permute-start.4 = (bf16[2,9,40,640]{3,2,1,0:T(8,128)(2,1)S(1)}, bf16[2,9,40,640]{3,2,1,0:T(8,128)(2,1)S(1)}, u32[]{:S(2)}, u32[]{:S(2)}) collective-permute-start(bf16[2,9,40,640]{3,2,1,0:T(8,128)(2,1)S(1)} %get-tuple-element.73.refs_2_.refs_3_), channel_id=1, source_target_pairs={{0,1},{1,2},{2,3},{4,5},{5,6},{6,7},{8,9},{9,10},{10,11},{12,13},{... | collective-permute-start | bytes 2764808 | tf_op jit(solution)/shard_map/ppermute | solution.py:69
  57.7 18.9 %copy-start.21 = (bf16[1,9,40,640]{3,2,1,0:T(8,128)(2,1)}, bf16[1,9,40,640]{3,2,1,0:T(8,128)(2,1)S(1)}, u32[]{:S(2)}) copy-start(bf16[1,9,40,640]{3,2,1,0:T(8,128)(2,1)S(1)} %get-tuple-element.71.refs_2_.refs_3_) | copy-start | bytes 1382404
  57.7 18.9 %collective-permute-start.3 = (bf16[1,9,40,640]{3,2,1,0:T(8,128)(2,1)S(1)}, bf16[1,9,40,640]{3,2,1,0:T(8,128)(2,1)S(1)}, u32[]{:S(2)}, u32[]{:S(2)}) collective-permute-start(bf16[1,9,40,640]{3,2,1,0:T(8,128)(2,1)S(1)} %get-tuple-element.71.refs_2_.refs_3_), channel_id=1, source_target_pairs={{1,0},{2,1},{3,2},{5,4},{6,5},{7,6},{9,8},{10,9},{11,10},{13,12},{... | collective-permute-start | bytes 1382408 | tf_op jit(solution)/shard_map/ppermute | solution.py:70
  59.0 17.6 %collective-permute-start.2 = (bf16[1,9,40,640]{3,2,1,0:T(8,128)(2,1)S(1)}, bf16[1,9,40,640]{3,2,1,0:T(8,128)(2,1)S(1)}, u32[]{:S(2)}, u32[]{:S(2)}) collective-permute-start(bf16[1,9,40,640]{3,2,1,0:T(8,128)(2,1)S(1)} %get-tuple-element.71.refs_2_.refs_3_), channel_id=1, source_target_pairs={{0,1},{1,2},{2,3},{4,5},{5,6},{6,7},{8,9},{9,10},{10,11},{12,13},{... | collective-permute-start | bytes 1382408 | tf_op jit(solution)/shard_map/ppermute | solution.py:69
  76.6 24.0 %copy-start.41 = (bf16[320,1280]{1,0:T(8,128)(2,1)S(1)}, bf16[320,1280]{1,0:T(8,128)(2,1)}, u32[]{:S(2)}) copy-start(bf16[320,1280]{1,0:T(8,128)(2,1)} %refs_9_.1) | copy-start | bytes 2457604
  76.6 24.0 %copy-start.42 = (bf16[1280,320]{0,1:T(8,128)(2,1)S(1)}, bf16[1280,320]{0,1:T(8,128)(2,1)}, u32[]{:S(2)}) copy-start(bf16[1280,320]{0,1:T(8,128)(2,1)} %param.31) | copy-start | bytes 2457604
  83.1 17.5 %collective-permute-start.7 = (f32[6,2,40,320]{3,2,1,0:T(8,128)S(1)}, f32[6,2,40,320]{3,2,1,0:T(8,128)S(1)}, u32[]{:S(2)}, u32[]{:S(2)}) collective-permute-start(f32[6,2,40,320]{3,2,1,0:T(8,128)S(1)} %get-tuple-element.122), channel_id=1, source_target_pairs={{1,0},{2,1},{3,2},{5,4},{6,5},{7,6},{9,8},{10,9},{11,10},{13,12},{... | collective-permute-start | bytes 1843208 | tf_op jit(solution)/shard_map/ppermute | solution.py:70
  84.6 16.1 %collective-permute-start.6 = (f32[6,2,40,320]{3,2,1,0:T(8,128)S(1)}, f32[6,2,40,320]{3,2,1,0:T(8,128)S(1)}, u32[]{:S(2)}, u32[]{:S(2)}) collective-permute-start(f32[6,2,40,320]{3,2,1,0:T(8,128)S(1)} %get-tuple-element.123), channel_id=1, source_target_pairs={{0,1},{1,2},{2,3},{4,5},{5,6},{6,7},{8,9},{9,10},{10,11},{12,13},{... | collective-permute-start | bytes 1843208 | tf_op jit(solution)/shard_map/ppermute | solution.py:69
  182.2 5.2 %collective-permute-start.9 = (bf16[1,9,40,640]{3,2,1,0:T(8,128)(2,1)S(1)}, bf16[1,9,40,640]{3,2,1,0:T(8,128)(2,1)S(1)}, u32[]{:S(2)}, u32[]{:S(2)}) collective-permute-start(bf16[1,9,40,640]{3,2,1,0:T(8,128)(2,1)S(1)} %get-tuple-element.89.refs_0_), channel_id=1, source_target_pairs={{1,0},{2,1},{3,2},{5,4},{6,5},{7,6},{9,8},{10,9},{11,10},{13,12},{... | collective-permute-start | bytes 1382408 | tf_op jit(solution)/shard_map/ppermute | solution.py:70
  183.4 4.6 %collective-permute-start.8 = (bf16[1,9,40,640]{3,2,1,0:T(8,128)(2,1)S(1)}, bf16[1,9,40,640]{3,2,1,0:T(8,128)(2,1)S(1)}, u32[]{:S(2)}, u32[]{:S(2)}) collective-permute-start(bf16[1,9,40,640]{3,2,1,0:T(8,128)(2,1)S(1)} %get-tuple-element.89.refs_0_), channel_id=1, source_target_pairs={{0,1},{1,2},{2,3},{4,5},{5,6},{6,7},{8,9},{9,10},{10,11},{12,13},{... | collective-permute-start | bytes 1382408 | tf_op jit(solution)/shard_map/ppermute | solution.py:69
  188.9 97.4 %all-to-all-start.3 = ((bf16[32,200,128]{2,1,0:T(8,128)(2,1)}), bf16[32,200,128]{2,1,0:T(8,128)(2,1)}, u32[]{:S(2)}, u32[]{:S(2)}) async-start(bf16[32,200,128]{2,1,0:T(8,128)(2,1)} %bitcast.22), calls=%async_computation.3 | async-start | bytes 3276800 | tf_op jit(solution)/shard_map/all_to_all | solution.py:34
  197.4 149.5 %all-gather.2.cloned.1.call-start = ((), (), s32[]{:S(2)}) async-start(), calls=%async_computation.4 | async-start | bytes 1689600 | tf_op jit(solution)/shard_map/all_gather | solution.py:1287
  197.5 9.7 %collective-permute-start.11 = (bf16[2,9,40,640]{3,2,1,0:T(8,128)(2,1)}, bf16[2,9,40,640]{3,2,1,0:T(8,128)(2,1)}, u32[]{:S(2)}, u32[]{:S(2)}) collective-permute-start(bf16[2,9,40,640]{3,2,1,0:T(8,128)(2,1)} %copy-done.25), channel_id=1, source_target_pairs={{1,0},{2,1},{3,2},{5,4},{6,5},{7,6},{9,8},{10,9},{11,10},{13,12},{... | collective-permute-start | bytes 2764808 | tf_op jit(solution)/shard_map/ppermute | solution.py:70
  198.8 8.4 %collective-permute-start.10 = (bf16[2,9,40,640]{3,2,1,0:T(8,128)(2,1)}, bf16[2,9,40,640]{3,2,1,0:T(8,128)(2,1)}, u32[]{:S(2)}, u32[]{:S(2)}) collective-permute-start(bf16[2,9,40,640]{3,2,1,0:T(8,128)(2,1)} %copy-done.25), channel_id=1, source_target_pairs={{0,1},{1,2},{2,3},{4,5},{5,6},{6,7},{8,9},{9,10},{10,11},{12,13},{... | collective-permute-start | bytes 2764808 | tf_op jit(solution)/shard_map/ppermute | solution.py:69
  207.2 44.5 %copy-start.8 = (bf16[3,360,640]{2,1,0:T(8,128)(2,1)S(1)}, bf16[3,360,640]{2,1,0:T(8,128)(2,1)}, u32[]{:S(2)}) copy-start(bf16[3,360,640]{2,1,0:T(8,128)(2,1)} %copy-done.7) | copy-start | bytes 4147204
  207.2 44.5 %copy-start.10 = (bf16[3,360,640]{2,1,0:T(8,128)(2,1)S(1)}, bf16[3,360,640]{2,1,0:T(8,128)(2,1)}, u32[]{:S(2)}) copy-start(bf16[3,360,640]{2,1,0:T(8,128)(2,1)} %copy-done.9) | copy-start | bytes 4147204
  221.6 30.0 %copy-start.3 = (bf16[640,640]{1,0:T(8,128)(2,1)S(1)}, bf16[640,640]{1,0:T(8,128)(2,1)}, u32[]{:S(2)}) copy-start(bf16[640,640]{1,0:T(8,128)(2,1)} %pad_maximum_fusion.refs_6_.refs_11_) | copy-start | bytes 2457604
  221.7 30.0 %copy-start.5 = (f32[3,360,640]{2,1,0:T(8,128)S(1)}, f32[3,360,640]{2,1,0:T(8,128)}, u32[]{:S(2)}) copy-start(f32[3,360,640]{2,1,0:T(8,128)} %copy-done.4) | copy-start | bytes 8294404
  228.1 22.4 %collective-permute-start.13 = (bf16[3,2,40,640]{3,2,1,0:T(8,128)(2,1)S(1)}, bf16[3,2,40,640]{3,2,1,0:T(8,128)(2,1)S(1)}, u32[]{:S(2)}, u32[]{:S(2)}) collective-permute-start(bf16[3,2,40,640]{3,2,1,0:T(8,128)(2,1)S(1)} %get-tuple-element.131), channel_id=1, source_target_pairs={{1,0},{2,1},{3,2},{5,4},{6,5},{7,6},{9,8},{10,9},{11,10},{13,12},{... | collective-permute-start | bytes 921608 | tf_op jit(solution)/shard_map/ppermute | solution.py:70
  229.4 22.2 %collective-permute-start.12 = (bf16[3,2,40,640]{3,2,1,0:T(8,128)(2,1)S(1)}, bf16[3,2,40,640]{3,2,1,0:T(8,128)(2,1)S(1)}, u32[]{:S(2)}, u32[]{:S(2)}) collective-permute-start(bf16[3,2,40,640]{3,2,1,0:T(8,128)(2,1)S(1)} %get-tuple-element.132), channel_id=1, source_target_pairs={{0,1},{1,2},{2,3},{4,5},{5,6},{6,7},{8,9},{9,10},{10,11},{12,13},{... | collective-permute-start | bytes 921608 | tf_op jit(solution)/shard_map/ppermute | solution.py:69
  279.0 6.0 %collective-permute-start.14 = (bf16[552,320]{1,0:T(8,128)(2,1)}, bf16[552,320]{1,0:T(8,128)(2,1)}, u32[]{:S(2)}, u32[]{:S(2)}) collective-permute-start(bf16[552,320]{1,0:T(8,128)(2,1)} %concatenate.90), channel_id=1, source_target_pairs={{0,1},{1,0},{2,3},{3,2},{4,5},{5,4},{6,7},{7,6},{8,9},{9,8},{10,11... | collective-permute-start | bytes 1059848 | tf_op jit(solution)/shard_map/ppermute | solution.py:26
  288.6 8.4 %collective-permute-start.15 = (bf16[280,320]{1,0:T(8,128)(2,1)S(1)}, bf16[280,320]{1,0:T(8,128)(2,1)S(1)}, u32[]{:S(2)}, u32[]{:S(2)}) collective-permute-start(bf16[280,320]{1,0:T(8,128)(2,1)S(1)} %pad_maximum_fusion.17), channel_id=1, source_target_pairs={{0,2},{1,3},{2,0},{3,1},{4,6},{5,7},{6,4},{7,5},{8,10},{9,11},{10,... | collective-permute-start | bytes 537608 | tf_op jit(solution)/shard_map/ppermute | solution.py:26
  297.2 4.8 %collective-permute-start.16 = (bf16[144,320]{1,0:T(8,128)(2,1)S(1)}, bf16[144,320]{1,0:T(8,128)(2,1)S(1)}, u32[]{:S(2)}, u32[]{:S(2)}) collective-permute-start(bf16[144,320]{1,0:T(8,128)(2,1)S(1)} %pad_maximum_fusion.19), channel_id=1, source_target_pairs={{0,4},{4,0},{8,12},{12,8},{16,20},{20,16},{24,28},{28,24},{1,5},{5... | collective-permute-start | bytes 276488 | tf_op jit(solution)/shard_map/ppermute | solution.py:26
  302.1 5.1 %collective-permute-start.17 = (bf16[144,320]{1,0:T(8,128)(2,1)S(1)}, bf16[144,320]{1,0:T(8,128)(2,1)S(1)}, u32[]{:S(2)}, u32[]{:S(2)}) collective-permute-start(bf16[144,320]{1,0:T(8,128)(2,1)S(1)} %add_convert_fusion.6), channel_id=1, source_target_pairs={{0,8},{4,12},{8,0},{12,4},{16,24},{20,28},{24,16},{28,20},{1,9},{5... | collective-permute-start | bytes 276488 | tf_op jit(solution)/shard_map/ppermute | solution.py:26
  307.2 6.9 %collective-permute-start.18 = (bf16[144,320]{1,0:T(8,128)(2,1)S(1)}, bf16[144,320]{1,0:T(8,128)(2,1)S(1)}, u32[]{:S(2)}, u32[]{:S(2)}) collective-permute-start(bf16[144,320]{1,0:T(8,128)(2,1)S(1)} %add_convert_fusion.5), channel_id=1, source_target_pairs={{0,16},{4,20},{8,24},{12,28},{16,0},{20,4},{24,8},{28,12},{1,17},{... | collective-permute-start | bytes 276488 | tf_op jit(solution)/shard_map/ppermute | solution.py:26
  314.1 5.5 %collective-permute-start.19 = (bf16[136,320]{1,0:T(8,128)(2,1)S(1)}, bf16[136,320]{1,0:T(8,128)(2,1)S(1)}, u32[]{:S(2)}, u32[]{:S(2)}) collective-permute-start(bf16[136,320]{1,0:T(8,128)(2,1)S(1)} %slice.203), channel_id=1, source_target_pairs={{0,4},{4,0},{8,12},{12,8},{16,20},{20,16},{24,28},{28,24},{1,5},{5... | collective-permute-start | bytes 261128 | tf_op jit(solution)/shard_map/ppermute | solution.py:26
  319.7 5.9 %collective-permute-start.20 = (bf16[272,320]{1,0:T(8,128)(2,1)S(1)}, bf16[272,320]{1,0:T(8,128)(2,1)S(1)}, u32[]{:S(2)}, u32[]{:S(2)}) collective-permute-start(bf16[272,320]{1,0:T(8,128)(2,1)S(1)} %maximum_select_fusion.2), channel_id=1, source_target_pairs={{0,2},{1,3},{2,0},{3,1},{4,6},{5,7},{6,4},{7,5},{8,10},{9,11},{10,... | collective-permute-start | bytes 522248 | tf_op jit(solution)/shard_map/ppermute | solution.py:26
  325.7 7.0 %collective-permute-start.21 = (bf16[544,320]{1,0:T(8,128)(2,1)S(1)}, bf16[544,320]{1,0:T(8,128)(2,1)S(1)}, u32[]{:S(2)}, u32[]{:S(2)}) collective-permute-start(bf16[544,320]{1,0:T(8,128)(2,1)S(1)} %maximum_select_fusion.1), channel_id=1, source_target_pairs={{0,1},{1,0},{2,3},{3,2},{4,5},{5,4},{6,7},{7,6},{8,9},{9,8},{10,11... | collective-permute-start | bytes 1044488 | tf_op jit(solution)/shard_map/ppermute | solution.py:26
  (51 other events, 306.3 us)
Sparse Core Ops, SparseCore 0:
  288.7 58.1 all-gather.1
